TPU v7x, 32 devices: a whole 2x2x4 slice. The times are simulated.
32 devices in a mesh: expert: 8 (over y, x, core), dp: 4 (over z).
Axes of the slice: x: 2, y: 2, z: 4, core: 2. Of those that a mesh axis runs over, the one named last changes fastest.
Arguments:
- tokens: bfloat16 [2048, 2048], P('expert'), may hold values from -6 to 6
- grad_out: bfloat16 [2048, 2048], P('expert'), may hold values from -6 to 6
- expert_ids: int32 [2048, 2], P('expert'), may hold values from 0 to 7, all different within a row; in each aligned block of 256 rows (0 to 255, 256 to 511, ...) at most 96 rows name the same one
- gate_vals: float32 [2048, 2], P('expert'), may hold values from 0.2 to 1
- w_gate: bfloat16 [8, 2048, 4096], P('expert', None, 'dp'), may hold values from -0.125 to 0.125
- w_up: bfloat16 [8, 2048, 4096], P('expert', None, 'dp'), may hold values from -0.125 to 0.125
- w_down: bfloat16 [8, 4096, 2048], P('expert', 'dp'), may hold values from -0.09375 to 0.09375
Outputs:
- grad_tokens: bfloat16 [2048, 2048], P('expert', 'dp')
- grad_gate: bfloat16 [8, 2048, 4096], P('expert', None, 'dp')
- grad_up: bfloat16 [8, 2048, 4096], P('expert', None, 'dp')
- grad_down: bfloat16 [8, 4096, 2048], P('expert', 'dp')
Inputs may be any that keep to these rules, and one draw needn't show every extreme that they name: `expert_ids`: each row names 2 different experts; among the 256 rows of one index of the expert axis no expert is named more than 96 times.
All inputs are finite; a program needn't handle non-finite values.
Results may differ from a plain program's by a relative error of at most 0.0058.
Values may be sent and summed in bfloat16 or wider, within the bound.
No kernel may reach another device: no remote copies, remote signals or barrier semaphores. Data moves between devices by JAX's collectives and lax.ppermute only.
A program may use at most 128 MiB of HBM per device.

v0:
```python
import jax
import jax.numpy as jnp
from jax import lax
from jax.sharding import PartitionSpec as P

TOP = 2


def contract(left, right, left_dim, right_dim):
    return lax.dot_general(
        left, right, (((left_dim,), (right_dim,)), ((), ())), preferred_element_type=jnp.float32
    )


def body(tokens, grad_out, expert_ids, gate_vals, w_gate, w_up, w_down):
    experts = lax.axis_size("expert")
    tok_rows = tokens.shape[0]
    capacity = 3 * tok_rows // experts
    flat_ids = expert_ids.reshape(-1)
    onehot = (flat_ids[:, None] == jnp.arange(experts, dtype=jnp.int32)[None, :]).astype(jnp.int32)
    before = jnp.cumsum(onehot, axis=0) - onehot
    slot_rank = jnp.sum(before * onehot, axis=1)
    target = flat_ids * capacity + slot_rank
    placing = (jnp.arange(experts * capacity, dtype=jnp.int32)[:, None] == target[None, :]).astype(
        jnp.bfloat16
    )
    repeated = jnp.repeat(tokens, TOP, axis=0)
    scaled = (
        gate_vals.reshape(-1)[:, None] * jnp.repeat(grad_out, TOP, axis=0).astype(jnp.float32)
    ).astype(jnp.bfloat16)
    send_x = jnp.dot(placing, repeated, preferred_element_type=jnp.float32).astype(jnp.bfloat16)
    send_r = jnp.dot(placing, scaled, preferred_element_type=jnp.float32).astype(jnp.bfloat16)
    recv_x, recv_r = (
        lax.all_to_all(send_x, "expert", split_axis=0, concat_axis=0, tiled=True),
        lax.all_to_all(send_r, "expert", split_axis=0, concat_axis=0, tiled=True),
    )
    gate_mat = w_gate[0]
    up_mat = w_up[0]
    down_mat = w_down[0]
    pre_gate = jnp.dot(recv_x, gate_mat, preferred_element_type=jnp.float32)
    pre_up = jnp.dot(recv_x, up_mat, preferred_element_type=jnp.float32)
    grad_hidden = contract(recv_r, down_mat, 1, 1)
    squash = jax.nn.sigmoid(pre_gate)
    hidden = (squash * pre_gate * pre_up).astype(jnp.bfloat16)
    grad_a = (grad_hidden * pre_up * squash * (1.0 + pre_gate * (1.0 - squash))).astype(
        jnp.bfloat16
    )
    grad_b = (grad_hidden * squash * pre_gate).astype(jnp.bfloat16)
    grad_gate = contract(recv_x, grad_a, 0, 0).astype(jnp.bfloat16)
    grad_up = contract(recv_x, grad_b, 0, 0).astype(jnp.bfloat16)
    grad_down = contract(hidden, recv_r, 0, 0).astype(jnp.bfloat16)
    partial_sum = contract(gate_mat, grad_a, 1, 1) + contract(up_mat, grad_b, 1, 1)
    own_sum = lax.psum_scatter(partial_sum, "dp", scatter_dimension=0, tiled=True)
    returned_cols = lax.all_to_all(own_sum, "expert", split_axis=1, concat_axis=1, tiled=True)
    picked = jnp.take(returned_cols, target, axis=1)
    grad_tokens = jnp.sum(picked.T.reshape(tok_rows, TOP, -1), axis=1).astype(jnp.bfloat16)
    return (grad_tokens, grad_gate[None], grad_up[None], grad_down[None])


def solution(mesh):
    in_specs = (
        P("expert", None),
        P("expert", None),
        P("expert", None),
        P("expert", None),
        P("expert", None, "dp"),
        P("expert", None, "dp"),
        P("expert", "dp", None),
    )
    out_specs = (
        P("expert", "dp"),
        P("expert", None, "dp"),
        P("expert", None, "dp"),
        P("expert", "dp", None),
    )
    return jax.shard_map(body, mesh=mesh, in_specs=in_specs, out_specs=out_specs, check_vma=False)
```

profile of v0, /device:TPU:0, one launch (start us, length us, event | category | flops | bytes accessed | tf_op | source)
XLA Modules:
  0.0 272.9 jit_solution(10005001404148023522)
XLA Ops:
  8.3 1.1 reduce-window.6
  9.8 2.5 broadcast_in_dim.30
  12.3 2.2 reshape.88
  14.5 5.0 %convolution_convert_fusion = bf16[768,2048]{1,0:T(8,128)(2,1)} fusion(bf16[512,2048]{1,0:T(8,128)(2,1)} %reshape.88, s32[512]{0:T(512)S(1)} %get-tuple-element.5), kind=kOutput, calls=%fused_computation.16 | convolution fusion | flops 1612578816 | bytes 5244928 | tf_op jit(solution)/shard_map/dot_general | solution.py:31
  19.6 5.2 %all-to-all-start.1 = ((bf16[8,96,2048]{2,1,0:T(8,128)(2,1)}), bf16[8,96,2048]{2,1,0:T(8,128)(2,1)S(1)}, u32[]{:S(2)}, u32[]{:S(2)}) async-start(bf16[8,96,2048]{2,1,0:T(8,128)(2,1)} %bitcast.57), calls=%async_computation.1 | async-start | bytes 6291456 | tf_op jit(solution)/shard_map/all_to_all | solution.py:34
  24.7 5.4 %broadcast_in_dim.29 = f32[256,2,2048]{2,1,0:T(2,128)} broadcast(bf16[256,2048]{1,0:T(8,128)(2,1)} %param.8), dimensions={0,2} | broadcast | bytes 5242880 | tf_op jit(solution)/shard_map/broadcast_in_dim | solution.py:29
  30.1 6.1 %convert_element_type.48 = f32[512,2048]{1,0:T(8,128)} reshape(f32[256,2,2048]{2,1,0:T(2,128)} %broadcast_in_dim.29) | data formatting | bytes 8388608 | tf_op jit(solution)/shard_map/convert_element_type | solution.py:29
  36.4 5.7 %convolution_convert_fusion.1 = bf16[768,2048]{1,0:T(8,128)(2,1)} fusion(f32[512,2048]{1,0:T(8,128)} %convert_element_type.48, f32[512]{0:T(512)S(1)} %mul.66, s32[512]{0:T(512)S(1)} %get-tuple-element.5), kind=kOutput, calls=%fused_computation.17 | convolution fusion | flops 1614675968 | bytes 7344128 | tf_op jit(solution)/shard_map/dot_general | solution.py:32
  42.2 20.4 %all-to-all-done.1 = bf16[8,96,2048]{2,1,0:T(8,128)(2,1)S(1)} async-done(((bf16[8,96,2048]{2,1,0:T(8,128)(2,1)}), bf16[8,96,2048]{2,1,0:T(8,128)(2,1)S(1)}, u32[]{:S(2)}, u32[]{:S(2)}) %all-to-all-start.1) | async-done | bytes 3145760 | tf_op jit(solution)/shard_map/all_to_all | solution.py:34
  62.6 4.5 %all-to-all-start = ((bf16[8,96,2048]{2,1,0:T(8,128)(2,1)}), bf16[8,96,2048]{2,1,0:T(8,128)(2,1)}, u32[]{:S(2)}, u32[]{:S(2)}) async-start(bf16[8,96,2048]{2,1,0:T(8,128)(2,1)} %bitcast.58), calls=%async_computation | async-start | bytes 6291456 | tf_op jit(solution)/shard_map/all_to_all | solution.py:35
  67.1 7.2 %fusion.6 = f32[768,1024]{1,0:T(8,128)} fusion(bf16[768,2048]{1,0:T(8,128)(2,1)S(1)} %bitcast.53, bf16[1,2048,1024]{2,1,0:T(8,128)(2,1)} %param.12), kind=kOutput, calls=%fused_computation.8 | convolution fusion | flops 3221225472 | bytes 10485760 | tf_op jit(solution)/shard_map/dot_general | solution.py:41
  74.4 30.6 %all-to-all-done = bf16[8,96,2048]{2,1,0:T(8,128)(2,1)} async-done(((bf16[8,96,2048]{2,1,0:T(8,128)(2,1)}), bf16[8,96,2048]{2,1,0:T(8,128)(2,1)}, u32[]{:S(2)}, u32[]{:S(2)}) %all-to-all-start) | async-done | bytes 3145760 | tf_op jit(solution)/shard_map/all_to_all | solution.py:35
  105.0 6.3 %fusion.8 = f32[768,1024]{1,0:T(8,128)S(1)} fusion(bf16[768,2048]{1,0:T(8,128)(2,1)} %bitcast.3, bf16[1,1024,2048]{2,1,0:T(8,128)(2,1)} %param.13), kind=kOutput, calls=%fused_computation.10 | convolution fusion | flops 3221225472 | bytes 10485760 | tf_op jit(solution)/shard_map/dot_general | solution.py:10
  111.3 6.2 %multiply_convert_fusion.2 = (bf16[768,1024]{1,0:T(8,128)(2,1)S(1)}, bf16[768,1024]{1,0:T(8,128)(2,1)S(1)}, f32[768,1024]{1,0:T(8,128)}) fusion(f32[768,1024]{1,0:T(8,128)S(1)} %fusion.8, f32[768,1024]{1,0:T(8,128)S(1)} %copy-done.8, bf16[768,2048]{1,0:T(8,128)(2,1)S(1)} %bitcast.54, bf16[1,2048,1024]{2,1,0:T(8,128)(2,1)S(1)} %copy-done.3), kind=kOutput, calls=%fused_computation.19 | convolution fusion | flops 3231449088 | bytes 19922944 | tf_op jit(solution)/shard_map/dot_general | solution.py:40
  117.6 3.5 %fusion = f32[768,2048]{1,0:T(8,128)S(1)} fusion(bf16[768,1024]{1,0:T(8,128)(2,1)S(1)} %get-tuple-element.7, bf16[1,2048,1024]{2,1,0:T(8,128)(2,1)S(1)} %copy-done.3), kind=kOutput, calls=%fused_computation.2 | convolution fusion | flops 3221225472 | bytes 12058624 | tf_op jit(solution)/shard_map/dot_general | solution.py:10
  121.1 5.5 %add_bitcast_fusion = f32[2048,768]{0,1:T(8,128)} fusion(f32[768,2048]{1,0:T(8,128)S(1)} %fusion, bf16[768,1024]{1,0:T(8,128)(2,1)S(1)} %get-tuple-element.6, bf16[1,2048,1024]{2,1,0:T(8,128)(2,1)S(1)} %copy-done.4), kind=kOutput, calls=%fused_computation.1 | convolution fusion | flops 3222798336 | bytes 18350080 | tf_op jit(solution)/shard_map/dot_general | solution.py:10
  127.6 6.4 %convert_bitcast_fusion.1 = bf16[1,2048,1024]{2,1,0:T(8,128)(2,1)} fusion(bf16[768,2048]{1,0:T(8,128)(2,1)S(1)} %bitcast.55, bf16[768,1024]{1,0:T(8,128)(2,1)} %copy-done.5), kind=kOutput, calls=%fused_computation.13 | convolution fusion | flops 3223322624 | bytes 8912896 | tf_op jit(solution)/shard_map/dot_general | solution.py:10
  134.0 102.9 %reduce-scatter.2.cloned.1.call-done = f32[512,768]{0,1:T(8,128)} async-done(((f32[2048,768]{0,1:T(8,128)}), f32[512,768]{0,1:T(8,128)}) %reduce-scatter.2.cloned.1.call-update) | async-done | bytes 1572880 | tf_op jit(solution)/shard_map/reduce_scatter | solution.py:53
  236.9 3.8 %all-to-all-start.2 = ((f32[512,8,96]{0,2,1:T(8,128)}), f32[512,8,96]{0,2,1:T(8,128)S(1)}, u32[]{:S(2)}, u32[]{:S(2)}) async-start(f32[512,8,96]{0,2,1:T(8,128)} %bitcast.59), calls=%async_computation.3 | async-start | bytes 3145728 | tf_op jit(solution)/shard_map/all_to_all | solution.py:54
  240.7 7.1 %convert_bitcast_fusion.2 = bf16[1,2048,1024]{2,1,0:T(8,128)(2,1)} fusion(bf16[768,2048]{1,0:T(8,128)(2,1)} %bitcast.56, bf16[768,1024]{1,0:T(8,128)(2,1)S(1)} %copy-done.7), kind=kOutput, calls=%fused_computation.14 | convolution fusion | flops 3223322624 | bytes 8912896 | tf_op jit(solution)/shard_map/dot_general | solution.py:10
  247.8 7.1 %convert_bitcast_fusion = bf16[1,1024,2048]{2,1,0:T(8,128)(2,1)} fusion(bf16[768,2048]{1,0:T(8,128)(2,1)} %bitcast.3, f32[768,1024]{1,0:T(8,128)S(1)} %copy-done.9, f32[768,1024]{1,0:T(8,128)S(1)} %copy-done.10), kind=kOutput, calls=%fused_computation.12 | convolution fusion | flops 3228041216 | bytes 13631488 | tf_op jit(solution)/shard_map/dot_general | solution.py:10
  255.0 6.6 %all-to-all-done.2 = f32[512,8,96]{0,2,1:T(8,128)S(1)} async-done(((f32[512,8,96]{0,2,1:T(8,128)}), f32[512,8,96]{0,2,1:T(8,128)S(1)}, u32[]{:S(2)}, u32[]{:S(2)}) %all-to-all-start.2) | async-done | bytes 1572896 | tf_op jit(solution)/shard_map/all_to_all | solution.py:54
  261.6 1.6 gather_fusion
  264.0 2.1 reduce_sum.22
  (42 shorter events, 3.5 us)
Async XLA Ops:
  19.6 43.1 %all-to-all-start.1 = ((bf16[8,96,2048]{2,1,0:T(8,128)(2,1)}), bf16[8,96,2048]{2,1,0:T(8,128)(2,1)S(1)}, u32[]{:S(2)}, u32[]{:S(2)}) async-start(bf16[8,96,2048]{2,1,0:T(8,128)(2,1)} %bitcast.57), calls=%async_computation.1 | async-start | bytes 6291456 | tf_op jit(solution)/shard_map/all_to_all | solution.py:34
  30.1 6.1 %copy-start.2 = (f32[256,2]{0,1:T(2,128)S(1)}, f32[256,2]{0,1:T(2,128)}, u32[]{:S(2)}) copy-start(f32[256,2]{0,1:T(2,128)} %param.10) | copy-start | bytes 6148
  62.6 65.0 %copy-start = (bf16[8,96,2048]{2,1,0:T(8,128)(2,1)}, bf16[8,96,2048]{2,1,0:T(8,128)(2,1)S(1)}, u32[]{:S(2)}) copy-start(bf16[8,96,2048]{2,1,0:T(8,128)(2,1)S(1)} %all-to-all-done.1) | copy-start | bytes 9437188
  62.6 42.4 %all-to-all-start = ((bf16[8,96,2048]{2,1,0:T(8,128)(2,1)}), bf16[8,96,2048]{2,1,0:T(8,128)(2,1)}, u32[]{:S(2)}, u32[]{:S(2)}) async-start(bf16[8,96,2048]{2,1,0:T(8,128)(2,1)} %bitcast.58), calls=%async_computation | async-start | bytes 6291456 | tf_op jit(solution)/shard_map/all_to_all | solution.py:35
  67.1 169.8 %reduce-scatter.2.cloned.1.call-start = ((), (), s32[]{:S(2)}) async-start(), calls=%async_computation.4 | async-start | bytes 7864320 | tf_op jit(solution)/shard_map/reduce_scatter | solution.py:53
  105.0 6.4 %copy-start.3 = (bf16[1,2048,1024]{2,1,0:T(8,128)(2,1)S(1)}, bf16[1,2048,1024]{2,1,0:T(8,128)(2,1)}, u32[]{:S(2)}) copy-start(bf16[1,2048,1024]{2,1,0:T(8,128)(2,1)} %param.11) | copy-start | bytes 12582916
  105.0 6.4 %copy-start.8 = (f32[768,1024]{1,0:T(8,128)S(1)}, f32[768,1024]{1,0:T(8,128)}, u32[]{:S(2)}) copy-start(f32[768,1024]{1,0:T(8,128)} %fusion.6) | copy-start | bytes 9437188
  117.6 3.5 %copy-start.6 = (bf16[768,1024]{1,0:T(8,128)(2,1)}, bf16[768,1024]{1,0:T(8,128)(2,1)S(1)}, u32[]{:S(2)}) copy-start(bf16[768,1024]{1,0:T(8,128)(2,1)S(1)} %get-tuple-element.7) | copy-start | bytes 4718596
  117.6 3.5 %copy-start.5 = (bf16[768,1024]{1,0:T(8,128)(2,1)}, bf16[768,1024]{1,0:T(8,128)(2,1)S(1)}, u32[]{:S(2)}) copy-start(bf16[768,1024]{1,0:T(8,128)(2,1)S(1)} %get-tuple-element.6) | copy-start | bytes 4718596
  117.6 3.5 %copy-start.4 = (bf16[1,2048,1024]{2,1,0:T(8,128)(2,1)S(1)}, bf16[1,2048,1024]{2,1,0:T(8,128)(2,1)}, u32[]{:S(2)}) copy-start(bf16[1,2048,1024]{2,1,0:T(8,128)(2,1)} %param.12) | copy-start | bytes 12582916
  126.6 0.7 copy-start.1
  134.0 106.7 %copy-start.7 = (bf16[768,1024]{1,0:T(8,128)(2,1)S(1)}, bf16[768,1024]{1,0:T(8,128)(2,1)}, u32[]{:S(2)}) copy-start(bf16[768,1024]{1,0:T(8,128)(2,1)} %copy-done.6) | copy-start | bytes 4718596
  236.9 24.7 %all-to-all-start.2 = ((f32[512,8,96]{0,2,1:T(8,128)}), f32[512,8,96]{0,2,1:T(8,128)S(1)}, u32[]{:S(2)}, u32[]{:S(2)}) async-start(f32[512,8,96]{0,2,1:T(8,128)} %bitcast.59), calls=%async_computation.3 | async-start | bytes 3145728 | tf_op jit(solution)/shard_map/all_to_all | solution.py:54
  240.7 7.1 %copy-start.9 = (f32[768,1024]{1,0:T(8,128)S(1)}, f32[768,1024]{1,0:T(8,128)}, u32[]{:S(2)}) copy-start(f32[768,1024]{1,0:T(8,128)} %fusion.6) | copy-start | bytes 9437188
  240.7 7.1 %copy-start.10 = (f32[768,1024]{1,0:T(8,128)S(1)}, f32[768,1024]{1,0:T(8,128)}, u32[]{:S(2)}) copy-start(f32[768,1024]{1,0:T(8,128)} %get-tuple-element.8) | copy-start | bytes 9437188
Sparse Core Ops, SparseCore 0:
  126.7 110.1 reduce-scatter.1
where the time goes:
time: 274 us; the launch traced here: 273 us
  waiting for transfers between devices  161 us (59%)
  matrix products  60.2 us (22%)
  local copies, waits for them, and re-layouts  20.9 us (8%)
  between operations  14.2 us (5%)
  starting transfers between devices  13.5 us (5%)
  other arithmetic  3.52 us (1%)
    reduce_scatter x1, waiting for transfers between devices, body(): lax.psum_scatter(partial_sum, 'dp', scatter_dimension=0, tiled=True)  103 us
    dot_general x6, matrix products, contract(): lax.dot_general(left, right, (((left_dim,), (right_dim,)), ((), ())), pre...  35.9 us
    all_to_all x1, waiting for transfers between devices, body(): lax.all_to_all(send_r, 'expert', split_axis=0, concat_axis=0, tiled=True)  30.6 us
    all_to_all x1, waiting for transfers between devices, body(): lax.all_to_all(send_x, 'expert', split_axis=0, concat_axis=0, tiled=True)  20.4 us
    dot_general x1, matrix products, body(): pre_up = jnp.dot(recv_x, up_mat, preferred_element_type=jnp.float32)  7.24 us
    all_to_all x1, waiting for transfers between devices, body(): lax.all_to_all(own_sum, 'expert', split_axis=1, concat_axis=1, tiled=True)  6.63 us
    dot_general x1, matrix products, body(): pre_gate = jnp.dot(recv_x, gate_mat, preferred_element_type=jnp.float32)  6.24 us
    convert_element_type x1, local copies, waits for them, and re-layouts, body(): jnp.repeat(grad_out, TOP, axis=0).astype(jnp.float32)  6.06 us
  transfers between devices with their start and end apart: 4, of which 4 were waited for; matrix products, arithmetic and copies ran while one was open for 17% of the time, Pallas kernels for 0%

commit v1 on v0

v1 whole, which is shorter than its diff:
```python
import functools

import jax
import jax.numpy as jnp
from jax import lax
from jax.experimental import pallas as pl
from jax.experimental.pallas import tpu as pltpu
from jax.sharding import PartitionSpec as P

F32 = jnp.float32
BF16 = jnp.bfloat16
VMEM_LIMIT = 56 * 1024 * 1024


def contract(left, right, left_dim, right_dim):
    return lax.dot_general(
        left, right, (((left_dim,), (right_dim,)), ((), ())), preferred_element_type=F32
    )


def place_kernel(experts, cap, with_gate, *refs):
    if with_gate:
        ids_ref, gate_ref, rows_ref, *outs = refs
    else:
        ids_ref, rows_ref, *outs = refs
    toks = rows_ref.shape[0]
    ids0 = ids_ref[0:1, :]
    ids1 = ids_ref[1:2, :]
    rel = lax.broadcasted_iota(jnp.int32, (experts, toks), 0)
    match = (rel == ids0) | (rel == ids1)
    earlier = (
        lax.broadcasted_iota(jnp.int32, (toks, toks), 0)
        < lax.broadcasted_iota(jnp.int32, (toks, toks), 1)
    ).astype(BF16)
    rank = jnp.dot(match.astype(BF16), earlier, preferred_element_type=F32).astype(jnp.int32)
    rank = jnp.where(match, rank, -1)
    slot = lax.broadcasted_iota(jnp.int32, (cap, toks), 0)
    rows = rows_ref[...]
    for d in range(experts):
        placing = slot == rank[d : d + 1, :]
        block = jnp.dot(placing.astype(BF16), rows, preferred_element_type=F32)
        if with_gate:
            gate = jnp.where(ids0 == d, gate_ref[0:1, :], gate_ref[1:2, :])
            slot_gate = jnp.sum(jnp.where(placing, gate, 0.0), axis=1, keepdims=True)
            block = block * slot_gate
        else:
            outs[experts][d * cap : (d + 1) * cap, :] = placing.astype(BF16)
        outs[d][...] = block.astype(BF16)


def place(ids_rel, rows, experts, cap, gate=None):
    toks, width = rows.shape
    with_gate = gate is not None
    outs = [jax.ShapeDtypeStruct((cap, width), BF16)] * experts
    if not with_gate:
        outs = outs + [jax.ShapeDtypeStruct((experts * cap, toks), BF16)]
    args = (ids_rel, gate, rows) if with_gate else (ids_rel, rows)
    return pl.pallas_call(
        functools.partial(place_kernel, experts, cap, with_gate),
        out_shape=outs,
        name="place_scaled" if with_gate else "place_tokens",
        compiler_params=pltpu.CompilerParams(vmem_limit_bytes=VMEM_LIMIT),
        cost_estimate=pl.CostEstimate(
            flops=2 * experts * cap * toks * width,
            bytes_accessed=2 * width * (toks + experts * cap),
            transcendentals=0,
        ),
    )(*args)


def swap(rows, axis, mask):
    count = lax.axis_size(axis)
    return lax.ppermute(rows, axis, [(i, i ^ mask) for i in range(count)])


def send_order(experts):
    return sorted(range(1, experts), key=lambda d: (-(d >> 1).bit_count(), d))


def body(tokens, grad_out, expert_ids, gate_vals, w_gate, w_up, w_down):
    experts = lax.axis_size("expert")
    dp = lax.axis_size("dp")
    toks, width = tokens.shape
    cap = 3 * toks // experts
    me = lax.axis_index("expert")
    mine = lax.axis_index("dp")
    ids_rel = expert_ids.T ^ me
    *send_x, placing = place(ids_rel, tokens, experts, cap)
    send_r = place(ids_rel, grad_out, experts, cap, gate_vals.T)
    order = send_order(experts)
    recv_x, recv_r = [send_x[0]] * experts, [send_r[0]] * experts
    for d in order:
        recv_x[d] = swap(send_x[d], "expert", d)
    for d in order:
        recv_r[d] = swap(send_r[d], "expert", d)
    recv_x = jnp.concatenate(recv_x, axis=0)
    recv_r = jnp.concatenate(recv_r, axis=0)
    gate_mat, up_mat, down_mat = w_gate[0], w_up[0], w_down[0]
    pre_gate = jnp.dot(recv_x, gate_mat, preferred_element_type=F32)
    pre_up = jnp.dot(recv_x, up_mat, preferred_element_type=F32)
    grad_hidden = contract(recv_r, down_mat, 1, 1)
    squash = jax.nn.sigmoid(pre_gate)
    hidden = (squash * pre_gate * pre_up).astype(BF16)
    grad_a = (grad_hidden * pre_up * squash * (1.0 + pre_gate * (1.0 - squash))).astype(BF16)
    grad_b = (grad_hidden * squash * pre_gate).astype(BF16)
    partial = (contract(grad_a, gate_mat, 1, 1) + contract(grad_b, up_mat, 1, 1)).astype(BF16)
    back = [partial[d * cap : (d + 1) * cap] for d in range(experts)]
    for d in order:
        back[d] = swap(back[d], "expert", d)
    grad_gate = contract(recv_x, grad_a, 0, 0).astype(BF16)
    grad_up = contract(recv_x, grad_b, 0, 0).astype(BF16)
    grad_down = contract(hidden, recv_r, 0, 0).astype(BF16)
    combined = contract(placing, jnp.concatenate(back, axis=0), 0, 0)
    part = width // dp
    total = lax.dynamic_slice_in_dim(combined, mine * part, part, 1)
    for s in range(1, dp):
        other = lax.dynamic_slice_in_dim(combined, (mine ^ s) * part, part, 1)
        total = total + swap(other.astype(BF16), "dp", s).astype(F32)
    return (total.astype(BF16), grad_gate[None], grad_up[None], grad_down[None])


def solution(mesh):
    in_specs = (
        P("expert", None),
        P("expert", None),
        P("expert", None),
        P("expert", None),
        P("expert", None, "dp"),
        P("expert", None, "dp"),
        P("expert", "dp", None),
    )
    out_specs = (
        P("expert", "dp"),
        P("expert", None, "dp"),
        P("expert", None, "dp"),
        P("expert", "dp", None),
    )
    return jax.shard_map(body, mesh=mesh, in_specs=in_specs, out_specs=out_specs, check_vma=False)
```

time: 274 us -> 174 us (0.64)
  waiting for transfers between devices: 161 us -> 90.4 us
  matrix products: 60.2 us -> 39 us
  local copies, waits for them, and re-layouts: 20.9 us -> 2.18 us
  starting transfers between devices: 13.5 us -> 28.9 us
  between operations: 14.2 us -> 1.1 us
  Pallas kernels: 0 us -> 7.6 us
    reduce_scatter x1 -> x0, waiting for transfers between devices: 103 us -> none  [body(): lax.psum_scatter(partial_sum, 'dp', scatter_dimension=0, tiled=True)]
    ppermute x0 -> x24, waiting for transfers between devices: none -> 90.4 us  [swap(): return lax.ppermute(rows, axis, [(i, i ^ mask) for i in range(count)])]
    all_to_all x3 -> x0, waiting for transfers between devices: 57.7 us -> none  [the longest x1 30.6 us: body(): lax.all_to_all(send_r, 'expert', split_axis=0, concat_axis=0, tiled=True)]
    ppermute x0 -> x24, starting transfers between devices: none -> 28.9 us  [swap(): return lax.ppermute(rows, axis, [(i, i ^ mask) for i in range(count)])]
    dot_general x4 -> x2, matrix products: 24.3 us -> 8.48 us  [the longest x1 5.07 us: body(): pre_up = jnp.dot(recv_x, up_mat, preferred_element_type=F32)]
    all_to_all x3 -> x0, starting transfers between devices: 13.4 us -> none  [the longest x1 5.17 us: body(): lax.all_to_all(send_x, 'expert', split_axis=0, concat_axis=0, tiled=True)]
    broadcast_in_dim x2 -> x0, local copies, waits for them, and re-layouts: 7.86 us -> none  [the longest x1 5.37 us: body(): jnp.repeat(grad_out, TOP, axis=0).astype(jnp.float32)]
    pallas_call x0 -> x2, Pallas kernels: none -> 7.6 us  [place(): pl.pallas_call(functools.partial(place_kernel, experts, cap, with_gate),...]
  transfers between devices with their start and end apart: 4 -> 24, of which waited for: 4 -> 9; matrix products, arithmetic and copies ran while one was open for 17% -> 12% of each run, Pallas kernels for 0% -> 2%
where the time goes in v1:
time: 174 us; the launch traced here: 171 us
  waiting for transfers between devices  90.4 us (52%)
  matrix products  39 us (22%)
  starting transfers between devices  28.9 us (17%)
  Pallas kernels  7.6 us (4%)
  local copies, waits for them, and re-layouts  2.18 us (1%)
  other arithmetic  2.1 us (1%)
    ppermute x24, waiting for transfers between devices, swap(): return lax.ppermute(rows, axis, [(i, i ^ mask) for i in range(count)])  90.4 us
    dot_general x7, matrix products, contract(): lax.dot_general(left, right, (((left_dim,), (right_dim,)), ((), ())), pre...  30.5 us
    ppermute x24, starting transfers between devices, swap(): return lax.ppermute(rows, axis, [(i, i ^ mask) for i in range(count)])  28.9 us
    pallas_call x2, Pallas kernels, place(): pl.pallas_call(functools.partial(place_kernel, experts, cap, with_gate),...  7.6 us
    dot_general x1, matrix products, body(): pre_up = jnp.dot(recv_x, up_mat, preferred_element_type=F32)  5.07 us
  transfers between devices with their start and end apart: 24, of which 9 were waited for; matrix products, arithmetic and copies ran while one was open for 12% of the time, Pallas kernels for 2%

profile of v1, /device:TPU:0, one launch (start us, length us, event | category | flops | bytes accessed | tf_op | source)
XLA Modules:
  0.0 171.3 jit_solution(14921512074852801371)
XLA Ops:
  1.9 3.8 %place_tokens.1 = (bf16[96,2048]{1,0:T(8,128)(2,1)}, bf16[96,2048]{1,0:T(8,128)(2,1)}, bf16[96,2048]{1,0:T(8,128)(2,1)}, bf16[96,2048]{1,0:T(8,128)(2,1)}, bf16[...) custom-call(s32[2,256]{1,0:T(2,128)} %xor_bitcast_fusion.refs_0_, ...), custom_call_target="tpu_custom_call" | custom-call | flops 805306368 | bytes 4194304 | tf_op jit(solution)/shard_map/place_tokens/pallas_call | solution.py:58
  6.2 2.6 %collective-permute-start.8 = (bf16[96,2048]{1,0:T(8,128)(2,1)}, bf16[96,2048]{1,0:T(8,128)(2,1)S(1)}, u32[]{:S(2)}, u32[]{:S(2)}) collective-permute-start(bf16[96,2048]{1,0:T(8,128)(2,1)} %get-tuple-element.32), channel_id=1, source_target_pairs={{0,8},{4,12},{8,0},{12,4},{16,24},{20,28},{24,16},{28,20},{1,9},{5... | collective-permute-start | bytes 1179656 | tf_op jit(solution)/shard_map/ppermute | solution.py:73
  8.9 1.8 %collective-permute-start.10 = (bf16[96,2048]{1,0:T(8,128)(2,1)}, bf16[96,2048]{1,0:T(8,128)(2,1)S(1)}, u32[]{:S(2)}, u32[]{:S(2)}) collective-permute-start(bf16[96,2048]{1,0:T(8,128)(2,1)} %get-tuple-element.34), channel_id=1, source_target_pairs={{0,16},{4,20},{8,24},{12,28},{16,0},{20,4},{24,8},{28,12},{1,17},{... | collective-permute-start | bytes 1179656 | tf_op jit(solution)/shard_map/ppermute | solution.py:73
  10.7 3.8 %place_scaled.1 = (bf16[96,2048]{1,0:T(8,128)(2,1)}, bf16[96,2048]{1,0:T(8,128)(2,1)}, bf16[96,2048]{1,0:T(8,128)(2,1)}, bf16[96,2048]{1,0:T(8,128)(2,1)}, bf16[...) custom-call(s32[2,256]{1,0:T(2,128)} %xor_bitcast_fusion.refs_0_, ...), custom_call_target="tpu_custom_call" | custom-call | flops 805306368 | bytes 4194304 | tf_op jit(solution)/shard_map/place_scaled/pallas_call | solution.py:58
  15.7 2.7 %collective-permute-start.12 = (bf16[96,2048]{1,0:T(8,128)(2,1)S(1)}, bf16[96,2048]{1,0:T(8,128)(2,1)S(1)}, u32[]{:S(2)}, u32[]{:S(2)}) collective-permute-start(bf16[96,2048]{1,0:T(8,128)(2,1)S(1)} %copy-done.9), channel_id=1, source_target_pairs={{0,24},{4,28},{8,16},{12,20},{16,8},{20,12},{24,0},{28,4},{1,25},{... | collective-permute-start | bytes 1179656 | tf_op jit(solution)/shard_map/ppermute | solution.py:73
  20.7 6.2 %collective-permute-done.9 = bf16[96,2048]{1,0:T(8,128)(2,1)S(1)} collective-permute-done((bf16[96,2048]{1,0:T(8,128)(2,1)}, bf16[96,2048]{1,0:T(8,128)(2,1)S(1)}, u32[]{:S(2)}, u32[]{:S(2)}) %collective-permute-start.9) | collective-permute-done | bytes 393248 | tf_op jit(solution)/shard_map/ppermute | solution.py:73
  27.6 2.0 %collective-permute-start.1 = (bf16[96,2048]{1,0:T(8,128)(2,1)S(1)}, bf16[96,2048]{1,0:T(8,128)(2,1)S(1)}, u32[]{:S(2)}, u32[]{:S(2)}) collective-permute-start(bf16[96,2048]{1,0:T(8,128)(2,1)S(1)} %copy-done.12), channel_id=1, source_target_pairs={{0,8},{4,12},{8,0},{12,4},{16,24},{20,28},{24,16},{28,20},{1,9},{5... | collective-permute-start | bytes 1179656 | tf_op jit(solution)/shard_map/ppermute | solution.py:73
  29.6 15.5 %collective-permute-done.11 = bf16[96,2048]{1,0:T(8,128)(2,1)S(1)} collective-permute-done((bf16[96,2048]{1,0:T(8,128)(2,1)}, bf16[96,2048]{1,0:T(8,128)(2,1)S(1)}, u32[]{:S(2)}, u32[]{:S(2)}) %collective-permute-start.11) | collective-permute-done | bytes 393248 | tf_op jit(solution)/shard_map/ppermute | solution.py:73
  45.1 2.1 %collective-permute-start.2 = (bf16[96,2048]{1,0:T(8,128)(2,1)S(1)}, bf16[96,2048]{1,0:T(8,128)(2,1)S(1)}, u32[]{:S(2)}, u32[]{:S(2)}) collective-permute-start(bf16[96,2048]{1,0:T(8,128)(2,1)S(1)} %copy-done.11), channel_id=1, source_target_pairs={{0,12},{4,8},{8,4},{12,0},{16,28},{20,24},{24,20},{28,16},{1,13},{... | collective-permute-start | bytes 1179656 | tf_op jit(solution)/shard_map/ppermute | solution.py:73
  49.0 3.4 %fusion.2 = f32[768,1024]{1,0:T(8,128)S(1)} fusion(bf16[768,2048]{1,0:T(8,128)(2,1)S(1)} %constant_dynamic-update-slice_fusion.8, bf16[1,2048,1024]{2,1,0:T(8,128)(2,1)S(1)} %copy-done.3), kind=kOutput, calls=%fused_computation.3 | convolution fusion | flops 3221225472 | bytes 10485760 | tf_op jit(solution)/shard_map/dot_general | solution.py:99
  52.5 5.1 %fusion.6 = f32[768,1024]{1,0:T(8,128)} fusion(bf16[768,2048]{1,0:T(8,128)(2,1)S(1)} %constant_dynamic-update-slice_fusion.8, bf16[1,2048,1024]{2,1,0:T(8,128)(2,1)S(1)} %copy-done.4), kind=kOutput, calls=%fused_computation.7 | convolution fusion | flops 3221225472 | bytes 10485760 | tf_op jit(solution)/shard_map/dot_general | solution.py:100
  58.8 1.8 %collective-permute-start.6 = (bf16[96,2048]{1,0:T(8,128)(2,1)S(1)}, bf16[96,2048]{1,0:T(8,128)(2,1)S(1)}, u32[]{:S(2)}, u32[]{:S(2)}) collective-permute-start(bf16[96,2048]{1,0:T(8,128)(2,1)S(1)} %copy-done.5), channel_id=1, source_target_pairs={{0,28},{4,24},{8,20},{12,16},{16,12},{20,8},{24,4},{28,0},{1,29},{... | collective-permute-start | bytes 1179656 | tf_op jit(solution)/shard_map/ppermute | solution.py:73
  60.7 21.7 %collective-permute-done.4 = bf16[96,2048]{1,0:T(8,128)(2,1)S(1)} collective-permute-done((bf16[96,2048]{1,0:T(8,128)(2,1)S(1)}, bf16[96,2048]{1,0:T(8,128)(2,1)S(1)}, u32[]{:S(2)}, u32[]{:S(2)}) %collective-permute-start.4) | collective-permute-done | bytes 393248 | tf_op jit(solution)/shard_map/ppermute | solution.py:73
  82.6 5.4 %convert_bitcast_fusion = bf16[1,1024,2048]{2,1,0:T(8,128)(2,1)} fusion(bf16[768,2048]{1,0:T(8,128)(2,1)S(1)} %constant_dynamic-update-slice_fusion, f32[768,1024]{1,0:T(8,128)S(1)} %copy-done.17, f32[768,1024]{1,0:T(8,128)S(1)} %fusion.2), kind=kOutput, calls=%fused_computation.11 | convolution fusion | flops 3228041216 | bytes 13631488 | tf_op jit(solution)/shard_map/dot_general | solution.py:16
  88.0 6.9 %multiply_convert_fusion.1 = (bf16[768,1024]{1,0:T(8,128)(2,1)}, bf16[768,1024]{1,0:T(8,128)(2,1)S(1)}) fusion(f32[768,1024]{1,0:T(8,128)} %copy-done.16, f32[768,1024]{1,0:T(8,128)S(1)} %copy-done.17, bf16[768,2048]{1,0:T(8,128)(2,1)S(1)} %constant_dynamic-update-slice_fusion, bf16[1,1024,2048]{2,1,0:T(8,128)(2,1)S(1)} %copy-done.2), kind=kOutput, calls=%fused_computation.15 | convolution fusion | flops 3231449088 | bytes 16777216 | tf_op jit(solution)/shard_map/dot_general | solution.py:16
  94.9 3.4 %fusion = f32[768,2048]{1,0:T(8,128)S(1)} fusion(bf16[768,1024]{1,0:T(8,128)(2,1)S(1)} %get-tuple-element.39, bf16[1,2048,1024]{2,1,0:T(8,128)(2,1)S(1)} %copy-done.3), kind=kOutput, calls=%fused_computation.1 | convolution fusion | flops 3221225472 | bytes 12058624 | tf_op jit(solution)/shard_map/dot_general | solution.py:16
  98.4 3.7 %add_convert_fusion = bf16[768,2048]{1,0:T(8,128)(2,1)S(1)} fusion(f32[768,2048]{1,0:T(8,128)S(1)} %fusion, bf16[768,1024]{1,0:T(8,128)(2,1)S(1)} %copy-done.18, bf16[1,2048,1024]{2,1,0:T(8,128)(2,1)S(1)} %copy-done.4), kind=kOutput, calls=%fused_computation | convolution fusion | flops 3224371200 | bytes 15204352 | tf_op jit(solution)/shard_map/dot_general | solution.py:16
  103.8 5.0 %convert_bitcast_fusion.1 = bf16[1,2048,1024]{2,1,0:T(8,128)(2,1)} fusion(bf16[768,2048]{1,0:T(8,128)(2,1)S(1)} %constant_dynamic-update-slice_fusion.8, bf16[768,1024]{1,0:T(8,128)(2,1)S(1)} %copy-done.18), kind=kOutput, calls=%fused_computation.12 | convolution fusion | flops 3223322624 | bytes 8912896 | tf_op jit(solution)/shard_map/dot_general | solution.py:16
  115.0 6.7 %collective-permute-done.16 = bf16[96,2048]{1,0:T(8,128)(2,1)S(1)} collective-permute-done((bf16[96,2048]{1,0:T(8,128)(2,1)S(1)}, bf16[96,2048]{1,0:T(8,128)(2,1)S(1)}, u32[]{:S(2)}, u32[]{:S(2)}) %collective-permute-start.16) | collective-permute-done | bytes 393248 | tf_op jit(solution)/shard_map/ppermute | solution.py:73
  121.8 24.4 %collective-permute-done.18 = bf16[96,2048]{1,0:T(8,128)(2,1)S(1)} collective-permute-done((bf16[96,2048]{1,0:T(8,128)(2,1)S(1)}, bf16[96,2048]{1,0:T(8,128)(2,1)S(1)}, u32[]{:S(2)}, u32[]{:S(2)}) %collective-permute-start.18) | collective-permute-done | bytes 393248 | tf_op jit(solution)/shard_map/ppermute | solution.py:73
  149.1 2.6 %collective-permute-start.22 = (bf16[256,512]{1,0:T(8,128)(2,1)S(1)}, bf16[256,512]{1,0:T(8,128)(2,1)S(1)}, u32[]{:S(2)}, u32[]{:S(2)}) collective-permute-start(bf16[256,512]{1,0:T(8,128)(2,1)S(1)} %get-tuple-element.50), channel_id=1, source_target_pairs={{0,2},{1,3},{2,0},{3,1},{4,6},{5,7},{6,4},{7,5},{8,10},{9,11},{10,... | collective-permute-start | bytes 786440 | tf_op jit(solution)/shard_map/ppermute | solution.py:73
  151.9 5.0 %convert_bitcast_fusion.2 = bf16[1,2048,1024]{2,1,0:T(8,128)(2,1)} fusion(bf16[768,2048]{1,0:T(8,128)(2,1)S(1)} %constant_dynamic-update-slice_fusion.8, bf16[768,1024]{1,0:T(8,128)(2,1)S(1)} %copy-done.15), kind=kOutput, calls=%fused_computation.13 | convolution fusion | flops 3223322624 | bytes 8912896 | tf_op jit(solution)/shard_map/dot_general | solution.py:16
  156.9 3.9 %collective-permute-done.21 = bf16[256,512]{1,0:T(8,128)(2,1)S(1)} collective-permute-done((bf16[256,512]{1,0:T(8,128)(2,1)S(1)}, bf16[256,512]{1,0:T(8,128)(2,1)S(1)}, u32[]{:S(2)}, u32[]{:S(2)}) %collective-permute-start.21) | collective-permute-done | bytes 262176 | tf_op jit(solution)/shard_map/ppermute | solution.py:73
  160.8 9.6 %collective-permute-done.22 = bf16[256,512]{1,0:T(8,128)(2,1)S(1)} collective-permute-done((bf16[256,512]{1,0:T(8,128)(2,1)S(1)}, bf16[256,512]{1,0:T(8,128)(2,1)S(1)}, u32[]{:S(2)}, u32[]{:S(2)}) %collective-permute-start.22) | collective-permute-done | bytes 262176 | tf_op jit(solution)/shard_map/ppermute | solution.py:73
  (100 shorter events, 21.1 us)
Async XLA Ops:
  5.7 10.0 %collective-permute-start.7 = (bf16[96,2048]{1,0:T(8,128)(2,1)}, bf16[96,2048]{1,0:T(8,128)(2,1)S(1)}, u32[]{:S(2)}, u32[]{:S(2)}) collective-permute-start(bf16[96,2048]{1,0:T(8,128)(2,1)} %get-tuple-element.31), channel_id=1, source_target_pairs={{0,4},{4,0},{8,12},{12,8},{16,20},{20,16},{24,28},{28,24},{1,5},{5... | collective-permute-start | bytes 1179656 | tf_op jit(solution)/shard_map/ppermute | solution.py:73
  6.2 12.7 %collective-permute-start.8 = (bf16[96,2048]{1,0:T(8,128)(2,1)}, bf16[96,2048]{1,0:T(8,128)(2,1)S(1)}, u32[]{:S(2)}, u32[]{:S(2)}) collective-permute-start(bf16[96,2048]{1,0:T(8,128)(2,1)} %get-tuple-element.32), channel_id=1, source_target_pairs={{0,8},{4,12},{8,0},{12,4},{16,24},{20,28},{24,16},{28,20},{1,9},{5... | collective-permute-start | bytes 1179656 | tf_op jit(solution)/shard_map/ppermute | solution.py:73
  8.8 18.2 %collective-permute-start.9 = (bf16[96,2048]{1,0:T(8,128)(2,1)}, bf16[96,2048]{1,0:T(8,128)(2,1)S(1)}, u32[]{:S(2)}, u32[]{:S(2)}) collective-permute-start(bf16[96,2048]{1,0:T(8,128)(2,1)} %get-tuple-element.33), channel_id=1, source_target_pairs={{0,12},{4,8},{8,4},{12,0},{16,28},{20,24},{24,20},{28,16},{1,13},{... | collective-permute-start | bytes 1179656 | tf_op jit(solution)/shard_map/ppermute | solution.py:73
  8.9 18.7 %collective-permute-start.10 = (bf16[96,2048]{1,0:T(8,128)(2,1)}, bf16[96,2048]{1,0:T(8,128)(2,1)S(1)}, u32[]{:S(2)}, u32[]{:S(2)}) collective-permute-start(bf16[96,2048]{1,0:T(8,128)(2,1)} %get-tuple-element.34), channel_id=1, source_target_pairs={{0,16},{4,20},{8,24},{12,28},{16,0},{20,4},{24,8},{28,12},{1,17},{... | collective-permute-start | bytes 1179656 | tf_op jit(solution)/shard_map/ppermute | solution.py:73
  10.7 34.5 %collective-permute-start.11 = (bf16[96,2048]{1,0:T(8,128)(2,1)}, bf16[96,2048]{1,0:T(8,128)(2,1)S(1)}, u32[]{:S(2)}, u32[]{:S(2)}) collective-permute-start(bf16[96,2048]{1,0:T(8,128)(2,1)} %get-tuple-element.35), channel_id=1, source_target_pairs={{0,20},{4,16},{8,28},{12,24},{16,4},{20,0},{24,12},{28,8},{1,21},{... | collective-permute-start | bytes 1179656 | tf_op jit(solution)/shard_map/ppermute | solution.py:73
  15.7 31.5 %collective-permute-start.12 = (bf16[96,2048]{1,0:T(8,128)(2,1)S(1)}, bf16[96,2048]{1,0:T(8,128)(2,1)S(1)}, u32[]{:S(2)}, u32[]{:S(2)}) collective-permute-start(bf16[96,2048]{1,0:T(8,128)(2,1)S(1)} %copy-done.9), channel_id=1, source_target_pairs={{0,24},{4,28},{8,16},{12,20},{16,8},{20,12},{24,0},{28,4},{1,25},{... | collective-permute-start | bytes 1179656 | tf_op jit(solution)/shard_map/ppermute | solution.py:73
  19.0 29.9 %collective-permute-start.13 = (bf16[96,2048]{1,0:T(8,128)(2,1)S(1)}, bf16[96,2048]{1,0:T(8,128)(2,1)S(1)}, u32[]{:S(2)}, u32[]{:S(2)}) collective-permute-start(bf16[96,2048]{1,0:T(8,128)(2,1)S(1)} %copy-done.6), channel_id=1, source_target_pairs={{0,28},{4,24},{8,20},{12,16},{16,12},{20,8},{24,4},{28,0},{1,29},{... | collective-permute-start | bytes 1179656 | tf_op jit(solution)/shard_map/ppermute | solution.py:73
  27.0 30.5 %collective-permute-start = (bf16[96,2048]{1,0:T(8,128)(2,1)S(1)}, bf16[96,2048]{1,0:T(8,128)(2,1)S(1)}, u32[]{:S(2)}, u32[]{:S(2)}) collective-permute-start(bf16[96,2048]{1,0:T(8,128)(2,1)S(1)} %copy-done.13), channel_id=1, source_target_pairs={{0,4},{4,0},{8,12},{12,8},{16,20},{20,16},{24,28},{28,24},{1,5},{5... | collective-permute-start | bytes 1179656 | tf_op jit(solution)/shard_map/ppermute | solution.py:73
  27.6 31.2 %collective-permute-start.1 = (bf16[96,2048]{1,0:T(8,128)(2,1)S(1)}, bf16[96,2048]{1,0:T(8,128)(2,1)S(1)}, u32[]{:S(2)}, u32[]{:S(2)}) collective-permute-start(bf16[96,2048]{1,0:T(8,128)(2,1)S(1)} %copy-done.12), channel_id=1, source_target_pairs={{0,8},{4,12},{8,0},{12,4},{16,24},{20,28},{24,16},{28,20},{1,9},{5... | collective-permute-start | bytes 1179656 | tf_op jit(solution)/shard_map/ppermute | solution.py:73
  45.1 15.5 %collective-permute-start.2 = (bf16[96,2048]{1,0:T(8,128)(2,1)S(1)}, bf16[96,2048]{1,0:T(8,128)(2,1)S(1)}, u32[]{:S(2)}, u32[]{:S(2)}) collective-permute-start(bf16[96,2048]{1,0:T(8,128)(2,1)S(1)} %copy-done.11), channel_id=1, source_target_pairs={{0,12},{4,8},{8,4},{12,0},{16,28},{20,24},{24,20},{28,16},{1,13},{... | collective-permute-start | bytes 1179656 | tf_op jit(solution)/shard_map/ppermute | solution.py:73
  47.2 13.4 %collective-permute-start.3 = (bf16[96,2048]{1,0:T(8,128)(2,1)S(1)}, bf16[96,2048]{1,0:T(8,128)(2,1)S(1)}, u32[]{:S(2)}, u32[]{:S(2)}) collective-permute-start(bf16[96,2048]{1,0:T(8,128)(2,1)S(1)} %copy-done.10), channel_id=1, source_target_pairs={{0,16},{4,20},{8,24},{12,28},{16,0},{20,4},{24,8},{28,12},{1,17},{... | collective-permute-start | bytes 1179656 | tf_op jit(solution)/shard_map/ppermute | solution.py:73
  48.9 33.6 %collective-permute-start.4 = (bf16[96,2048]{1,0:T(8,128)(2,1)S(1)}, bf16[96,2048]{1,0:T(8,128)(2,1)S(1)}, u32[]{:S(2)}, u32[]{:S(2)}) collective-permute-start(bf16[96,2048]{1,0:T(8,128)(2,1)S(1)} %copy-done.8), channel_id=1, source_target_pairs={{0,20},{4,16},{8,28},{12,24},{16,4},{20,0},{24,12},{28,8},{1,21},{... | collective-permute-start | bytes 1179656 | tf_op jit(solution)/shard_map/ppermute | solution.py:73
  57.5 24.9 %collective-permute-start.5 = (bf16[96,2048]{1,0:T(8,128)(2,1)S(1)}, bf16[96,2048]{1,0:T(8,128)(2,1)S(1)}, u32[]{:S(2)}, u32[]{:S(2)}) collective-permute-start(bf16[96,2048]{1,0:T(8,128)(2,1)S(1)} %copy-done.7), channel_id=1, source_target_pairs={{0,24},{4,28},{8,16},{12,20},{16,8},{20,12},{24,0},{28,4},{1,25},{... | collective-permute-start | bytes 1179656 | tf_op jit(solution)/shard_map/ppermute | solution.py:73
  58.8 23.7 %collective-permute-start.6 = (bf16[96,2048]{1,0:T(8,128)(2,1)S(1)}, bf16[96,2048]{1,0:T(8,128)(2,1)S(1)}, u32[]{:S(2)}, u32[]{:S(2)}) collective-permute-start(bf16[96,2048]{1,0:T(8,128)(2,1)S(1)} %copy-done.5), channel_id=1, source_target_pairs={{0,28},{4,24},{8,20},{12,16},{16,12},{20,8},{24,4},{28,0},{1,29},{... | collective-permute-start | bytes 1179656 | tf_op jit(solution)/shard_map/ppermute | solution.py:73
  102.3 9.2 %collective-permute-start.14 = (bf16[96,2048]{1,0:T(8,128)(2,1)S(1)}, bf16[96,2048]{1,0:T(8,128)(2,1)S(1)}, u32[]{:S(2)}, u32[]{:S(2)}) collective-permute-start(bf16[96,2048]{1,0:T(8,128)(2,1)S(1)} %get-tuple-element.46), channel_id=1, source_target_pairs={{0,4},{4,0},{8,12},{12,8},{16,20},{20,16},{24,28},{28,24},{1,5},{5... | collective-permute-start | bytes 1179656 | tf_op jit(solution)/shard_map/ppermute | solution.py:73
  103.0 12.0 %collective-permute-start.15 = (bf16[96,2048]{1,0:T(8,128)(2,1)S(1)}, bf16[96,2048]{1,0:T(8,128)(2,1)S(1)}, u32[]{:S(2)}, u32[]{:S(2)}) collective-permute-start(bf16[96,2048]{1,0:T(8,128)(2,1)S(1)} %get-tuple-element.45), channel_id=1, source_target_pairs={{0,8},{4,12},{8,0},{12,4},{16,24},{20,28},{24,16},{28,20},{1,9},{5... | collective-permute-start | bytes 1179656 | tf_op jit(solution)/shard_map/ppermute | solution.py:73
  108.8 12.9 %collective-permute-start.16 = (bf16[96,2048]{1,0:T(8,128)(2,1)S(1)}, bf16[96,2048]{1,0:T(8,128)(2,1)S(1)}, u32[]{:S(2)}, u32[]{:S(2)}) collective-permute-start(bf16[96,2048]{1,0:T(8,128)(2,1)S(1)} %get-tuple-element.44), channel_id=1, source_target_pairs={{0,12},{4,8},{8,4},{12,0},{16,28},{20,24},{24,20},{28,16},{1,13},{... | collective-permute-start | bytes 1179656 | tf_op jit(solution)/shard_map/ppermute | solution.py:73
  109.4 12.3 %collective-permute-start.17 = (bf16[96,2048]{1,0:T(8,128)(2,1)S(1)}, bf16[96,2048]{1,0:T(8,128)(2,1)S(1)}, u32[]{:S(2)}, u32[]{:S(2)}) collective-permute-start(bf16[96,2048]{1,0:T(8,128)(2,1)S(1)} %get-tuple-element.43), channel_id=1, source_target_pairs={{0,16},{4,20},{8,24},{12,28},{16,0},{20,4},{24,8},{28,12},{1,17},{... | collective-permute-start | bytes 1179656 | tf_op jit(solution)/shard_map/ppermute | solution.py:73
  111.2 35.0 %collective-permute-start.18 = (bf16[96,2048]{1,0:T(8,128)(2,1)S(1)}, bf16[96,2048]{1,0:T(8,128)(2,1)S(1)}, u32[]{:S(2)}, u32[]{:S(2)}) collective-permute-start(bf16[96,2048]{1,0:T(8,128)(2,1)S(1)} %get-tuple-element.42), channel_id=1, source_target_pairs={{0,20},{4,16},{8,28},{12,24},{16,4},{20,0},{24,12},{28,8},{1,21},{... | collective-permute-start | bytes 1179656 | tf_op jit(solution)/shard_map/ppermute | solution.py:73
  111.5 34.7 %collective-permute-start.19 = (bf16[96,2048]{1,0:T(8,128)(2,1)S(1)}, bf16[96,2048]{1,0:T(8,128)(2,1)S(1)}, u32[]{:S(2)}, u32[]{:S(2)}) collective-permute-start(bf16[96,2048]{1,0:T(8,128)(2,1)S(1)} %get-tuple-element.41), channel_id=1, source_target_pairs={{0,24},{4,28},{8,16},{12,20},{16,8},{20,12},{24,0},{28,4},{1,25},{... | collective-permute-start | bytes 1179656 | tf_op jit(solution)/shard_map/ppermute | solution.py:73
  114.9 31.3 %collective-permute-start.20 = (bf16[96,2048]{1,0:T(8,128)(2,1)S(1)}, bf16[96,2048]{1,0:T(8,128)(2,1)S(1)}, u32[]{:S(2)}, u32[]{:S(2)}) collective-permute-start(bf16[96,2048]{1,0:T(8,128)(2,1)S(1)} %get-tuple-element.40), channel_id=1, source_target_pairs={{0,28},{4,24},{8,20},{12,16},{16,12},{20,8},{24,4},{28,0},{1,29},{... | collective-permute-start | bytes 1179656 | tf_op jit(solution)/shard_map/ppermute | solution.py:73
  147.4 13.4 %collective-permute-start.21 = (bf16[256,512]{1,0:T(8,128)(2,1)S(1)}, bf16[256,512]{1,0:T(8,128)(2,1)S(1)}, u32[]{:S(2)}, u32[]{:S(2)}) collective-permute-start(bf16[256,512]{1,0:T(8,128)(2,1)S(1)} %get-tuple-element.48), channel_id=1, source_target_pairs={{0,1},{1,0},{2,3},{3,2},{4,5},{5,4},{6,7},{7,6},{8,9},{9,8},{10,11... | collective-permute-start | bytes 786440 | tf_op jit(solution)/shard_map/ppermute | solution.py:73
  149.1 21.3 %collective-permute-start.22 = (bf16[256,512]{1,0:T(8,128)(2,1)S(1)}, bf16[256,512]{1,0:T(8,128)(2,1)S(1)}, u32[]{:S(2)}, u32[]{:S(2)}) collective-permute-start(bf16[256,512]{1,0:T(8,128)(2,1)S(1)} %get-tuple-element.50), channel_id=1, source_target_pairs={{0,2},{1,3},{2,0},{3,1},{4,6},{5,7},{6,4},{7,5},{8,10},{9,11},{10,... | collective-permute-start | bytes 786440 | tf_op jit(solution)/shard_map/ppermute | solution.py:73
  151.7 18.7 %collective-permute-start.23 = (bf16[256,512]{1,0:T(8,128)(2,1)S(1)}, bf16[256,512]{1,0:T(8,128)(2,1)S(1)}, u32[]{:S(2)}, u32[]{:S(2)}) collective-permute-start(bf16[256,512]{1,0:T(8,128)(2,1)S(1)} %get-tuple-element.49), channel_id=1, source_target_pairs={{0,3},{1,2},{2,1},{3,0},{4,7},{5,6},{6,5},{7,4},{8,11},{9,10},{10,... | collective-permute-start | bytes 786440 | tf_op jit(solution)/shard_map/ppermute | solution.py:73
  (19 other events, 315.6 us)

commit v2 on v0

v2 whole, which is shorter than its diff:
```python
import functools

import jax
import jax.numpy as jnp
from jax import lax
from jax.experimental import pallas as pl
from jax.experimental.pallas import tpu as pltpu
from jax.sharding import PartitionSpec as P

F32 = jnp.float32
BF16 = jnp.bfloat16
VMEM_LIMIT = 20 * 1024 * 1024
AWAY_FLOPS = 2 * 10**9


def contract(left, right, left_dim, right_dim):
    return lax.dot_general(
        left, right, (((left_dim,), (right_dim,)), ((), ())), preferred_element_type=F32
    )


def like(*shape, dtype=BF16):
    return jax.ShapeDtypeStruct(shape, dtype)


def call(kernel, name, where, args, in_specs, out_shape, out_specs, grid, flops, kept=()):
    moved = sum(a.size * a.dtype.itemsize for a in (*args, *out_shape)) // (2 if kept else 1)
    args = (*kept, *args)
    in_specs = [pl.BlockSpec(memory_space=pl.ANY)] * len(kept) + in_specs

    def inner(where, *refs):
        kernel(where, *refs[len(kept) :])

    return pl.pallas_call(
        inner,
        input_output_aliases={i + 1: i for i in range(len(kept))},
        grid_spec=pltpu.PrefetchScalarGridSpec(
            num_scalar_prefetch=1, grid=grid, in_specs=in_specs, out_specs=out_specs
        ),
        out_shape=out_shape,
        name=name,
        compiler_params=pltpu.CompilerParams(vmem_limit_bytes=VMEM_LIMIT),
        cost_estimate=pl.CostEstimate(flops=flops // 64, bytes_accessed=moved // 64, transcendentals=0),
    )(where, *args)


def whole(array):
    return pl.BlockSpec(array.shape, lambda *_: (0,) * len(array.shape))


class Plan:
    def __init__(self, experts):
        chips = experts // 2
        by_hops = sorted(range(1, chips), key=lambda c: (-c.bit_count(), c))
        self.experts = experts
        self.far = sorted(by_hops[: chips // 2 - 1])
        self.near = sorted(by_hops[chips // 2 - 1 :])
        self.chips = [0] + self.far + self.near


def after(array, *earlier):
    return lax.optimization_barrier((array, *earlier))[0]


def place_kernel(plan, cap, with_gate, where, *refs):
    metas, tables, outs = refs[:2], refs[2:4], refs[4:]
    chips, experts = len(plan.chips), plan.experts
    toks, width = tables[0].shape
    half = pl.ds(pl.multiple_of((where[1] & 1) * (width // 2), 128), width // 2)
    earlier = (
        lax.broadcasted_iota(jnp.int32, (toks, toks), 0)
        < lax.broadcasted_iota(jnp.int32, (toks, toks), 1)
    ).astype(BF16)
    slot = lax.broadcasted_iota(jnp.int32, (cap, toks), 0)
    for side in range(2):
        ids = metas[side][0:2, :].astype(jnp.int32) ^ where[0]
        ids0, ids1 = ids[0:1, :], ids[1:2, :]
        rel = lax.broadcasted_iota(jnp.int32, (experts, toks), 0)
        match = (rel == ids0) | (rel == ids1)
        rank = jnp.dot(match.astype(BF16), earlier, preferred_element_type=F32).astype(jnp.int32)
        rank = jnp.where(match, rank, -1)
        for place, chip in enumerate(plan.chips):
            d = 2 * chip
            placing = slot == rank[d : d + 1, :]
            rows = tables[side][:, half] if chip in plan.far else tables[side][...]
            block = jnp.dot(placing.astype(BF16), rows, preferred_element_type=F32)
            if with_gate:
                gate = jnp.where(ids0 == d, metas[side][2:3, :], metas[side][3:4, :])
                slot_gate = jnp.sum(jnp.where(placing, gate, 0.0), axis=1, keepdims=True)
                block = block * slot_gate
            else:
                outs[chips + side][place * cap : (place + 1) * cap, :] = placing.astype(BF16)
            outs[chip][side * cap : (side + 1) * cap, :] = block.astype(BF16)


def place(plan, where, metas, tables, cap, with_gate):
    toks, width = tables[0].shape
    chips = len(plan.chips)
    outs = [like(2 * cap, width // 2 if c in plan.far else width) for c in range(chips)]
    if not with_gate:
        outs = outs + [like(chips * cap, toks)] * 2
    args = (*metas, *tables)
    return call(
        functools.partial(place_kernel, plan, cap, with_gate),
        "place_scaled" if with_gate else "place_tokens",
        where,
        args,
        [whole(a) for a in args],
        outs,
        [whole(o) for o in outs],
        (1,),
        2 * plan.experts * cap * toks * width,
    )


def gather_blocks(where, out_ref, full, halves, others):
    cap = full[0].shape[0]
    width = out_ref.shape[1]
    part = width // 2
    for i, block in enumerate(full):
        out_ref[i * cap : (i + 1) * cap, :] = block[...]
    if not halves:
        return
    mine = pl.ds(pl.multiple_of((where[1] & 1) * part, 128), part)
    theirs = pl.ds(pl.multiple_of((1 - (where[1] & 1)) * part, 128), part)
    base = len(full) * cap
    for i, block in enumerate(halves):
        out_ref[base + i * cap : base + (i + 1) * cap, mine] = block[...]
    out_ref[base : base + len(halves) * cap, theirs] = others[...]


def split_refs(refs, n_full, n_halves):
    full = refs[:n_full]
    halves = refs[n_full : n_full + n_halves]
    rest = refs[n_full + n_halves :]
    if n_halves:
        return full, halves, rest[0], rest[1:]
    return full, halves, None, rest


def forward_kernel(n_full, n_halves, where, *refs):
    full, halves, others, rest = split_refs(refs, n_full, n_halves)
    gate_ref, up_ref, rows_ref, hidden_ref, to_a_ref, to_b_ref = rest

    @pl.when(pl.program_id(0) == 0)
    def _():
        gather_blocks(where, rows_ref, full, halves, others)

    rows = rows_ref[...]
    pre_gate = jnp.dot(rows, gate_ref[0], preferred_element_type=F32)
    pre_up = jnp.dot(rows, up_ref[0], preferred_element_type=F32)
    squash = jax.nn.sigmoid(pre_gate)
    swish = squash * pre_gate
    hidden_ref[...] = (swish * pre_up).astype(BF16)
    to_a_ref[...] = pre_up * squash * (1.0 + pre_gate * (1.0 - squash))
    to_b_ref[...] = swish


def forward(name, where, chunk, full, halves, others, w_gate, w_up, kept=()):
    cap, width = full[0].shape
    count = (len(full) + len(halves)) * cap
    rows = 2 * count
    units = w_gate.shape[2]
    tile = 256
    blocks = [*full, *halves, *others]
    column = pl.BlockSpec((1, width, tile), lambda j, _: (0, 0, j))
    out_column = pl.BlockSpec((count, tile), lambda j, _: (0, j))
    outs = [
        like(rows, width),
        like(rows, units),
        like(count, units, dtype=F32),
        like(count, units, dtype=F32),
    ]
    return call(
        functools.partial(forward_kernel, len(full), len(halves)),
        name,
        where,
        (*blocks, w_gate, w_up),
        [whole(b) for b in blocks] + [column, column],
        outs,
        [
            pl.BlockSpec((count, width), lambda j, _: (chunk, 0)),
            pl.BlockSpec((count, tile), lambda j, _: (chunk, j)),
            out_column,
            out_column,
        ],
        (units // tile,),
        4 * count * width * units,
        kept,
    )


def backward_kernel(n_full, n_halves, where, *refs):
    full, halves, others, rest = split_refs(refs, n_full, n_halves)
    down_ref, to_a_ref, to_b_ref, rows_ref, grad_a_ref, grad_b_ref = rest

    @pl.when(pl.program_id(0) == 0)
    def _():
        gather_blocks(where, rows_ref, full, halves, others)

    grad_hidden = contract(rows_ref[...], down_ref[0], 1, 1)
    grad_a_ref[...] = (grad_hidden * to_a_ref[...]).astype(BF16)
    grad_b_ref[...] = (grad_hidden * to_b_ref[...]).astype(BF16)


def backward(name, where, chunk, full, halves, others, w_down, to_a, to_b, kept=()):
    cap, width = full[0].shape
    count = (len(full) + len(halves)) * cap
    rows = 2 * count
    units = w_down.shape[1]
    tile = 256
    blocks = [*full, *halves, *others]
    column = pl.BlockSpec((count, tile), lambda j, _: (0, j))
    out_column = pl.BlockSpec((count, tile), lambda j, _: (chunk, j))
    outs = [like(rows, width), like(rows, units), like(rows, units)]
    return call(
        functools.partial(backward_kernel, len(full), len(halves)),
        name,
        where,
        (*blocks, w_down, to_a, to_b),
        [whole(b) for b in blocks]
        + [pl.BlockSpec((1, tile, width), lambda j, _: (0, j, 0)), column, column],
        outs,
        [pl.BlockSpec((count, width), lambda j, _: (chunk, 0)), out_column, out_column],
        (units // tile,),
        2 * count * width * units,
        kept,
    )


def input_grad(grad_a_ref, grad_b_ref, gate_ref, up_ref):
    return contract(grad_a_ref[...], gate_ref[0], 1, 1) + contract(
        grad_b_ref[...], up_ref[0], 1, 1
    )


def first_grad_kernel(cap, where, grad_a_ref, grad_b_ref, gate_ref, up_ref, *outs):
    own_ref, give_ref, keep_ref = outs
    part = input_grad(grad_a_ref, grad_b_ref, gate_ref, up_ref)
    own_ref[...] = part[: 2 * cap].astype(BF16)
    far = part[2 * cap :]
    step, steps = pl.program_id(0), pl.num_programs(0)

    @pl.when(step < steps // 2)
    def _():
        give_ref[...] = far.astype(BF16)

    @pl.when(step >= steps // 2)
    def _():
        keep_ref[...] = far


def first_grad(plan, where, grad_a, grad_b, w_gate, w_up, dp, cap):
    width, units = w_gate.shape[1:]
    slab = width // dp
    far = 2 * len(plan.far) * cap

    def at(i, where):
        parity = where[1] & 1
        late = jnp.where(i < dp // 2, 1 - parity, parity)
        return 2 * lax.rem(i, dp // 2) + late

    weight = pl.BlockSpec((1, slab, units), lambda i, where: (0, at(i, where), 0))
    chunk = pl.BlockSpec((grad_a.shape[0] // 2, units), lambda i, where: (0, 0))
    outs = [
        like(2 * cap, width),
        like(far, width // 2),
        like(far, width // 2, dtype=F32),
    ]
    return call(
        functools.partial(first_grad_kernel, cap),
        "own_and_far_input_grads",
        where,
        (grad_a, grad_b, w_gate, w_up),
        [chunk, chunk, weight, weight],
        outs,
        [
            pl.BlockSpec((2 * cap, slab), lambda i, where: (0, at(i, where))),
            pl.BlockSpec((far, slab), lambda i, where: (0, jnp.minimum(i, dp // 2 - 1))),
            pl.BlockSpec((far, slab), lambda i, where: (0, jnp.maximum(i - dp // 2, 0))),
        ],
        (dp,),
        2 * grad_a.shape[0] * width * units,
    )


def near_grad_kernel(cap, where, grad_a_ref, grad_b_ref, gate_ref, up_ref, *outs):
    part = input_grad(grad_a_ref, grad_b_ref, gate_ref, up_ref)
    for i, out in enumerate(outs):
        out[...] = part[2 * i * cap : 2 * (i + 1) * cap].astype(BF16)


def near_grad(plan, where, grad_a, grad_b, w_gate, w_up, dp, cap, away):
    width, units = w_gate.shape[1:]
    tile = width // 4
    steps = 2

    def at(i, where):
        side = (where[1] >= dp // 2).astype(jnp.int32)
        return steps * (1 - side if away else side) + i

    weight = pl.BlockSpec((1, tile, units), lambda i, where: (0, at(i, where), 0))
    chunk = pl.BlockSpec((grad_a.shape[0] // 2, units), lambda i, where: (1, 0))
    outs = [like(2 * cap, width // 2)] * len(plan.near)
    return call(
        functools.partial(near_grad_kernel, cap),
        "near_input_grads",
        where,
        (grad_a, grad_b, w_gate, w_up),
        [chunk, chunk, weight, weight],
        outs,
        [pl.BlockSpec((2 * cap, tile), lambda i, where: (0, i))] * len(plan.near),
        (steps,),
        grad_a.shape[0] * width * units,
    )


def outer_kernel(n_right, where, left_ref, *refs):
    left = left_ref[...].T
    for right, out in zip(refs[:n_right], refs[n_right:], strict=True):
        out[0] = jnp.dot(left, right[...], preferred_element_type=F32).astype(BF16)


def outer(name, where, left, rights, part=0, parts=1, kept=()):
    rows, width = left.shape
    tile = 256
    steps = width // tile // parts
    first = part * steps
    outs = [like(1, width, r.shape[1]) for r in rights]
    return call(
        functools.partial(outer_kernel, len(rights)),
        name,
        where,
        (left, *rights),
        [pl.BlockSpec((rows, tile), lambda i, _: (0, first + i))] + [whole(r) for r in rights],
        outs,
        [pl.BlockSpec((1, tile, o.shape[2]), lambda i, _: (0, first + i, 0)) for o in outs],
        (steps,),
        2 * rows * width * sum(o.shape[2] for o in outs) // parts,
        kept,
    )


def combine_kernel(plan, cap, dp, shifts, side_by_side, where, *refs):
    chips = len(plan.chips)
    placings, blocks, outs, rows_ref = refs[:2], refs[2 : 2 + chips], refs[2 + chips : -1], refs[-1]
    slab = rows_ref.shape[1]
    side_rows = chips * cap
    for n, shift in enumerate(shifts):
        to = where[1] ^ shift
        for place, (chip, block) in enumerate(zip(plan.chips, blocks, strict=True)):
            if chip == 0:
                column = to
            elif chip in plan.far:
                column = to >> 1
            else:
                column = lax.rem(to, dp // 2)
            column = pl.ds(pl.multiple_of(column * slab, 128), slab)
            for side in range(2):
                base = side * side_rows + place * cap
                if chip in plan.far and shift % 2:
                    rows_ref[base : base + cap, :] = jnp.zeros((cap, slab), BF16)
                else:
                    rows_ref[base : base + cap, :] = block[side * cap : (side + 1) * cap, column]
        own = contract(placings[0][...], rows_ref[:side_rows, :], 0, 0)
        other = contract(placings[1][...], rows_ref[side_rows:, :], 0, 0)
        if side_by_side:
            outs[0][:, n * slab : (n + 1) * slab] = own
            outs[1][:, n * slab : (n + 1) * slab] = other.astype(BF16)
        else:
            outs[2 * n][...] = own.astype(outs[2 * n].dtype)
            outs[2 * n + 1][...] = other.astype(BF16)


def combine(plan, where, placings, blocks, dp, cap, shifts, side_by_side):
    width = blocks[0].shape[1]
    slab = width // dp
    toks = placings[0].shape[1]
    args = (*placings, *blocks)
    if side_by_side:
        outs = [like(toks, slab * len(shifts), dtype=F32), like(toks, slab * len(shifts))]
    else:
        pairs = [[like(toks, slab, dtype=BF16 if s else F32), like(toks, slab)] for s in shifts]
        outs = [o for pair in pairs for o in pair]
    moved = sum(a.size * a.dtype.itemsize for a in args)
    flops = 4 * placings[0].size * slab * len(shifts)
    return pl.pallas_call(
        functools.partial(combine_kernel, plan, cap, dp, shifts, side_by_side),
        grid_spec=pltpu.PrefetchScalarGridSpec(
            num_scalar_prefetch=1,
            grid=(1,),
            in_specs=[whole(a) for a in args],
            out_specs=[whole(o) for o in outs],
            scratch_shapes=[pltpu.VMEM((plan.experts * cap, slab), BF16)],
        ),
        out_shape=outs,
        name="combine_away" if side_by_side else "combine_here",
        compiler_params=pltpu.CompilerParams(vmem_limit_bytes=VMEM_LIMIT),
        cost_estimate=pl.CostEstimate(
            flops=flops // 64, bytes_accessed=moved // 64, transcendentals=0
        ),
    )(where, *args)


def sum_kernel(*refs):
    *parts, out = refs
    out[...] = functools.reduce(lambda a, b: a + b, [p[...].astype(F32) for p in parts])


def add_up(parts):
    out = like(*parts[0].shape, dtype=F32)
    return pl.pallas_call(
        sum_kernel,
        out_shape=out,
        name="add_up",
        compiler_params=pltpu.CompilerParams(vmem_limit_bytes=VMEM_LIMIT),
        cost_estimate=pl.CostEstimate(
            flops=AWAY_FLOPS, bytes_accessed=2 * out.size, transcendentals=0
        ),
    )(*parts)


def swap(rows, axis, mask):
    count = lax.axis_size(axis)
    return lax.ppermute(rows, axis, [(i, i ^ mask) for i in range(count)])


def cross(rows, shift):
    dp = lax.axis_size("dp")
    count = lax.axis_size("expert") * dp
    return lax.ppermute(rows, ("expert", "dp"), [(i, i ^ (dp + shift)) for i in range(count)])


def body(tokens, grad_out, expert_ids, gate_vals, w_gate, w_up, w_down):
    plan = Plan(lax.axis_size("expert"))
    dp = lax.axis_size("dp")
    toks, width = tokens.shape
    cap = 3 * toks // plan.experts
    where = jnp.stack([lax.axis_index("expert"), lax.axis_index("dp")]).astype(jnp.int32)
    meta = jnp.concatenate([expert_ids.T.astype(F32), gate_vals.T], axis=0)
    meta_other = swap(meta, "expert", 1)
    tokens_other = swap(tokens, "expert", 1)
    out_other = swap(grad_out, "expert", 1)
    metas = (meta, meta_other)
    *x, placing, placing_other = place(plan, where, metas, (tokens, tokens_other), cap, False)
    r = list(place(plan, where, metas, (grad_out, out_other), cap, True))
    placings = (placing, placing_other)

    def over(blocks, which):
        for c in which:
            blocks[c] = swap(blocks[c], "expert", 2 * c)

    def share(blocks):
        return [swap(jnp.concatenate([blocks[c] for c in plan.far], axis=0), "dp", 1)]

    def pick(blocks, which):
        return [blocks[c] for c in which]

    over(x, plan.far)
    over(r, plan.far)
    x_others, r_others = share(x), share(r)
    over(x, plan.near)
    for c in plan.near:
        r[c] = after(r[c], *x_others)
    over(r, plan.near)

    x_all, hidden, to_a, to_b = forward(
        "forward_own_and_far", where, 0, pick(x, [0]), pick(x, plan.far), x_others, w_gate, w_up
    )
    r_all, grad_a, grad_b = backward(
        "backward_own_and_far", where, 0, pick(r, [0]), pick(r, plan.far), r_others, w_down, to_a, to_b
    )
    own, give, keep = first_grad(plan, where, grad_a, grad_b, w_gate, w_up, dp, cap)
    got = swap(give, "dp", 1)

    x_all, hidden, to_a, to_b = forward(
        "forward_near", where, 1, pick(x, plan.near), [], [], w_gate, w_up, (after(x_all, give), hidden)
    )
    far_sum = (keep + after(got, hidden, *pick(r, plan.near)).astype(F32)).astype(BF16)
    rows = 2 * cap
    far = [swap(far_sum[i * rows : (i + 1) * rows], "expert", 2 * c) for i, c in enumerate(plan.far)]
    kept = (after(r_all, far_sum), after(grad_a, give), after(grad_b, give))
    r_all, grad_a, grad_b = backward(
        "backward_near", where, 1, pick(r, plan.near), [], [], w_down, to_a, to_b, kept
    )
    away_part = near_grad(plan, where, grad_a, grad_b, w_gate, w_up, dp, cap, True)
    here_part = near_grad(plan, where, after(grad_a, *far), grad_b, w_gate, w_up, dp, cap, False)

    def send_back(part):
        return [swap(b, "expert", 2 * c) for b, c in zip(part, plan.near, strict=True)]

    away_rows, here_rows = send_back(away_part), send_back(here_part)
    slab = width // dp
    away, here = list(range(dp // 2, dp)), list(range(dp // 2))

    (grad_down,) = outer("down_grad", where, after(hidden, here_part[0]), [r_all])
    away_rows[0] = after(away_rows[0], grad_down)
    away_sum, other = combine(
        plan, where, placings, [own, *far, *away_rows], dp, cap, away, True
    )
    other = swap(other, "expert", 1)
    grads = outer("gate_and_up_grads", where, after(x_all, away_sum), [grad_a, grad_b], 0, 4)
    away_sum = (away_sum + after(other, grads[0]).astype(F32)).astype(BF16)
    parts = [away_sum[:, n * slab : (n + 1) * slab] for n in range(len(away))]
    grads = outer("gate_and_up_grads", where, after(x_all, *parts), [grad_a, grad_b], 1, 4, grads)
    away_sums = [swap(part, "dp", s) for part, s in zip(parts, away, strict=True)]
    here_rows[0] = after(here_rows[0], grads[0])
    total, other, *rest = combine(
        plan, where, placings, [own, *far, *here_rows], dp, cap, here, False
    )
    got = [swap(other, "expert", 1)]
    for n, s in enumerate(here[1:]):
        got += [swap(rest[2 * n], "dp", s), cross(rest[2 * n + 1], s)]
    grads = outer("gate_and_up_grads", where, after(x_all, total), [grad_a, grad_b], 2, 4, grads)
    grad_gate, grad_up = outer("gate_and_up_grads", where, x_all, [grad_a, grad_b], 3, 4, grads)
    total = total + add_up(away_sums)
    for part in got:
        total = total + part.astype(F32)
    return (total.astype(BF16), grad_gate, grad_up, grad_down)


def solution(mesh):
    in_specs = (
        P("expert", None),
        P("expert", None),
        P("expert", None),
        P("expert", None),
        P("expert", None, "dp"),
        P("expert", None, "dp"),
        P("expert", "dp", None),
    )
    out_specs = (
        P("expert", "dp"),
        P("expert", None, "dp"),
        P("expert", None, "dp"),
        P("expert", "dp", None),
    )
    return jax.shard_map(body, mesh=mesh, in_specs=in_specs, out_specs=out_specs, check_vma=False)
```

time: 274 us -> 124 us (0.45)
  waiting for transfers between devices: 161 us -> 34.6 us
  matrix products: 60.2 us -> 0 us
  Pallas kernels: 0 us -> 57.1 us
  local copies, waits for them, and re-layouts: 20.9 us -> 4.69 us
  between operations: 14.2 us -> 0.83 us
  starting transfers between devices: 13.5 us -> 23.8 us
    reduce_scatter x1 -> x0, waiting for transfers between devices: 103 us -> none  [body(): lax.psum_scatter(partial_sum, 'dp', scatter_dimension=0, tiled=True)]
    dot_general x10 -> x0, matrix products: 60.2 us -> none  [the longest x6 35.9 us: contract(): lax.dot_general(left, right, (((left_dim,), (right_dim,)), ((), ())), pre...]
    all_to_all x3 -> x0, waiting for transfers between devices: 57.7 us -> none  [the longest x1 30.6 us: body(): lax.all_to_all(send_r, 'expert', split_axis=0, concat_axis=0, tiled=True)]
    pallas_call x0 -> x17, Pallas kernels: none -> 57.1 us  [the longest x14 54.5 us: call(): pl.pallas_call(inner, input_output_aliases={i + 1: i for i in range(len(k...]
    ppermute x0 -> x23, waiting for transfers between devices: none -> 34.6 us  [the longest x22 33.4 us: swap(): return lax.ppermute(rows, axis, [(i, i ^ mask) for i in range(count)])]
    ppermute x0 -> x23, starting transfers between devices: none -> 23.8 us  [the longest x22 23.7 us: swap(): return lax.ppermute(rows, axis, [(i, i ^ mask) for i in range(count)])]
    all_to_all x3 -> x0, starting transfers between devices: 13.4 us -> none  [the longest x1 5.17 us: body(): lax.all_to_all(send_x, 'expert', split_axis=0, concat_axis=0, tiled=True)]
    broadcast_in_dim x2 -> x0, local copies, waits for them, and re-layouts: 7.86 us -> none  [the longest x1 5.37 us: body(): jnp.repeat(grad_out, TOP, axis=0).astype(jnp.float32)]
  transfers between devices with their start and end apart: 4 -> 23, of which waited for: 4 -> 9; matrix products, arithmetic and copies ran while one was open for 17% -> 1% of each run, Pallas kernels for 0% -> 45%
where the time goes in v2:
time: 124 us
  Pallas kernels  57.1 us (46%)
  waiting for transfers between devices  34.6 us (28%)
  starting transfers between devices  23.8 us (19%)
  local copies, waits for them, and re-layouts  4.69 us (4%)
  other arithmetic  2.6 us (2%)
    pallas_call x14, Pallas kernels, call(): pl.pallas_call(inner, input_output_aliases={i + 1: i for i in range(len(k...  54.5 us
    ppermute x22, waiting for transfers between devices, swap(): return lax.ppermute(rows, axis, [(i, i ^ mask) for i in range(count)])  33.4 us
    ppermute x22, starting transfers between devices, swap(): return lax.ppermute(rows, axis, [(i, i ^ mask) for i in range(count)])  23.7 us
    unnamed x12, local copies, waits for them, and re-layouts  4.65 us
    pallas_call x2, Pallas kernels, combine(): pl.pallas_call(functools.partial(combine_kernel, plan, cap, dp, shifts, s...  2.53 us
  transfers between devices with their start and end apart: 23, of which 9 were waited for; matrix products, arithmetic and copies ran while one was open for 1% of the time, Pallas kernels for 45%

profile of v2, /device:TPU:0, one launch (start us, length us, event | category | flops | bytes accessed | tf_op | source)
XLA Modules:
  0.0 123.7 jit_solution(12324518341581110638)
XLA Ops:
  3.1 1.8 %collective-permute-done.refs_1_ = f32[4,256]{1,0:T(4,128)S(1)} collective-permute-done((f32[4,256]{1,0:T(4,128)S(1)}, f32[4,256]{1,0:T(4,128)S(1)}, u32[]{:S(2)}, u32[]{:S(2)}) %collective-permute-start) | collective-permute-done | bytes 4128 | tf_op jit(solution)/shard_map/ppermute | solution.py:425
  6.2 2.1 %place_tokens.1 = (bf16[192,2048]{1,0:T(8,128)(2,1)S(1)}, bf16[192,2048]{1,0:T(8,128)(2,1)S(1)}, bf16[192,2048]{1,0:T(8,128)(2,1)S(1)}, bf16[192,1024]{1,0:T(8,1...) custom-call(s32[2]{0:T(128)S(1)} %pad_add_fusion.where, f32[4,256]{1,0:T(4,128)S(1)} %pad_maximum_fusion.refs_0_, ...), custom_call_target="tpu_custom_call" | custom-call | flops 12582912 | bytes 82048 | tf_op jit(solution)/shard_map/place_tokens/pallas_call | solution.py:34
  8.3 3.9 %collective-permute-start.5 = (bf16[192,1024]{1,0:T(8,128)(2,1)S(1)}, bf16[192,1024]{1,0:T(8,128)(2,1)S(1)}, u32[]{:S(2)}, u32[]{:S(2)}) collective-permute-start(bf16[192,1024]{1,0:T(8,128)(2,1)S(1)} %get-tuple-element.69), channel_id=1, source_target_pairs={{0,24},{4,28},{8,16},{12,20},{16,8},{20,12},{24,0},{28,4},{1,25},{... | collective-permute-start | bytes 1179656 | tf_op jit(solution)/shard_map/ppermute | solution.py:425
  13.4 2.2 %place_scaled.1 = (bf16[192,2048]{1,0:T(8,128)(2,1)S(1)}, bf16[192,2048]{1,0:T(8,128)(2,1)S(1)}, bf16[192,2048]{1,0:T(8,128)(2,1)S(1)}, bf16[192,1024]{1,0:T(8,128)(2,1)S(1)}) custom-call(s32[2]{0:T(128)S(1)} %pad_add_fusion.where, f32[4,256]{1,0:T(4,128)S(1)} %pad_maximum_fusion.refs_0_, f32[4,256]{1,0:T(4,128)S(1)} %collective-permute-done.refs_1_, ...), custom_call_target="tpu_custom_call" | custom-call | flops 12582912 | bytes 75904 | tf_op jit(solution)/shard_map/place_scaled/pallas_call | solution.py:34
  15.7 6.4 %collective-permute-done.5.refs_1_ = bf16[192,1024]{1,0:T(8,128)(2,1)S(1)} collective-permute-done((bf16[192,1024]{1,0:T(8,128)(2,1)S(1)}, bf16[192,1024]{1,0:T(8,128)(2,1)S(1)}, u32[]{:S(2)}, u32[]{:S(2)}) %collective-permute-start.5) | collective-permute-done | bytes 393248 | tf_op jit(solution)/shard_map/ppermute | solution.py:425
  22.1 2.1 %collective-permute-start.6 = (bf16[192,1024]{1,0:T(8,128)(2,1)S(1)}, bf16[192,1024]{1,0:T(8,128)(2,1)S(1)}, u32[]{:S(2)}, u32[]{:S(2)}) collective-permute-start(bf16[192,1024]{1,0:T(8,128)(2,1)S(1)} %collective-permute-done.5.refs_1_), channel_id=1, source_target_pairs={{0,1},{1,0},{2,3},{3,2},{4,5},{5,4},{6,7},{7,6},{8,9},{9,8},{10,11... | collective-permute-start | bytes 1179656 | tf_op jit(solution)/shard_map/ppermute | solution.py:425
  24.2 5.8 %collective-permute-done.3.refs_1_ = bf16[192,1024]{1,0:T(8,128)(2,1)S(1)} collective-permute-done((bf16[192,1024]{1,0:T(8,128)(2,1)S(1)}, bf16[192,1024]{1,0:T(8,128)(2,1)S(1)}, u32[]{:S(2)}, u32[]{:S(2)}) %collective-permute-start.3) | collective-permute-done | bytes 393248 | tf_op jit(solution)/shard_map/ppermute | solution.py:425
  35.9 2.2 %copy-done.1 = bf16[1,2048,1024]{2,1,0:T(8,128)(2,1)S(1)} copy-done((bf16[1,2048,1024]{2,1,0:T(8,128)(2,1)S(1)}, bf16[1,2048,1024]{2,1,0:T(8,128)(2,1)}, u32[]{:S(2)}) %copy-start.1) | copy-done | bytes 4194328
  38.1 6.5 %forward_own_and_far.1 = (bf16[768,2048]{1,0:T(8,128)(2,1)S(1)}, bf16[768,1024]{1,0:T(8,128)(2,1)S(1)}, f32[384,1024]{1,0:T(8,128)S(1)}, f32[384,1024]{1,0:T(8,128)S(1)}) custom-call(s32[2]{0:T(128)S(1)} %pad_add_fusion.where, bf16[192,2048]{1,0:T(8,128)(2,1)S(1)} %get-tuple-element.68.refs_0_, bf16[192,1024]{1,0:T(8,128)(2,1)S(1)} %collective-permute-done.5.refs_1_, ...), custom_call_target="tpu_custom_call" | custom-call | flops 50331648 | bytes 278528 | tf_op jit(solution)/shard_map/forward_own_and_far/pallas_call | solution.py:34
  44.6 3.6 %backward_own_and_far.1 = (bf16[768,2048]{1,0:T(8,128)(2,1)S(1)}, bf16[768,1024]{1,0:T(8,128)(2,1)S(1)}, bf16[768,1024]{1,0:T(8,128)(2,1)S(1)}) custom-call(s32[2]{0:T(128)S(1)} %pad_add_fusion.where, bf16[192,2048]{1,0:T(8,128)(2,1)S(1)} %get-tuple-element.66.refs_0_, bf16[192,1024]{1,0:T(8,128)(2,1)S(1)} %collective-permute-done.3.refs_1_, ...), custom_call_target="tpu_custom_call" | custom-call | flops 25165824 | bytes 237568 | tf_op jit(solution)/shard_map/backward_own_and_far/pallas_call | solution.py:34
  48.2 5.0 %own_and_far_input_grads.1 = (bf16[192,2048]{1,0:T(8,128)(2,1)S(1)}, bf16[192,1024]{1,0:T(8,128)(2,1)S(1)}, f32[192,1024]{1,0:T(8,128)S(1)}) custom-call(s32[2]{0:T(128)S(1)} %pad_add_fusion.where, bf16[768,1024]{1,0:T(8,128)(2,1)S(1)} %get-tuple-element.90.refs_0_.refs_1_, bf16[768,1024]{1,0:T(8,128)(2,1)S(1)} %get-tuple-element.91.refs_1_.refs_2_, ...), custom_call_target="tpu_custom_call" | custom-call | flops 50331648 | bytes 210944 | tf_op jit(solution)/shard_map/own_and_far_input_grads/pallas_call | solution.py:34
  54.2 6.3 %forward_near.1 = (bf16[768,2048]{1,0:T(8,128)(2,1)S(1)}, bf16[768,1024]{1,0:T(8,128)(2,1)S(1)}, f32[384,1024]{1,0:T(8,128)S(1)}, f32[384,1024]{1,0:T(8,128)S(1)}) custom-call(s32[2]{0:T(128)S(1)} %pad_add_fusion.where, bf16[768,2048]{1,0:T(8,128)(2,1)S(1)} %get-tuple-element.78.refs_0_, ...), custom_call_target="tpu_custom_call", output_to_operand_aliasing={{0}: (1, {}), {1}: (2, {})} | custom-call | flops 50331648 | bytes 139264 | tf_op jit(solution)/shard_map/forward_near/pallas_call | solution.py:34
  62.2 4.9 %collective-permute-done.10.refs_3_ = bf16[192,2048]{1,0:T(8,128)(2,1)S(1)} collective-permute-done((bf16[192,2048]{1,0:T(8,128)(2,1)S(1)}, bf16[192,2048]{1,0:T(8,128)(2,1)S(1)}, u32[]{:S(2)}, u32[]{:S(2)}) %collective-permute-start.10) | collective-permute-done | bytes 786464 | tf_op jit(solution)/shard_map/ppermute | solution.py:425
  70.0 3.5 %backward_near.1 = (bf16[768,2048]{1,0:T(8,128)(2,1)S(1)}, bf16[768,1024]{1,0:T(8,128)(2,1)S(1)}, bf16[768,1024]{1,0:T(8,128)(2,1)S(1)}) custom-call(s32[2]{0:T(128)S(1)} %pad_add_fusion.where, bf16[768,2048]{1,0:T(8,128)(2,1)S(1)} %get-tuple-element.89.refs_0_, ...), custom_call_target="tpu_custom_call", output_to_operand_aliasing={{0}: (1, {}), {1}: (2, {}), {2}: (3, {})} | custom-call | flops 25165824 | bytes 118784 | tf_op jit(solution)/shard_map/backward_near/pallas_call | solution.py:34
  73.6 2.6 %near_input_grads.3 = (bf16[192,1024]{1,0:T(8,128)(2,1)S(1)}, bf16[192,1024]{1,0:T(8,128)(2,1)S(1)}) custom-call(s32[2]{0:T(128)S(1)} %pad_add_fusion.where, bf16[768,1024]{1,0:T(8,128)(2,1)S(1)} %get-tuple-element.95.refs_0_.refs_1_.refs_3_, bf16[768,1024]{1,0:T(8,128)(2,1)S(1)} %get-tuple-element.96.refs_1_.refs_2_.refs_4_, ...), custom_call_target="tpu_custom_call" | custom-call | flops 25165824 | bytes 192512 | tf_op jit(solution)/shard_map/near_input_grads/pallas_call | solution.py:34
  80.1 2.6 %near_input_grads.2 = (bf16[192,1024]{1,0:T(8,128)(2,1)S(1)}, bf16[192,1024]{1,0:T(8,128)(2,1)S(1)}) custom-call(s32[2]{0:T(128)S(1)} %pad_add_fusion.where, bf16[768,1024]{1,0:T(8,128)(2,1)S(1)} %get-tuple-element.95.refs_0_.refs_1_.refs_3_, bf16[768,1024]{1,0:T(8,128)(2,1)S(1)} %get-tuple-element.96.refs_1_.refs_2_.refs_4_, ...), custom_call_target="tpu_custom_call" | custom-call | flops 25165824 | bytes 192512 | tf_op jit(solution)/shard_map/near_input_grads/pallas_call | solution.py:34
  82.7 5.9 %down_grad.1 = bf16[1,1024,2048]{2,1,0:T(8,128)(2,1)} custom-call(s32[2]{0:T(128)S(1)} %pad_add_fusion.where, bf16[768,1024]{1,0:T(8,128)(2,1)S(1)} %get-tuple-element.100.refs_0_, bf16[768,2048]{1,0:T(8,128)(2,1)S(1)} %get-tuple-element.101.refs_1_), custom_call_target="tpu_custom_call" | custom-call | flops 50331648 | bytes 139264 | tf_op jit(solution)/shard_map/down_grad/pallas_call | solution.py:34
  91.6 3.5 %gate_and_up_grads.4 = (bf16[1,2048,1024]{2,1,0:T(8,128)(2,1)}, bf16[1,2048,1024]{2,1,0:T(8,128)(2,1)}) custom-call(s32[2]{0:T(128)S(1)} %pad_add_fusion.where, bf16[768,2048]{1,0:T(8,128)(2,1)S(1)} %get-tuple-element.119.refs_0_.refs_2_, bf16[768,1024]{1,0:T(8,128)(2,1)S(1)} %get-tuple-element.95.refs_0_.refs_1_.refs_3_, ...), custom_call_target="tpu_custom_call" | custom-call | flops 25165824 | bytes 229376 | tf_op jit(solution)/shard_map/gate_and_up_grads/pallas_call | solution.py:34
  95.3 2.5 %collective-permute-start.19 = (bf16[256,512]{1,0:T(8,128)(2,1)S(1)}, bf16[256,512]{1,0:T(8,128)(2,1)S(1)}, u32[]{:S(2)}, u32[]{:S(2)}) collective-permute-start(bf16[256,512]{1,0:T(8,128)(2,1)S(1)} %get-tuple-element.124), channel_id=1, source_target_pairs={{0,3},{1,2},{2,1},{3,0},{4,7},{5,6},{6,5},{7,4},{8,11},{9,10},{10,... | collective-permute-start | bytes 786440 | tf_op jit(solution)/shard_map/ppermute | solution.py:425
  98.1 3.5 %gate_and_up_grads.5 = (bf16[1,2048,1024]{2,1,0:T(8,128)(2,1)}, bf16[1,2048,1024]{2,1,0:T(8,128)(2,1)}) custom-call(s32[2]{0:T(128)S(1)} %pad_add_fusion.where, bf16[1,2048,1024]{2,1,0:T(8,128)(2,1)} %get-tuple-element.106.refs_0_, bf16[1,2048,1024]{2,1,0:T(8,128)(2,1)} %get-tuple-element.107.refs_1_, ...), custom_call_target="tpu_custom_call", output_to_operand_aliasing={{0}: (1, {}), {1}: (2, {})} | custom-call | flops 25165824 | bytes 114688 | tf_op jit(solution)/shard_map/gate_and_up_grads/pallas_call | solution.py:34
  103.0 1.8 %collective-permute-start.21 = (bf16[256,512]{1,0:T(8,128)(2,1)S(1)}, bf16[256,512]{1,0:T(8,128)(2,1)S(1)}, u32[]{:S(2)}, u32[]{:S(2)}) collective-permute-start(bf16[256,512]{1,0:T(8,128)(2,1)S(1)} %get-tuple-element.116), channel_id=1, source_target_pairs={{0,1},{1,0},{2,3},{3,2},{4,5},{5,4},{6,7},{7,6},{8,9},{9,8},{10,11... | collective-permute-start | bytes 786440 | tf_op jit(solution)/shard_map/ppermute | solution.py:425
  104.8 3.5 %gate_and_up_grads.6 = (bf16[1,2048,1024]{2,1,0:T(8,128)(2,1)}, bf16[1,2048,1024]{2,1,0:T(8,128)(2,1)}) custom-call(s32[2]{0:T(128)S(1)} %pad_add_fusion.where, bf16[1,2048,1024]{2,1,0:T(8,128)(2,1)} %get-tuple-element.111.refs_0_, bf16[1,2048,1024]{2,1,0:T(8,128)(2,1)} %get-tuple-element.118.refs_1_, ...), custom_call_target="tpu_custom_call", output_to_operand_aliasing={{0}: (1, {}), {1}: (2, {})} | custom-call | flops 25165824 | bytes 114688 | tf_op jit(solution)/shard_map/gate_and_up_grads/pallas_call | solution.py:34
  108.4 3.5 %gate_and_up_grads.7 = (bf16[1,2048,1024]{2,1,0:T(8,128)(2,1)}, bf16[1,2048,1024]{2,1,0:T(8,128)(2,1)}) custom-call(s32[2]{0:T(128)S(1)} %pad_add_fusion.where, bf16[1,2048,1024]{2,1,0:T(8,128)(2,1)} %get-tuple-element.120.refs_0_, bf16[1,2048,1024]{2,1,0:T(8,128)(2,1)} %get-tuple-element.121.refs_1_, ...), custom_call_target="tpu_custom_call", output_to_operand_aliasing={{0}: (1, {}), {1}: (2, {})} | custom-call | flops 25165824 | bytes 114688 | tf_op jit(solution)/shard_map/gate_and_up_grads/pallas_call | solution.py:34
  111.9 9.6 %collective-permute-done.18.refs_0_ = bf16[256,512]{1,0:T(8,128)(2,1)S(1)} collective-permute-done((bf16[256,512]{1,0:T(8,128)(2,1)S(1)}, bf16[256,512]{1,0:T(8,128)(2,1)S(1)}, u32[]{:S(2)}, u32[]{:S(2)}) %collective-permute-start.18) | collective-permute-done | bytes 262176 | tf_op jit(solution)/shard_map/ppermute | solution.py:425
  (58 shorter events, 27.2 us)
Async XLA Ops:
  0.6 4.3 %collective-permute-start.1 = (bf16[256,2048]{1,0:T(8,128)(2,1)}, bf16[256,2048]{1,0:T(8,128)(2,1)S(1)}, u32[]{:S(2)}, u32[]{:S(2)}) collective-permute-start(bf16[256,2048]{1,0:T(8,128)(2,1)} %refs_2_.5), channel_id=1, source_target_pairs={{0,4},{4,0},{8,12},{12,8},{16,20},{20,16},{24,28},{28,24},{1,5},{5... | collective-permute-start | bytes 3145736 | tf_op jit(solution)/shard_map/ppermute | solution.py:425
  1.1 11.0 %collective-permute-start.2 = (bf16[256,2048]{1,0:T(8,128)(2,1)}, bf16[256,2048]{1,0:T(8,128)(2,1)S(1)}, u32[]{:S(2)}, u32[]{:S(2)}) collective-permute-start(bf16[256,2048]{1,0:T(8,128)(2,1)} %refs_2_.6), channel_id=1, source_target_pairs={{0,4},{4,0},{8,12},{12,8},{16,20},{20,16},{24,28},{28,24},{1,5},{5... | collective-permute-start | bytes 3145736 | tf_op jit(solution)/shard_map/ppermute | solution.py:425
  2.6 2.3 %collective-permute-start = (f32[4,256]{1,0:T(4,128)S(1)}, f32[4,256]{1,0:T(4,128)S(1)}, u32[]{:S(2)}, u32[]{:S(2)}) collective-permute-start(f32[4,256]{1,0:T(4,128)S(1)} %pad_maximum_fusion.refs_0_), channel_id=1, source_target_pairs={{0,4},{4,0},{8,12},{12,8},{16,20},{20,16},{24,28},{28,24},{1,5},{5... | collective-permute-start | bytes 12296 | tf_op jit(solution)/shard_map/ppermute | solution.py:425
  3.0 32.8 %copy-start = (bf16[1,2048,1024]{2,1,0:T(8,128)(2,1)S(1)}, bf16[1,2048,1024]{2,1,0:T(8,128)(2,1)}, u32[]{:S(2)}) copy-start(bf16[1,2048,1024]{2,1,0:T(8,128)(2,1)} %refs_2_.9) | copy-start | bytes 12582916
  8.3 13.8 %collective-permute-start.5 = (bf16[192,1024]{1,0:T(8,128)(2,1)S(1)}, bf16[192,1024]{1,0:T(8,128)(2,1)S(1)}, u32[]{:S(2)}, u32[]{:S(2)}) collective-permute-start(bf16[192,1024]{1,0:T(8,128)(2,1)S(1)} %get-tuple-element.69), channel_id=1, source_target_pairs={{0,24},{4,28},{8,16},{12,20},{16,8},{20,12},{24,0},{28,4},{1,25},{... | collective-permute-start | bytes 1179656 | tf_op jit(solution)/shard_map/ppermute | solution.py:425
  15.6 14.4 %collective-permute-start.3 = (bf16[192,1024]{1,0:T(8,128)(2,1)S(1)}, bf16[192,1024]{1,0:T(8,128)(2,1)S(1)}, u32[]{:S(2)}, u32[]{:S(2)}) collective-permute-start(bf16[192,1024]{1,0:T(8,128)(2,1)S(1)} %get-tuple-element.67), channel_id=1, source_target_pairs={{0,24},{4,28},{8,16},{12,20},{16,8},{20,12},{24,0},{28,4},{1,25},{... | collective-permute-start | bytes 1179656 | tf_op jit(solution)/shard_map/ppermute | solution.py:425
  22.1 12.7 %collective-permute-start.6 = (bf16[192,1024]{1,0:T(8,128)(2,1)S(1)}, bf16[192,1024]{1,0:T(8,128)(2,1)S(1)}, u32[]{:S(2)}, u32[]{:S(2)}) collective-permute-start(bf16[192,1024]{1,0:T(8,128)(2,1)S(1)} %collective-permute-done.5.refs_1_), channel_id=1, source_target_pairs={{0,1},{1,0},{2,3},{3,2},{4,5},{5,4},{6,7},{7,6},{8,9},{9,8},{10,11... | collective-permute-start | bytes 1179656 | tf_op jit(solution)/shard_map/ppermute | solution.py:425
  30.0 14.6 %collective-permute-start.4 = (bf16[192,1024]{1,0:T(8,128)(2,1)S(1)}, bf16[192,1024]{1,0:T(8,128)(2,1)S(1)}, u32[]{:S(2)}, u32[]{:S(2)}) collective-permute-start(bf16[192,1024]{1,0:T(8,128)(2,1)S(1)} %collective-permute-done.3.refs_1_), channel_id=1, source_target_pairs={{0,1},{1,0},{2,3},{3,2},{4,5},{5,4},{6,7},{7,6},{8,9},{9,8},{10,11... | collective-permute-start | bytes 1179656 | tf_op jit(solution)/shard_map/ppermute | solution.py:425
  31.8 22.3 %collective-permute-start.8 = (bf16[192,2048]{1,0:T(8,128)(2,1)S(1)}, bf16[192,2048]{1,0:T(8,128)(2,1)S(1)}, u32[]{:S(2)}, u32[]{:S(2)}) collective-permute-start(bf16[192,2048]{1,0:T(8,128)(2,1)S(1)} %get-tuple-element.80), channel_id=1, source_target_pairs={{0,8},{4,12},{8,0},{12,4},{16,24},{20,28},{24,16},{28,20},{1,9},{5... | collective-permute-start | bytes 2359304 | tf_op jit(solution)/shard_map/ppermute | solution.py:425
  33.3 20.9 %collective-permute-start.9 = (bf16[192,2048]{1,0:T(8,128)(2,1)S(1)}, bf16[192,2048]{1,0:T(8,128)(2,1)S(1)}, u32[]{:S(2)}, u32[]{:S(2)}) collective-permute-start(bf16[192,2048]{1,0:T(8,128)(2,1)S(1)} %get-tuple-element.81), channel_id=1, source_target_pairs={{0,16},{4,20},{8,24},{12,28},{16,0},{20,4},{24,8},{28,12},{1,17},{... | collective-permute-start | bytes 2359304 | tf_op jit(solution)/shard_map/ppermute | solution.py:425
  34.8 32.3 %collective-permute-start.10 = (bf16[192,2048]{1,0:T(8,128)(2,1)S(1)}, bf16[192,2048]{1,0:T(8,128)(2,1)S(1)}, u32[]{:S(2)}, u32[]{:S(2)}) collective-permute-start(bf16[192,2048]{1,0:T(8,128)(2,1)S(1)} %get-tuple-element.84), channel_id=1, source_target_pairs={{0,8},{4,12},{8,0},{12,4},{16,24},{20,28},{24,16},{28,20},{1,9},{5... | collective-permute-start | bytes 2359304 | tf_op jit(solution)/shard_map/ppermute | solution.py:425
  35.4 33.0 %collective-permute-start.11 = (bf16[192,2048]{1,0:T(8,128)(2,1)S(1)}, bf16[192,2048]{1,0:T(8,128)(2,1)S(1)}, u32[]{:S(2)}, u32[]{:S(2)}) collective-permute-start(bf16[192,2048]{1,0:T(8,128)(2,1)S(1)} %get-tuple-element.86), channel_id=1, source_target_pairs={{0,16},{4,20},{8,24},{12,28},{16,0},{20,4},{24,8},{28,12},{1,17},{... | collective-permute-start | bytes 2359304 | tf_op jit(solution)/shard_map/ppermute | solution.py:425
  53.2 9.0 %collective-permute-start.7 = (bf16[192,1024]{1,0:T(8,128)(2,1)S(1)}, bf16[192,1024]{1,0:T(8,128)(2,1)S(1)}, u32[]{:S(2)}, u32[]{:S(2)}) collective-permute-start(bf16[192,1024]{1,0:T(8,128)(2,1)S(1)} %get-tuple-element.76), channel_id=1, source_target_pairs={{0,1},{1,0},{2,3},{3,2},{4,5},{5,4},{6,7},{7,6},{8,9},{9,8},{10,11... | collective-permute-start | bytes 1179656 | tf_op jit(solution)/shard_map/ppermute | solution.py:425
  68.5 11.6 %collective-permute-start.12 = (bf16[192,1024]{1,0:T(8,128)(2,1)S(1)}, bf16[192,1024]{1,0:T(8,128)(2,1)S(1)}, u32[]{:S(2)}, u32[]{:S(2)}) collective-permute-start(bf16[192,1024]{1,0:T(8,128)(2,1)S(1)} %add_convert_fusion.1), channel_id=1, source_target_pairs={{0,24},{4,28},{8,16},{12,20},{16,8},{20,12},{24,0},{28,4},{1,25},{... | collective-permute-start | bytes 1179656 | tf_op jit(solution)/shard_map/ppermute | solution.py:425
  76.2 12.4 %collective-permute-start.14 = (bf16[192,1024]{1,0:T(8,128)(2,1)S(1)}, bf16[192,1024]{1,0:T(8,128)(2,1)S(1)}, u32[]{:S(2)}, u32[]{:S(2)}) collective-permute-start(bf16[192,1024]{1,0:T(8,128)(2,1)S(1)} %get-tuple-element.99), channel_id=1, source_target_pairs={{0,8},{4,12},{8,0},{12,4},{16,24},{20,28},{24,16},{28,20},{1,9},{5... | collective-permute-start | bytes 1179656 | tf_op jit(solution)/shard_map/ppermute | solution.py:425
  77.8 10.8 %collective-permute-start.15 = (bf16[192,1024]{1,0:T(8,128)(2,1)S(1)}, bf16[192,1024]{1,0:T(8,128)(2,1)S(1)}, u32[]{:S(2)}, u32[]{:S(2)}) collective-permute-start(bf16[192,1024]{1,0:T(8,128)(2,1)S(1)} %get-tuple-element.103), channel_id=1, source_target_pairs={{0,16},{4,20},{8,24},{12,28},{16,0},{20,4},{24,8},{28,12},{1,17},{... | collective-permute-start | bytes 1179656 | tf_op jit(solution)/shard_map/ppermute | solution.py:425
  89.9 5.3 %collective-permute-start.16 = (bf16[256,1024]{1,0:T(8,128)(2,1)S(1)}, bf16[256,1024]{1,0:T(8,128)(2,1)S(1)}, u32[]{:S(2)}, u32[]{:S(2)}) collective-permute-start(bf16[256,1024]{1,0:T(8,128)(2,1)S(1)} %get-tuple-element.108), channel_id=1, source_target_pairs={{0,4},{4,0},{8,12},{12,8},{16,20},{20,16},{24,28},{28,24},{1,5},{5... | collective-permute-start | bytes 1572872 | tf_op jit(solution)/shard_map/ppermute | solution.py:425
  89.9 11.6 %collective-permute-start.13 = (bf16[192,1024]{1,0:T(8,128)(2,1)S(1)}, bf16[192,1024]{1,0:T(8,128)(2,1)S(1)}, u32[]{:S(2)}, u32[]{:S(2)}) collective-permute-start(bf16[192,1024]{1,0:T(8,128)(2,1)S(1)} %get-tuple-element.97), channel_id=1, source_target_pairs={{0,8},{4,12},{8,0},{12,4},{16,24},{20,28},{24,16},{28,20},{1,9},{5... | collective-permute-start | bytes 1179656 | tf_op jit(solution)/shard_map/ppermute | solution.py:425
  90.0 11.6 %collective-permute-start.17 = (bf16[192,1024]{1,0:T(8,128)(2,1)S(1)}, bf16[192,1024]{1,0:T(8,128)(2,1)S(1)}, u32[]{:S(2)}, u32[]{:S(2)}) collective-permute-start(bf16[192,1024]{1,0:T(8,128)(2,1)S(1)} %get-tuple-element.113), channel_id=1, source_target_pairs={{0,16},{4,20},{8,24},{12,28},{16,0},{20,4},{24,8},{28,12},{1,17},{... | collective-permute-start | bytes 1179656 | tf_op jit(solution)/shard_map/ppermute | solution.py:425
  95.3 16.6 %collective-permute-start.19 = (bf16[256,512]{1,0:T(8,128)(2,1)S(1)}, bf16[256,512]{1,0:T(8,128)(2,1)S(1)}, u32[]{:S(2)}, u32[]{:S(2)}) collective-permute-start(bf16[256,512]{1,0:T(8,128)(2,1)S(1)} %get-tuple-element.124), channel_id=1, source_target_pairs={{0,3},{1,2},{2,1},{3,0},{4,7},{5,6},{6,5},{7,4},{8,11},{9,10},{10,... | collective-permute-start | bytes 786440 | tf_op jit(solution)/shard_map/ppermute | solution.py:425
  97.9 23.6 %collective-permute-start.18 = (bf16[256,512]{1,0:T(8,128)(2,1)S(1)}, bf16[256,512]{1,0:T(8,128)(2,1)S(1)}, u32[]{:S(2)}, u32[]{:S(2)}) collective-permute-start(bf16[256,512]{1,0:T(8,128)(2,1)S(1)} %get-tuple-element.125), channel_id=1, source_target_pairs={{0,2},{1,3},{2,0},{3,1},{4,6},{5,7},{6,4},{7,5},{8,10},{9,11},{10,... | collective-permute-start | bytes 786440 | tf_op jit(solution)/shard_map/ppermute | solution.py:425
  102.9 18.7 %collective-permute-start.20 = (bf16[256,512]{1,0:T(8,128)(2,1)S(1)}, bf16[256,512]{1,0:T(8,128)(2,1)S(1)}, u32[]{:S(2)}, u32[]{:S(2)}) collective-permute-start(bf16[256,512]{1,0:T(8,128)(2,1)S(1)} %get-tuple-element.115), channel_id=1, source_target_pairs={{0,4},{4,0},{8,12},{12,8},{16,20},{20,16},{24,28},{28,24},{1,5},{5... | collective-permute-start | bytes 786440 | tf_op jit(solution)/shard_map/ppermute | solution.py:425
  103.0 18.6 %collective-permute-start.21 = (bf16[256,512]{1,0:T(8,128)(2,1)S(1)}, bf16[256,512]{1,0:T(8,128)(2,1)S(1)}, u32[]{:S(2)}, u32[]{:S(2)}) collective-permute-start(bf16[256,512]{1,0:T(8,128)(2,1)S(1)} %get-tuple-element.116), channel_id=1, source_target_pairs={{0,1},{1,0},{2,3},{3,2},{4,5},{5,4},{6,7},{7,6},{8,9},{9,8},{10,11... | collective-permute-start | bytes 786440 | tf_op jit(solution)/shard_map/ppermute | solution.py:425
  104.7 18.0 %collective-permute-start.22 = (bf16[256,512]{1,0:T(8,128)(2,1)S(1)}, bf16[256,512]{1,0:T(8,128)(2,1)S(1)}, u32[]{:S(2)}, u32[]{:S(2)}) collective-permute-start(bf16[256,512]{1,0:T(8,128)(2,1)S(1)} %get-tuple-element.117), channel_id=1, source_target_pairs={{0,5},{1,4},{2,7},{3,6},{4,1},{5,0},{6,3},{7,2},{8,13},{9,12},{10,... | collective-permute-start | bytes 786440 | tf_op jit(solution)/shard_map/ppermute | solution.py:431
  (5 other events, 14.8 us)

commit v3 on v2

--- a/solution.py
+++ b/solution.py
@@ -10,7 +10,11 @@
 F32 = jnp.float32
 BF16 = jnp.bfloat16
 VMEM_LIMIT = 20 * 1024 * 1024
-AWAY_FLOPS = 2 * 10**9
+COST = {"forward_near": 60000, "backward_near": 1000, "own_and_far_input_grads": 100, "near_grads_away": 20000, "near_grads_here": 100, "gate_and_up_0": 1000, "gate_and_up_1": 5000, "gate_and_up_2": 20000, "gate_and_up_3": 20000, "combine_away": 20000, "combine_here": 20000, "place_tokens": 100}
+COST = {name: 10**6 * cost for name, cost in COST.items()}
+LATE_QUARTER = True
+FAR_FIRST = 'here'
+SIDE_LAST = 'core'
 
 
 def contract(left, right, left_dim, right_dim):
@@ -23,8 +27,11 @@
     return jax.ShapeDtypeStruct(shape, dtype)
 
 
-def call(kernel, name, where, args, in_specs, out_shape, out_specs, grid, flops, kept=()):
-    moved = sum(a.size * a.dtype.itemsize for a in (*args, *out_shape)) // (2 if kept else 1)
+def estimate(name):
+    return pl.CostEstimate(flops=COST.get(name, 0), bytes_accessed=0, transcendentals=0)
+
+
+def call(kernel, name, where, args, in_specs, out_shape, out_specs, grid, kept=()):
     args = (*kept, *args)
     in_specs = [pl.BlockSpec(memory_space=pl.ANY)] * len(kept) + in_specs
 
@@ -40,7 +47,7 @@
         out_shape=out_shape,
         name=name,
         compiler_params=pltpu.CompilerParams(vmem_limit_bytes=VMEM_LIMIT),
-        cost_estimate=pl.CostEstimate(flops=flops // 64, bytes_accessed=moved // 64, transcendentals=0),
+        cost_estimate=estimate(name),
     )(where, *args)
 
 
@@ -62,9 +69,9 @@
     return lax.optimization_barrier((array, *earlier))[0]
 
 
-def place_kernel(plan, cap, with_gate, where, *refs):
+def place_kernel(plan, cap, with_gate, chips, placings, where, *refs):
     metas, tables, outs = refs[:2], refs[2:4], refs[4:]
-    chips, experts = len(plan.chips), plan.experts
+    experts = plan.experts
     toks, width = tables[0].shape
     half = pl.ds(pl.multiple_of((where[1] & 1) * (width // 2), 128), width // 2)
     earlier = (
@@ -82,34 +89,34 @@
         for place, chip in enumerate(plan.chips):
             d = 2 * chip
             placing = slot == rank[d : d + 1, :]
+            if placings:
+                outs[len(chips) + side][place * cap : (place + 1) * cap, :] = placing.astype(BF16)
+            if chip not in chips:
+                continue
             rows = tables[side][:, half] if chip in plan.far else tables[side][...]
             block = jnp.dot(placing.astype(BF16), rows, preferred_element_type=F32)
             if with_gate:
                 gate = jnp.where(ids0 == d, metas[side][2:3, :], metas[side][3:4, :])
                 slot_gate = jnp.sum(jnp.where(placing, gate, 0.0), axis=1, keepdims=True)
                 block = block * slot_gate
-            else:
-                outs[chips + side][place * cap : (place + 1) * cap, :] = placing.astype(BF16)
-            outs[chip][side * cap : (side + 1) * cap, :] = block.astype(BF16)
-
-
-def place(plan, where, metas, tables, cap, with_gate):
+            outs[chips.index(chip)][side * cap : (side + 1) * cap, :] = block.astype(BF16)
+
+
+def place(name, plan, where, metas, tables, cap, with_gate, chips, placings=False):
     toks, width = tables[0].shape
-    chips = len(plan.chips)
-    outs = [like(2 * cap, width // 2 if c in plan.far else width) for c in range(chips)]
-    if not with_gate:
-        outs = outs + [like(chips * cap, toks)] * 2
+    outs = [like(2 * cap, width // 2 if c in plan.far else width) for c in chips]
+    if placings:
+        outs = outs + [like(len(plan.chips) * cap, toks)] * 2
     args = (*metas, *tables)
     return call(
-        functools.partial(place_kernel, plan, cap, with_gate),
-        "place_scaled" if with_gate else "place_tokens",
+        functools.partial(place_kernel, plan, cap, with_gate, chips, placings),
+        name,
         where,
         args,
         [whole(a) for a in args],
         outs,
         [whole(o) for o in outs],
         (1,),
-        2 * plan.experts * cap * toks * width,
     )
 
 
@@ -185,7 +192,6 @@
             out_column,
         ],
         (units // tile,),
-        4 * count * width * units,
         kept,
     )
 
@@ -223,7 +229,6 @@
         outs,
         [pl.BlockSpec((count, width), lambda j, _: (chunk, 0)), out_column, out_column],
         (units // tile,),
-        2 * count * width * units,
         kept,
     )
 
@@ -280,7 +285,6 @@
             pl.BlockSpec((far, slab), lambda i, where: (0, jnp.maximum(i - dp // 2, 0))),
         ],
         (dp,),
-        2 * grad_a.shape[0] * width * units,
     )
 
 
@@ -304,14 +308,13 @@
     outs = [like(2 * cap, width // 2)] * len(plan.near)
     return call(
         functools.partial(near_grad_kernel, cap),
-        "near_input_grads",
+        "near_grads_away" if away else "near_grads_here",
         where,
         (grad_a, grad_b, w_gate, w_up),
         [chunk, chunk, weight, weight],
         outs,
         [pl.BlockSpec((2 * cap, tile), lambda i, where: (0, i))] * len(plan.near),
         (steps,),
-        grad_a.shape[0] * width * units,
     )
 
 
@@ -336,7 +339,6 @@
         outs,
         [pl.BlockSpec((1, tile, o.shape[2]), lambda i, _: (0, first + i, 0)) for o in outs],
         (steps,),
-        2 * rows * width * sum(o.shape[2] for o in outs) // parts,
         kept,
     )
 
@@ -397,7 +399,7 @@
         name="combine_away" if side_by_side else "combine_here",
         compiler_params=pltpu.CompilerParams(vmem_limit_bytes=VMEM_LIMIT),
         cost_estimate=pl.CostEstimate(
-            flops=flops // 64, bytes_accessed=moved // 64, transcendentals=0
+            flops=0, bytes_accessed=0, transcendentals=0
         ),
     )(where, *args)
 
@@ -414,9 +416,7 @@
         out_shape=out,
         name="add_up",
         compiler_params=pltpu.CompilerParams(vmem_limit_bytes=VMEM_LIMIT),
-        cost_estimate=pl.CostEstimate(
-            flops=AWAY_FLOPS, bytes_accessed=2 * out.size, transcendentals=0
-        ),
+        cost_estimate=estimate("add_up"),
     )(*parts)
 
 
@@ -442,8 +442,20 @@
     tokens_other = swap(tokens, "expert", 1)
     out_other = swap(grad_out, "expert", 1)
     metas = (meta, meta_other)
-    *x, placing, placing_other = place(plan, where, metas, (tokens, tokens_other), cap, False)
-    r = list(place(plan, where, metas, (grad_out, out_other), cap, True))
+    tables = (pltpu.with_memory_space_constraint(tokens, pltpu.HBM), tokens_other)
+    x = [None] * len(plan.chips)
+    blocks = place("place_far_tokens", plan, where, metas, tables, cap, False, plan.far)
+    for c, block in zip(plan.far, blocks, strict=True):
+        x[c] = block
+    rest = [0] + plan.near
+    metas = (after(meta, x[plan.far[-1]]), meta_other)
+    *blocks, placing, placing_other = place(
+        "place_tokens", plan, where, metas, tables, cap, False, rest, True
+    )
+    for c, block in zip(rest, blocks, strict=True):
+        x[c] = block
+    tables = (pltpu.with_memory_space_constraint(grad_out, pltpu.HBM), out_other)
+    r = list(place("place_scaled", plan, where, metas, tables, cap, True, list(range(len(x)))))
     placings = (placing, placing_other)
 
     def over(blocks, which):
@@ -484,7 +496,8 @@
         "backward_near", where, 1, pick(r, plan.near), [], [], w_down, to_a, to_b, kept
     )
     away_part = near_grad(plan, where, grad_a, grad_b, w_gate, w_up, dp, cap, True)
-    here_part = near_grad(plan, where, after(grad_a, *far), grad_b, w_gate, w_up, dp, cap, False)
+    grad_a = after(grad_a, away_part[0], *(far if FAR_FIRST == "here" else []))
+    here_part = near_grad(plan, where, grad_a, grad_b, w_gate, w_up, dp, cap, False)
 
     def send_back(part):
         return [swap(b, "expert", 2 * c) for b, c in zip(part, plan.near, strict=True)]
@@ -493,26 +506,38 @@
     slab = width // dp
     away, here = list(range(dp // 2, dp)), list(range(dp // 2))
 
-    (grad_down,) = outer("down_grad", where, after(hidden, here_part[0]), [r_all])
+    hidden = after(hidden, here_part[0], *(far if FAR_FIRST == "down" else []))
+    (grad_down,) = outer("down_grad", where, hidden, [r_all])
     away_rows[0] = after(away_rows[0], grad_down)
     away_sum, other = combine(
         plan, where, placings, [own, *far, *away_rows], dp, cap, away, True
     )
     other = swap(other, "expert", 1)
-    grads = outer("gate_and_up_grads", where, after(x_all, away_sum), [grad_a, grad_b], 0, 4)
-    away_sum = (away_sum + after(other, grads[0]).astype(F32)).astype(BF16)
+    away_sum = (away_sum + other.astype(F32)).astype(BF16)
     parts = [away_sum[:, n * slab : (n + 1) * slab] for n in range(len(away))]
-    grads = outer("gate_and_up_grads", where, after(x_all, *parts), [grad_a, grad_b], 1, 4, grads)
     away_sums = [swap(part, "dp", s) for part, s in zip(parts, away, strict=True)]
+    rights = [grad_a, grad_b]
+    x_all = after(x_all, *parts)
+    early = 1 if LATE_QUARTER else 2
+    grads = ()
+    for part in range(early):
+        grads = outer(f"gate_and_up_{part}", where, x_all, rights, part, 4, grads)
     here_rows[0] = after(here_rows[0], grads[0])
     total, other, *rest = combine(
         plan, where, placings, [own, *far, *here_rows], dp, cap, here, False
     )
     got = [swap(other, "expert", 1)]
-    for n, s in enumerate(here[1:]):
-        got += [swap(rest[2 * n], "dp", s), cross(rest[2 * n + 1], s)]
-    grads = outer("gate_and_up_grads", where, after(x_all, total), [grad_a, grad_b], 2, 4, grads)
-    grad_gate, grad_up = outer("gate_and_up_grads", where, x_all, [grad_a, grad_b], 3, 4, grads)
+    x_all = after(x_all, total)
+    for part in range(early, 4):
+        grads = outer(f"gate_and_up_{part}", where, x_all, rights, part, 4, grads)
+        for n, s in enumerate(here[1:] if part == early else []):
+            if SIDE_LAST == "cross":
+                got += [swap(rest[2 * n], "dp", s), cross(rest[2 * n + 1], s)]
+            else:
+                other = after(swap(rest[2 * n + 1], "expert", 1), grads[0])
+                both = rest[2 * n].astype(F32) + other.astype(F32)
+                got += [swap(both.astype(BF16), "dp", s)]
+    grad_gate, grad_up = grads
     total = total + add_up(away_sums)
     for part in got:
         total = total + part.astype(F32)

time: 124 us -> 119 us (0.960)
  waiting for transfers between devices: 34.6 us -> 22 us
  starting transfers between devices: 23.8 us -> 29.6 us
  Pallas kernels: 57.1 us -> 61.7 us
  local copies, waits for them, and re-layouts: 4.69 us -> 2.24 us
    ppermute x22 -> x23, waiting for transfers between devices: 33.4 us -> 22 us  [swap(): return lax.ppermute(rows, axis, [(i, i ^ mask) for i in range(count)])]
    ppermute x22 -> x23, starting transfers between devices: 23.7 us -> 29.6 us  [swap(): return lax.ppermute(rows, axis, [(i, i ^ mask) for i in range(count)])]
    pallas_call x14 -> x15, Pallas kernels: 54.5 us -> 59.1 us  [call(): pl.pallas_call(inner, input_output_aliases={i + 1: i for i in range(len(k...]
    unnamed x12 -> x8, local copies, waits for them, and re-layouts: 4.65 us -> 2.2 us
  transfers between devices with their start and end apart: 23 -> 23, of which waited for: 9 -> 10; matrix products, arithmetic and copies ran while one was open for 1% -> 1% of each run, Pallas kernels for 45% -> 51%
where the time goes in v3:
time: 119 us
  Pallas kernels  61.7 us (52%)
  starting transfers between devices  29.6 us (25%)
  waiting for transfers between devices  22 us (18%)
  other arithmetic  2.62 us (2%)
  local copies, waits for them, and re-layouts  2.24 us (2%)
    pallas_call x15, Pallas kernels, call(): pl.pallas_call(inner, input_output_aliases={i + 1: i for i in range(len(k...  59.1 us
    ppermute x23, starting transfers between devices, swap(): return lax.ppermute(rows, axis, [(i, i ^ mask) for i in range(count)])  29.6 us
    ppermute x23, waiting for transfers between devices, swap(): return lax.ppermute(rows, axis, [(i, i ^ mask) for i in range(count)])  22 us
    pallas_call x2, Pallas kernels, combine(): pl.pallas_call(functools.partial(combine_kernel, plan, cap, dp, shifts, s...  2.53 us
  transfers between devices with their start and end apart: 23, of which 10 were waited for; matrix products, arithmetic and copies ran while one was open for 1% of the time, Pallas kernels for 51%

profile of v3, /device:TPU:0, one launch (start us, length us, event | category | flops | bytes accessed | tf_op | source)
XLA Modules:
  0.0 119.0 jit_solution(888976677529474960)
XLA Ops:
  4.9 2.3 %place_far_tokens.1 = bf16[192,1024]{1,0:T(8,128)(2,1)S(1)} custom-call(s32[2]{0:T(128)S(1)} %pad_add_fusion.where, f32[4,256]{1,0:T(4,128)S(1)} %pad_maximum_fusion.refs_0_, f32[4,256]{1,0:T(4,128)S(1)} %collective-permute-done.refs_1_, bf16[256,2048]{1,0:T(8,128)(2,1)} %refs_2_.7, bf16[256,2048]{1,0:T(8,128)(2,1)S(1)} %collective-permute-done.1.refs_3_), custom_call_target="tpu_custom_call" | custom-call | tf_op jit(solution)/shard_map/place_far_tokens/pallas_call | solution.py:41
  7.3 3.9 %collective-permute-start.5 = (bf16[192,1024]{1,0:T(8,128)(2,1)S(1)}, bf16[192,1024]{1,0:T(8,128)(2,1)S(1)}, u32[]{:S(2)}, u32[]{:S(2)}) collective-permute-start(bf16[192,1024]{1,0:T(8,128)(2,1)S(1)} %place_far_tokens.1), channel_id=1, source_target_pairs={{0,24},{4,28},{8,16},{12,20},{16,8},{20,12},{24,0},{28,4},{1,25},{... | collective-permute-start | bytes 1179656 | tf_op jit(solution)/shard_map/ppermute | solution.py:425
  11.1 3.4 %place_scaled.1 = (bf16[192,2048]{1,0:T(8,128)(2,1)S(1)}, bf16[192,2048]{1,0:T(8,128)(2,1)S(1)}, bf16[192,2048]{1,0:T(8,128)(2,1)S(1)}, bf16[192,1024]{1,0:T(8,128)(2,1)S(1)}) custom-call(s32[2]{0:T(128)S(1)} %pad_add_fusion.where, f32[4,256]{1,0:T(4,128)S(1)} %pad_maximum_fusion.refs_0_, f32[4,256]{1,0:T(4,128)S(1)} %collective-permute-done.refs_1_, ...), custom_call_target="tpu_custom_call" | custom-call | tf_op jit(solution)/shard_map/place_scaled/pallas_call | solution.py:41
  14.6 3.2 %place_tokens.1 = (bf16[192,2048]{1,0:T(8,128)(2,1)S(1)}, bf16[192,2048]{1,0:T(8,128)(2,1)S(1)}, bf16[192,2048]{1,0:T(8,128)(2,1)S(1)}, bf16[384,256]{1,0:T(8,128)(2,1)S(1)}, bf16[384,256]{1,0:T(8,128)(2,1)S(1)}) custom-call(s32[2]{0:T(128)S(1)} %pad_add_fusion.where, f32[4,256]{1,0:T(4,128)S(1)} %pad_maximum_fusion.refs_0_, ...), custom_call_target="tpu_custom_call" | custom-call | flops 100000000 | tf_op jit(solution)/shard_map/place_tokens/pallas_call | solution.py:41
  23.1 6.4 %collective-permute-done.3.refs_1_ = bf16[192,1024]{1,0:T(8,128)(2,1)S(1)} collective-permute-done((bf16[192,1024]{1,0:T(8,128)(2,1)S(1)}, bf16[192,1024]{1,0:T(8,128)(2,1)S(1)}, u32[]{:S(2)}, u32[]{:S(2)}) %collective-permute-start.3) | collective-permute-done | bytes 393248 | tf_op jit(solution)/shard_map/ppermute | solution.py:425
  34.6 2.2 %copy-done.1 = bf16[1,2048,1024]{2,1,0:T(8,128)(2,1)S(1)} copy-done((bf16[1,2048,1024]{2,1,0:T(8,128)(2,1)S(1)}, bf16[1,2048,1024]{2,1,0:T(8,128)(2,1)}, u32[]{:S(2)}) %copy-start.1) | copy-done | bytes 4194328
  36.8 6.5 %forward_own_and_far.1 = (bf16[768,2048]{1,0:T(8,128)(2,1)S(1)}, bf16[768,1024]{1,0:T(8,128)(2,1)S(1)}, f32[384,1024]{1,0:T(8,128)S(1)}, f32[384,1024]{1,0:T(8,128)S(1)}) custom-call(s32[2]{0:T(128)S(1)} %pad_add_fusion.where, bf16[192,2048]{1,0:T(8,128)(2,1)S(1)} %get-tuple-element.68.refs_0_, bf16[192,1024]{1,0:T(8,128)(2,1)S(1)} %collective-permute-done.5.refs_1_, ...), custom_call_target="tpu_custom_call" | custom-call | tf_op jit(solution)/shard_map/forward_own_and_far/pallas_call | solution.py:41
  43.4 3.6 %backward_own_and_far.1 = (bf16[768,2048]{1,0:T(8,128)(2,1)S(1)}, bf16[768,1024]{1,0:T(8,128)(2,1)S(1)}, bf16[768,1024]{1,0:T(8,128)(2,1)S(1)}) custom-call(s32[2]{0:T(128)S(1)} %pad_add_fusion.where, bf16[192,2048]{1,0:T(8,128)(2,1)S(1)} %get-tuple-element.66.refs_0_, bf16[192,1024]{1,0:T(8,128)(2,1)S(1)} %collective-permute-done.3.refs_1_, ...), custom_call_target="tpu_custom_call" | custom-call | tf_op jit(solution)/shard_map/backward_own_and_far/pallas_call | solution.py:41
  47.0 5.0 %own_and_far_input_grads.1 = (bf16[192,2048]{1,0:T(8,128)(2,1)S(1)}, bf16[192,1024]{1,0:T(8,128)(2,1)S(1)}, f32[192,1024]{1,0:T(8,128)S(1)}) custom-call(s32[2]{0:T(128)S(1)} %pad_add_fusion.where, bf16[768,1024]{1,0:T(8,128)(2,1)S(1)} %get-tuple-element.89.refs_0_.refs_1_, bf16[768,1024]{1,0:T(8,128)(2,1)S(1)} %get-tuple-element.90.refs_1_.refs_2_, ...), custom_call_target="tpu_custom_call" | custom-call | flops 100000000 | tf_op jit(solution)/shard_map/own_and_far_input_grads/pallas_call | solution.py:41
  53.1 6.3 %forward_near.1 = (bf16[768,2048]{1,0:T(8,128)(2,1)S(1)}, bf16[768,1024]{1,0:T(8,128)(2,1)S(1)}, f32[384,1024]{1,0:T(8,128)S(1)}, f32[384,1024]{1,0:T(8,128)S(1)}) custom-call(s32[2]{0:T(128)S(1)} %pad_add_fusion.where, bf16[768,2048]{1,0:T(8,128)(2,1)S(1)} %get-tuple-element.77.refs_0_, ...), custom_call_target="tpu_custom_call", output_to_operand_aliasing={{0}: (1, {}), {1}: (2, {})} | custom-call | flops 60000002048 | tf_op jit(solution)/shard_map/forward_near/pallas_call | solution.py:41
  63.1 2.4 %collective-permute-start.12 = (bf16[192,1024]{1,0:T(8,128)(2,1)S(1)}, bf16[192,1024]{1,0:T(8,128)(2,1)S(1)}, u32[]{:S(2)}, u32[]{:S(2)}) collective-permute-start(bf16[192,1024]{1,0:T(8,128)(2,1)S(1)} %add_convert_fusion.1), channel_id=1, source_target_pairs={{0,24},{4,28},{8,16},{12,20},{16,8},{20,12},{24,0},{28,4},{1,25},{... | collective-permute-start | bytes 1179656 | tf_op jit(solution)/shard_map/ppermute | solution.py:425
  65.5 3.6 %backward_near.1 = (bf16[768,2048]{1,0:T(8,128)(2,1)S(1)}, bf16[768,1024]{1,0:T(8,128)(2,1)S(1)}, bf16[768,1024]{1,0:T(8,128)(2,1)S(1)}) custom-call(s32[2]{0:T(128)S(1)} %pad_add_fusion.where, bf16[768,2048]{1,0:T(8,128)(2,1)S(1)} %get-tuple-element.88.refs_0_, ...), custom_call_target="tpu_custom_call", output_to_operand_aliasing={{0}: (1, {}), {1}: (2, {}), {2}: (3, {})} | custom-call | flops 1000000000 | tf_op jit(solution)/shard_map/backward_near/pallas_call | solution.py:41
  69.0 2.6 %near_grads_away.1 = (bf16[192,1024]{1,0:T(8,128)(2,1)S(1)}, bf16[192,1024]{1,0:T(8,128)(2,1)S(1)}) custom-call(s32[2]{0:T(128)S(1)} %pad_add_fusion.where, bf16[768,1024]{1,0:T(8,128)(2,1)S(1)} %get-tuple-element.96.refs_0_.refs_1_.refs_3_, bf16[768,1024]{1,0:T(8,128)(2,1)S(1)} %get-tuple-element.94.refs_1_.refs_2_.refs_4_, ...), custom_call_target="tpu_custom_call" | custom-call | flops 20000000000 | tf_op jit(solution)/shard_map/near_grads_away/pallas_call | solution.py:41
  72.9 2.6 %collective-permute-done.12.refs_3_ = bf16[192,1024]{1,0:T(8,128)(2,1)S(1)} collective-permute-done((bf16[192,1024]{1,0:T(8,128)(2,1)S(1)}, bf16[192,1024]{1,0:T(8,128)(2,1)S(1)}, u32[]{:S(2)}, u32[]{:S(2)}) %collective-permute-start.12) | collective-permute-done | bytes 393248 | tf_op jit(solution)/shard_map/ppermute | solution.py:425
  75.5 2.6 %near_grads_here.1 = (bf16[192,1024]{1,0:T(8,128)(2,1)S(1)}, bf16[192,1024]{1,0:T(8,128)(2,1)S(1)}) custom-call(s32[2]{0:T(128)S(1)} %pad_add_fusion.where, bf16[768,1024]{1,0:T(8,128)(2,1)S(1)} %get-tuple-element.96.refs_0_.refs_1_.refs_3_, bf16[768,1024]{1,0:T(8,128)(2,1)S(1)} %get-tuple-element.94.refs_1_.refs_2_.refs_4_, ...), custom_call_target="tpu_custom_call" | custom-call | flops 100000000 | tf_op jit(solution)/shard_map/near_grads_here/pallas_call | solution.py:41
  78.1 5.9 %down_grad.1 = bf16[1,1024,2048]{2,1,0:T(8,128)(2,1)} custom-call(s32[2]{0:T(128)S(1)} %pad_add_fusion.where, bf16[768,1024]{1,0:T(8,128)(2,1)S(1)} %get-tuple-element.99.refs_0_, bf16[768,2048]{1,0:T(8,128)(2,1)S(1)} %get-tuple-element.100.refs_1_), custom_call_target="tpu_custom_call" | custom-call | tf_op jit(solution)/shard_map/down_grad/pallas_call | solution.py:41
  85.3 2.1 %collective-permute-start.13 = (bf16[192,1024]{1,0:T(8,128)(2,1)S(1)}, bf16[192,1024]{1,0:T(8,128)(2,1)S(1)}, u32[]{:S(2)}, u32[]{:S(2)}) collective-permute-start(bf16[192,1024]{1,0:T(8,128)(2,1)S(1)} %get-tuple-element.97), channel_id=1, source_target_pairs={{0,8},{4,12},{8,0},{12,4},{16,24},{20,28},{24,16},{28,20},{1,9},{5... | collective-permute-start | bytes 1179656 | tf_op jit(solution)/shard_map/ppermute | solution.py:425
  89.1 3.7 %collective-permute-start.19 = (bf16[256,512]{1,0:T(8,128)(2,1)S(1)}, bf16[256,512]{1,0:T(8,128)(2,1)S(1)}, u32[]{:S(2)}, u32[]{:S(2)}) collective-permute-start(bf16[256,512]{1,0:T(8,128)(2,1)S(1)} %get-tuple-element.122), channel_id=1, source_target_pairs={{0,3},{1,2},{2,1},{3,0},{4,7},{5,6},{6,5},{7,4},{8,11},{9,10},{10,... | collective-permute-start | bytes 786440 | tf_op jit(solution)/shard_map/ppermute | solution.py:425
  92.7 3.5 %gate_and_up_0.1 = (bf16[1,2048,1024]{2,1,0:T(8,128)(2,1)}, bf16[1,2048,1024]{2,1,0:T(8,128)(2,1)}) custom-call(s32[2]{0:T(128)S(1)} %pad_add_fusion.where, bf16[768,2048]{1,0:T(8,128)(2,1)S(1)} %get-tuple-element.114.refs_0_.refs_2_, bf16[768,1024]{1,0:T(8,128)(2,1)S(1)} %get-tuple-element.96.refs_0_.refs_1_.refs_3_, ...), custom_call_target="tpu_custom_call" | custom-call | flops 1000000000 | tf_op jit(solution)/shard_map/gate_and_up_0/pallas_call | solution.py:41
  100.5 3.5 %gate_and_up_1.1 = (bf16[1,2048,1024]{2,1,0:T(8,128)(2,1)}, bf16[1,2048,1024]{2,1,0:T(8,128)(2,1)}) custom-call(s32[2]{0:T(128)S(1)} %pad_add_fusion.where, bf16[1,2048,1024]{2,1,0:T(8,128)(2,1)} %get-tuple-element.106.refs_0_, bf16[1,2048,1024]{2,1,0:T(8,128)(2,1)} %get-tuple-element.113.refs_1_, ...), custom_call_target="tpu_custom_call", output_to_operand_aliasing={{0}: (1, {}), {1}: (2, {})} | custom-call | flops 5000000000 | tf_op jit(solution)/shard_map/gate_and_up_1/pallas_call | solution.py:41
  105.8 3.5 %gate_and_up_2.1 = (bf16[1,2048,1024]{2,1,0:T(8,128)(2,1)}, bf16[1,2048,1024]{2,1,0:T(8,128)(2,1)}) custom-call(s32[2]{0:T(128)S(1)} %pad_add_fusion.where, bf16[1,2048,1024]{2,1,0:T(8,128)(2,1)} %get-tuple-element.115.refs_0_, bf16[1,2048,1024]{2,1,0:T(8,128)(2,1)} %get-tuple-element.117.refs_1_, ...), custom_call_target="tpu_custom_call", output_to_operand_aliasing={{0}: (1, {}), {1}: (2, {})} | custom-call | flops 20000000000 | tf_op jit(solution)/shard_map/gate_and_up_2/pallas_call | solution.py:41
  109.3 3.5 %gate_and_up_3.1 = (bf16[1,2048,1024]{2,1,0:T(8,128)(2,1)}, bf16[1,2048,1024]{2,1,0:T(8,128)(2,1)}) custom-call(s32[2]{0:T(128)S(1)} %pad_add_fusion.where, bf16[1,2048,1024]{2,1,0:T(8,128)(2,1)} %get-tuple-element.118.refs_0_, bf16[1,2048,1024]{2,1,0:T(8,128)(2,1)} %get-tuple-element.119.refs_1_, ...), custom_call_target="tpu_custom_call", output_to_operand_aliasing={{0}: (1, {}), {1}: (2, {})} | custom-call | flops 20000000000 | tf_op jit(solution)/shard_map/gate_and_up_3/pallas_call | solution.py:41
  112.8 2.4 %collective-permute-done.18.refs_0_ = bf16[256,512]{1,0:T(8,128)(2,1)S(1)} collective-permute-done((bf16[256,512]{1,0:T(8,128)(2,1)S(1)}, bf16[256,512]{1,0:T(8,128)(2,1)S(1)}, u32[]{:S(2)}, u32[]{:S(2)}) %collective-permute-start.18) | collective-permute-done | bytes 262176 | tf_op jit(solution)/shard_map/ppermute | solution.py:425
  115.3 2.8 %collective-permute-done.22 = bf16[256,512]{1,0:T(8,128)(2,1)S(1)} collective-permute-done((bf16[256,512]{1,0:T(8,128)(2,1)S(1)}, bf16[256,512]{1,0:T(8,128)(2,1)S(1)}, u32[]{:S(2)}, u32[]{:S(2)}) %collective-permute-start.22) | collective-permute-done | bytes 262176 | tf_op jit(solution)/shard_map/ppermute | solution.py:425
  (56 shorter events, 30.6 us)
Async XLA Ops:
  0.6 4.3 %collective-permute-start.1 = (bf16[256,2048]{1,0:T(8,128)(2,1)}, bf16[256,2048]{1,0:T(8,128)(2,1)S(1)}, u32[]{:S(2)}, u32[]{:S(2)}) collective-permute-start(bf16[256,2048]{1,0:T(8,128)(2,1)} %refs_2_.7), channel_id=1, source_target_pairs={{0,4},{4,0},{8,12},{12,8},{16,20},{20,16},{24,28},{28,24},{1,5},{5... | collective-permute-start | bytes 3145736 | tf_op jit(solution)/shard_map/ppermute | solution.py:425
  1.1 10.0 %collective-permute-start.2 = (bf16[256,2048]{1,0:T(8,128)(2,1)}, bf16[256,2048]{1,0:T(8,128)(2,1)S(1)}, u32[]{:S(2)}, u32[]{:S(2)}) collective-permute-start(bf16[256,2048]{1,0:T(8,128)(2,1)} %refs_2_.8), channel_id=1, source_target_pairs={{0,4},{4,0},{8,12},{12,8},{16,20},{20,16},{24,28},{28,24},{1,5},{5... | collective-permute-start | bytes 3145736 | tf_op jit(solution)/shard_map/ppermute | solution.py:425
  2.6 2.3 %collective-permute-start = (f32[4,256]{1,0:T(4,128)S(1)}, f32[4,256]{1,0:T(4,128)S(1)}, u32[]{:S(2)}, u32[]{:S(2)}) collective-permute-start(f32[4,256]{1,0:T(4,128)S(1)} %pad_maximum_fusion.refs_0_), channel_id=1, source_target_pairs={{0,4},{4,0},{8,12},{12,8},{16,20},{20,16},{24,28},{28,24},{1,5},{5... | collective-permute-start | bytes 12296 | tf_op jit(solution)/shard_map/ppermute | solution.py:425
  3.1 31.5 %copy-start = (bf16[1,2048,1024]{2,1,0:T(8,128)(2,1)S(1)}, bf16[1,2048,1024]{2,1,0:T(8,128)(2,1)}, u32[]{:S(2)}) copy-start(bf16[1,2048,1024]{2,1,0:T(8,128)(2,1)} %refs_2_.11) | copy-start | bytes 12582916
  7.3 14.1 %collective-permute-start.5 = (bf16[192,1024]{1,0:T(8,128)(2,1)S(1)}, bf16[192,1024]{1,0:T(8,128)(2,1)S(1)}, u32[]{:S(2)}, u32[]{:S(2)}) collective-permute-start(bf16[192,1024]{1,0:T(8,128)(2,1)S(1)} %place_far_tokens.1), channel_id=1, source_target_pairs={{0,24},{4,28},{8,16},{12,20},{16,8},{20,12},{24,0},{28,4},{1,25},{... | collective-permute-start | bytes 1179656 | tf_op jit(solution)/shard_map/ppermute | solution.py:425
  14.5 15.0 %collective-permute-start.3 = (bf16[192,1024]{1,0:T(8,128)(2,1)S(1)}, bf16[192,1024]{1,0:T(8,128)(2,1)S(1)}, u32[]{:S(2)}, u32[]{:S(2)}) collective-permute-start(bf16[192,1024]{1,0:T(8,128)(2,1)S(1)} %get-tuple-element.67), channel_id=1, source_target_pairs={{0,24},{4,28},{8,16},{12,20},{16,8},{20,12},{24,0},{28,4},{1,25},{... | collective-permute-start | bytes 1179656 | tf_op jit(solution)/shard_map/ppermute | solution.py:425
  17.8 35.3 %collective-permute-start.8 = (bf16[192,2048]{1,0:T(8,128)(2,1)S(1)}, bf16[192,2048]{1,0:T(8,128)(2,1)S(1)}, u32[]{:S(2)}, u32[]{:S(2)}) collective-permute-start(bf16[192,2048]{1,0:T(8,128)(2,1)S(1)} %get-tuple-element.79), channel_id=1, source_target_pairs={{0,8},{4,12},{8,0},{12,4},{16,24},{20,28},{24,16},{28,20},{1,9},{5... | collective-permute-start | bytes 2359304 | tf_op jit(solution)/shard_map/ppermute | solution.py:425
  19.8 33.3 %collective-permute-start.9 = (bf16[192,2048]{1,0:T(8,128)(2,1)S(1)}, bf16[192,2048]{1,0:T(8,128)(2,1)S(1)}, u32[]{:S(2)}, u32[]{:S(2)}) collective-permute-start(bf16[192,2048]{1,0:T(8,128)(2,1)S(1)} %get-tuple-element.80), channel_id=1, source_target_pairs={{0,16},{4,20},{8,24},{12,28},{16,0},{20,4},{24,8},{28,12},{1,17},{... | collective-permute-start | bytes 2359304 | tf_op jit(solution)/shard_map/ppermute | solution.py:425
  21.4 10.2 %collective-permute-start.6 = (bf16[192,1024]{1,0:T(8,128)(2,1)S(1)}, bf16[192,1024]{1,0:T(8,128)(2,1)S(1)}, u32[]{:S(2)}, u32[]{:S(2)}) collective-permute-start(bf16[192,1024]{1,0:T(8,128)(2,1)S(1)} %collective-permute-done.5.refs_1_), channel_id=1, source_target_pairs={{0,1},{1,0},{2,3},{3,2},{4,5},{5,4},{6,7},{7,6},{8,9},{9,8},{10,11... | collective-permute-start | bytes 1179656 | tf_op jit(solution)/shard_map/ppermute | solution.py:425
  29.5 13.8 %collective-permute-start.4 = (bf16[192,1024]{1,0:T(8,128)(2,1)S(1)}, bf16[192,1024]{1,0:T(8,128)(2,1)S(1)}, u32[]{:S(2)}, u32[]{:S(2)}) collective-permute-start(bf16[192,1024]{1,0:T(8,128)(2,1)S(1)} %collective-permute-done.3.refs_1_), channel_id=1, source_target_pairs={{0,1},{1,0},{2,3},{3,2},{4,5},{5,4},{6,7},{7,6},{8,9},{9,8},{10,11... | collective-permute-start | bytes 1179656 | tf_op jit(solution)/shard_map/ppermute | solution.py:425
  31.6 31.1 %collective-permute-start.11 = (bf16[192,2048]{1,0:T(8,128)(2,1)S(1)}, bf16[192,2048]{1,0:T(8,128)(2,1)S(1)}, u32[]{:S(2)}, u32[]{:S(2)}) collective-permute-start(bf16[192,2048]{1,0:T(8,128)(2,1)S(1)} %get-tuple-element.85), channel_id=1, source_target_pairs={{0,16},{4,20},{8,24},{12,28},{16,0},{20,4},{24,8},{28,12},{1,17},{... | collective-permute-start | bytes 2359304 | tf_op jit(solution)/shard_map/ppermute | solution.py:425
  33.1 29.9 %collective-permute-start.10 = (bf16[192,2048]{1,0:T(8,128)(2,1)S(1)}, bf16[192,2048]{1,0:T(8,128)(2,1)S(1)}, u32[]{:S(2)}, u32[]{:S(2)}) collective-permute-start(bf16[192,2048]{1,0:T(8,128)(2,1)S(1)} %get-tuple-element.83), channel_id=1, source_target_pairs={{0,8},{4,12},{8,0},{12,4},{16,24},{20,28},{24,16},{28,20},{1,9},{5... | collective-permute-start | bytes 2359304 | tf_op jit(solution)/shard_map/ppermute | solution.py:425
  52.0 8.8 %collective-permute-start.7 = (bf16[192,1024]{1,0:T(8,128)(2,1)S(1)}, bf16[192,1024]{1,0:T(8,128)(2,1)S(1)}, u32[]{:S(2)}, u32[]{:S(2)}) collective-permute-start(bf16[192,1024]{1,0:T(8,128)(2,1)S(1)} %get-tuple-element.75), channel_id=1, source_target_pairs={{0,1},{1,0},{2,3},{3,2},{4,5},{5,4},{6,7},{7,6},{8,9},{9,8},{10,11... | collective-permute-start | bytes 1179656 | tf_op jit(solution)/shard_map/ppermute | solution.py:425
  63.1 12.4 %collective-permute-start.12 = (bf16[192,1024]{1,0:T(8,128)(2,1)S(1)}, bf16[192,1024]{1,0:T(8,128)(2,1)S(1)}, u32[]{:S(2)}, u32[]{:S(2)}) collective-permute-start(bf16[192,1024]{1,0:T(8,128)(2,1)S(1)} %add_convert_fusion.1), channel_id=1, source_target_pairs={{0,24},{4,28},{8,16},{12,20},{16,8},{20,12},{24,0},{28,4},{1,25},{... | collective-permute-start | bytes 1179656 | tf_op jit(solution)/shard_map/ppermute | solution.py:425
  71.7 12.3 %collective-permute-start.14 = (bf16[192,1024]{1,0:T(8,128)(2,1)S(1)}, bf16[192,1024]{1,0:T(8,128)(2,1)S(1)}, u32[]{:S(2)}, u32[]{:S(2)}) collective-permute-start(bf16[192,1024]{1,0:T(8,128)(2,1)S(1)} %get-tuple-element.95), channel_id=1, source_target_pairs={{0,8},{4,12},{8,0},{12,4},{16,24},{20,28},{24,16},{28,20},{1,9},{5... | collective-permute-start | bytes 1179656 | tf_op jit(solution)/shard_map/ppermute | solution.py:425
  72.3 11.7 %collective-permute-start.15 = (bf16[192,1024]{1,0:T(8,128)(2,1)S(1)}, bf16[192,1024]{1,0:T(8,128)(2,1)S(1)}, u32[]{:S(2)}, u32[]{:S(2)}) collective-permute-start(bf16[192,1024]{1,0:T(8,128)(2,1)S(1)} %get-tuple-element.102), channel_id=1, source_target_pairs={{0,16},{4,20},{8,24},{12,28},{16,0},{20,4},{24,8},{28,12},{1,17},{... | collective-permute-start | bytes 1179656 | tf_op jit(solution)/shard_map/ppermute | solution.py:425
  85.3 3.6 %collective-permute-start.16 = (bf16[256,1024]{1,0:T(8,128)(2,1)S(1)}, bf16[256,1024]{1,0:T(8,128)(2,1)S(1)}, u32[]{:S(2)}, u32[]{:S(2)}) collective-permute-start(bf16[256,1024]{1,0:T(8,128)(2,1)S(1)} %get-tuple-element.104), channel_id=1, source_target_pairs={{0,4},{4,0},{8,12},{12,8},{16,20},{20,16},{24,28},{28,24},{1,5},{5... | collective-permute-start | bytes 1572872 | tf_op jit(solution)/shard_map/ppermute | solution.py:425
  85.3 11.8 %collective-permute-start.13 = (bf16[192,1024]{1,0:T(8,128)(2,1)S(1)}, bf16[192,1024]{1,0:T(8,128)(2,1)S(1)}, u32[]{:S(2)}, u32[]{:S(2)}) collective-permute-start(bf16[192,1024]{1,0:T(8,128)(2,1)S(1)} %get-tuple-element.97), channel_id=1, source_target_pairs={{0,8},{4,12},{8,0},{12,4},{16,24},{20,28},{24,16},{28,20},{1,9},{5... | collective-permute-start | bytes 1179656 | tf_op jit(solution)/shard_map/ppermute | solution.py:425
  87.5 11.2 %collective-permute-start.17 = (bf16[192,1024]{1,0:T(8,128)(2,1)S(1)}, bf16[192,1024]{1,0:T(8,128)(2,1)S(1)}, u32[]{:S(2)}, u32[]{:S(2)}) collective-permute-start(bf16[192,1024]{1,0:T(8,128)(2,1)S(1)} %get-tuple-element.108), channel_id=1, source_target_pairs={{0,16},{4,20},{8,24},{12,28},{16,0},{20,4},{24,8},{28,12},{1,17},{... | collective-permute-start | bytes 1179656 | tf_op jit(solution)/shard_map/ppermute | solution.py:425
  89.1 23.7 %collective-permute-start.19 = (bf16[256,512]{1,0:T(8,128)(2,1)S(1)}, bf16[256,512]{1,0:T(8,128)(2,1)S(1)}, u32[]{:S(2)}, u32[]{:S(2)}) collective-permute-start(bf16[256,512]{1,0:T(8,128)(2,1)S(1)} %get-tuple-element.122), channel_id=1, source_target_pairs={{0,3},{1,2},{2,1},{3,0},{4,7},{5,6},{6,5},{7,4},{8,11},{9,10},{10,... | collective-permute-start | bytes 786440 | tf_op jit(solution)/shard_map/ppermute | solution.py:425
  92.7 22.5 %collective-permute-start.18 = (bf16[256,512]{1,0:T(8,128)(2,1)S(1)}, bf16[256,512]{1,0:T(8,128)(2,1)S(1)}, u32[]{:S(2)}, u32[]{:S(2)}) collective-permute-start(bf16[256,512]{1,0:T(8,128)(2,1)S(1)} %get-tuple-element.123), channel_id=1, source_target_pairs={{0,2},{1,3},{2,0},{3,1},{4,6},{5,7},{6,4},{7,5},{8,10},{9,11},{10,... | collective-permute-start | bytes 786440 | tf_op jit(solution)/shard_map/ppermute | solution.py:425
  99.9 15.4 %collective-permute-start.20 = (bf16[256,512]{1,0:T(8,128)(2,1)S(1)}, bf16[256,512]{1,0:T(8,128)(2,1)S(1)}, u32[]{:S(2)}, u32[]{:S(2)}) collective-permute-start(bf16[256,512]{1,0:T(8,128)(2,1)S(1)} %get-tuple-element.110), channel_id=1, source_target_pairs={{0,4},{4,0},{8,12},{12,8},{16,20},{20,16},{24,28},{28,24},{1,5},{5... | collective-permute-start | bytes 786440 | tf_op jit(solution)/shard_map/ppermute | solution.py:425
  100.0 4.0 %collective-permute-start.21 = (bf16[256,512]{1,0:T(8,128)(2,1)S(1)}, bf16[256,512]{1,0:T(8,128)(2,1)S(1)}, u32[]{:S(2)}, u32[]{:S(2)}) collective-permute-start(bf16[256,512]{1,0:T(8,128)(2,1)S(1)} %get-tuple-element.112), channel_id=1, source_target_pairs={{0,4},{4,0},{8,12},{12,8},{16,20},{20,16},{24,28},{28,24},{1,5},{5... | collective-permute-start | bytes 786440 | tf_op jit(solution)/shard_map/ppermute | solution.py:425
  104.1 14.0 %collective-permute-start.22 = (bf16[256,512]{1,0:T(8,128)(2,1)S(1)}, bf16[256,512]{1,0:T(8,128)(2,1)S(1)}, u32[]{:S(2)}, u32[]{:S(2)}) collective-permute-start(bf16[256,512]{1,0:T(8,128)(2,1)S(1)} %add_convert_fusion.3), channel_id=1, source_target_pairs={{0,1},{1,0},{2,3},{3,2},{4,5},{5,4},{6,7},{7,6},{8,9},{9,8},{10,11... | collective-permute-start | bytes 786440 | tf_op jit(solution)/shard_map/ppermute | solution.py:425
  (3 other events, 12.3 us)

commit v4 on v3

--- a/solution.py
+++ b/solution.py
@@ -12,9 +12,10 @@
 VMEM_LIMIT = 20 * 1024 * 1024
 COST = {"forward_near": 60000, "backward_near": 1000, "own_and_far_input_grads": 100, "near_grads_away": 20000, "near_grads_here": 100, "gate_and_up_0": 1000, "gate_and_up_1": 5000, "gate_and_up_2": 20000, "gate_and_up_3": 20000, "combine_away": 20000, "combine_here": 20000, "place_tokens": 100}
 COST = {name: 10**6 * cost for name, cost in COST.items()}
-LATE_QUARTER = True
-FAR_FIRST = 'here'
+FAR_FIRST = 'down'
 SIDE_LAST = 'core'
+OPT_DOWN_LATE = True
+OPT_FAR_WAITS = False
 
 
 def contract(left, right, left_dim, right_dim):
@@ -488,7 +489,7 @@
     x_all, hidden, to_a, to_b = forward(
         "forward_near", where, 1, pick(x, plan.near), [], [], w_gate, w_up, (after(x_all, give), hidden)
     )
-    far_sum = (keep + after(got, hidden, *pick(r, plan.near)).astype(F32)).astype(BF16)
+    far_sum = (keep + after(got, hidden, *(pick(r, plan.near) if OPT_FAR_WAITS else [])).astype(F32)).astype(BF16)
     rows = 2 * cap
     far = [swap(far_sum[i * rows : (i + 1) * rows], "expert", 2 * c) for i, c in enumerate(plan.far)]
     kept = (after(r_all, far_sum), after(grad_a, give), after(grad_b, give))
@@ -506,9 +507,14 @@
     slab = width // dp
     away, here = list(range(dp // 2, dp)), list(range(dp // 2))
 
-    hidden = after(hidden, here_part[0], *(far if FAR_FIRST == "down" else []))
-    (grad_down,) = outer("down_grad", where, hidden, [r_all])
-    away_rows[0] = after(away_rows[0], grad_down)
+    rights = [grad_a, grad_b]
+    first = [here_part[0], *(far if FAR_FIRST == "down" else [])]
+    if OPT_DOWN_LATE:
+        grads = outer("gate_and_up_0", where, after(x_all, *first), rights, 0, 4)
+        away_rows[0] = after(away_rows[0], grads[0])
+    else:
+        (grad_down,) = outer("down_grad", where, after(hidden, *first), [r_all])
+        away_rows[0] = after(away_rows[0], grad_down)
     away_sum, other = combine(
         plan, where, placings, [own, *far, *away_rows], dp, cap, away, True
     )
@@ -516,21 +522,20 @@
     away_sum = (away_sum + other.astype(F32)).astype(BF16)
     parts = [away_sum[:, n * slab : (n + 1) * slab] for n in range(len(away))]
     away_sums = [swap(part, "dp", s) for part, s in zip(parts, away, strict=True)]
-    rights = [grad_a, grad_b]
-    x_all = after(x_all, *parts)
-    early = 1 if LATE_QUARTER else 2
-    grads = ()
-    for part in range(early):
-        grads = outer(f"gate_and_up_{part}", where, x_all, rights, part, 4, grads)
-    here_rows[0] = after(here_rows[0], grads[0])
+    if OPT_DOWN_LATE:
+        (grad_down,) = outer("down_grad", where, after(hidden, *parts), [r_all])
+        here_rows[0] = after(here_rows[0], grad_down)
+    else:
+        grads = outer("gate_and_up_0", where, after(x_all, *parts), rights, 0, 4)
+        here_rows[0] = after(here_rows[0], grads[0])
     total, other, *rest = combine(
         plan, where, placings, [own, *far, *here_rows], dp, cap, here, False
     )
     got = [swap(other, "expert", 1)]
     x_all = after(x_all, total)
-    for part in range(early, 4):
+    for part in range(1, 4):
         grads = outer(f"gate_and_up_{part}", where, x_all, rights, part, 4, grads)
-        for n, s in enumerate(here[1:] if part == early else []):
+        for n, s in enumerate(here[1:] if part == 1 else []):
             if SIDE_LAST == "cross":
                 got += [swap(rest[2 * n], "dp", s), cross(rest[2 * n + 1], s)]
             else:

time: 119 us -> 116 us (0.975)
  waiting for transfers between devices: 22 us -> 20.2 us
  starting transfers between devices: 29.6 us -> 28 us
    ppermute x23, waiting for transfers between devices: 22 us -> 20.2 us  [swap(): return lax.ppermute(rows, axis, [(i, i ^ mask) for i in range(count)])]
    ppermute x23, starting transfers between devices: 29.6 us -> 28 us  [swap(): return lax.ppermute(rows, axis, [(i, i ^ mask) for i in range(count)])]
  transfers between devices with their start and end apart: 23 -> 23, of which waited for: 10 -> 9; matrix products, arithmetic and copies ran while one was open for 1% -> 2% of each run, Pallas kernels for 51% -> 52%
where the time goes in v4:
time: 116 us
  Pallas kernels  61.7 us (53%)
  starting transfers between devices  28 us (24%)
  waiting for transfers between devices  20.2 us (17%)
  other arithmetic  2.62 us (2%)
  local copies, waits for them, and re-layouts  2.24 us (2%)
    pallas_call x15, Pallas kernels, call(): pl.pallas_call(inner, input_output_aliases={i + 1: i for i in range(len(k...  59.1 us
    ppermute x23, starting transfers between devices, swap(): return lax.ppermute(rows, axis, [(i, i ^ mask) for i in range(count)])  28 us
    ppermute x23, waiting for transfers between devices, swap(): return lax.ppermute(rows, axis, [(i, i ^ mask) for i in range(count)])  20.2 us
    pallas_call x2, Pallas kernels, combine(): pl.pallas_call(functools.partial(combine_kernel, plan, cap, dp, shifts, s...  2.53 us
  transfers between devices with their start and end apart: 23, of which 9 were waited for; matrix products, arithmetic and copies ran while one was open for 2% of the time, Pallas kernels for 52%

profile of v4, /device:TPU:0, one launch (start us, length us, event | category | flops | bytes accessed | tf_op | source)
XLA Modules:
  0.0 115.6 jit_solution(12618320458313076225)
XLA Ops:
  3.1 1.8 %collective-permute-done.refs_1_ = f32[4,256]{1,0:T(4,128)S(1)} collective-permute-done((f32[4,256]{1,0:T(4,128)S(1)}, f32[4,256]{1,0:T(4,128)S(1)}, u32[]{:S(2)}, u32[]{:S(2)}) %collective-permute-start) | collective-permute-done | bytes 4128 | tf_op jit(solution)/shard_map/ppermute | solution.py:426
  4.9 2.3 %place_far_tokens.1 = bf16[192,1024]{1,0:T(8,128)(2,1)S(1)} custom-call(s32[2]{0:T(128)S(1)} %pad_add_fusion.where, f32[4,256]{1,0:T(4,128)S(1)} %pad_maximum_fusion.refs_0_, f32[4,256]{1,0:T(4,128)S(1)} %collective-permute-done.refs_1_, bf16[256,2048]{1,0:T(8,128)(2,1)} %refs_2_.7, bf16[256,2048]{1,0:T(8,128)(2,1)S(1)} %collective-permute-done.1.refs_3_), custom_call_target="tpu_custom_call" | custom-call | tf_op jit(solution)/shard_map/place_far_tokens/pallas_call | solution.py:42
  7.3 3.9 %collective-permute-start.5 = (bf16[192,1024]{1,0:T(8,128)(2,1)S(1)}, bf16[192,1024]{1,0:T(8,128)(2,1)S(1)}, u32[]{:S(2)}, u32[]{:S(2)}) collective-permute-start(bf16[192,1024]{1,0:T(8,128)(2,1)S(1)} %place_far_tokens.1), channel_id=1, source_target_pairs={{0,24},{4,28},{8,16},{12,20},{16,8},{20,12},{24,0},{28,4},{1,25},{... | collective-permute-start | bytes 1179656 | tf_op jit(solution)/shard_map/ppermute | solution.py:426
  11.1 3.4 %place_scaled.1 = (bf16[192,2048]{1,0:T(8,128)(2,1)S(1)}, bf16[192,2048]{1,0:T(8,128)(2,1)S(1)}, bf16[192,2048]{1,0:T(8,128)(2,1)S(1)}, bf16[192,1024]{1,0:T(8,128)(2,1)S(1)}) custom-call(s32[2]{0:T(128)S(1)} %pad_add_fusion.where, f32[4,256]{1,0:T(4,128)S(1)} %pad_maximum_fusion.refs_0_, f32[4,256]{1,0:T(4,128)S(1)} %collective-permute-done.refs_1_, ...), custom_call_target="tpu_custom_call" | custom-call | tf_op jit(solution)/shard_map/place_scaled/pallas_call | solution.py:42
  14.6 3.2 %place_tokens.1 = (bf16[192,2048]{1,0:T(8,128)(2,1)S(1)}, bf16[192,2048]{1,0:T(8,128)(2,1)S(1)}, bf16[192,2048]{1,0:T(8,128)(2,1)S(1)}, bf16[384,256]{1,0:T(8,128)(2,1)S(1)}, bf16[384,256]{1,0:T(8,128)(2,1)S(1)}) custom-call(s32[2]{0:T(128)S(1)} %pad_add_fusion.where, f32[4,256]{1,0:T(4,128)S(1)} %pad_maximum_fusion.refs_0_, ...), custom_call_target="tpu_custom_call" | custom-call | flops 100000000 | tf_op jit(solution)/shard_map/place_tokens/pallas_call | solution.py:42
  17.8 2.0 %collective-permute-start.8 = (bf16[192,2048]{1,0:T(8,128)(2,1)S(1)}, bf16[192,2048]{1,0:T(8,128)(2,1)S(1)}, u32[]{:S(2)}, u32[]{:S(2)}) collective-permute-start(bf16[192,2048]{1,0:T(8,128)(2,1)S(1)} %get-tuple-element.79), channel_id=1, source_target_pairs={{0,8},{4,12},{8,0},{12,4},{16,24},{20,28},{24,16},{28,20},{1,9},{5... | collective-permute-start | bytes 2359304 | tf_op jit(solution)/shard_map/ppermute | solution.py:426
  23.1 6.4 %collective-permute-done.3.refs_1_ = bf16[192,1024]{1,0:T(8,128)(2,1)S(1)} collective-permute-done((bf16[192,1024]{1,0:T(8,128)(2,1)S(1)}, bf16[192,1024]{1,0:T(8,128)(2,1)S(1)}, u32[]{:S(2)}, u32[]{:S(2)}) %collective-permute-start.3) | collective-permute-done | bytes 393248 | tf_op jit(solution)/shard_map/ppermute | solution.py:426
  29.5 2.1 %collective-permute-start.4 = (bf16[192,1024]{1,0:T(8,128)(2,1)S(1)}, bf16[192,1024]{1,0:T(8,128)(2,1)S(1)}, u32[]{:S(2)}, u32[]{:S(2)}) collective-permute-start(bf16[192,1024]{1,0:T(8,128)(2,1)S(1)} %collective-permute-done.3.refs_1_), channel_id=1, source_target_pairs={{0,1},{1,0},{2,3},{3,2},{4,5},{5,4},{6,7},{7,6},{8,9},{9,8},{10,11... | collective-permute-start | bytes 1179656 | tf_op jit(solution)/shard_map/ppermute | solution.py:426
  34.6 2.2 %copy-done.1 = bf16[1,2048,1024]{2,1,0:T(8,128)(2,1)S(1)} copy-done((bf16[1,2048,1024]{2,1,0:T(8,128)(2,1)S(1)}, bf16[1,2048,1024]{2,1,0:T(8,128)(2,1)}, u32[]{:S(2)}) %copy-start.1) | copy-done | bytes 4194328
  36.8 6.5 %forward_own_and_far.1 = (bf16[768,2048]{1,0:T(8,128)(2,1)S(1)}, bf16[768,1024]{1,0:T(8,128)(2,1)S(1)}, f32[384,1024]{1,0:T(8,128)S(1)}, f32[384,1024]{1,0:T(8,128)S(1)}) custom-call(s32[2]{0:T(128)S(1)} %pad_add_fusion.where, bf16[192,2048]{1,0:T(8,128)(2,1)S(1)} %get-tuple-element.68.refs_0_, bf16[192,1024]{1,0:T(8,128)(2,1)S(1)} %collective-permute-done.5.refs_1_, ...), custom_call_target="tpu_custom_call" | custom-call | tf_op jit(solution)/shard_map/forward_own_and_far/pallas_call | solution.py:42
  43.4 3.6 %backward_own_and_far.1 = (bf16[768,2048]{1,0:T(8,128)(2,1)S(1)}, bf16[768,1024]{1,0:T(8,128)(2,1)S(1)}, bf16[768,1024]{1,0:T(8,128)(2,1)S(1)}) custom-call(s32[2]{0:T(128)S(1)} %pad_add_fusion.where, bf16[192,2048]{1,0:T(8,128)(2,1)S(1)} %get-tuple-element.66.refs_0_, bf16[192,1024]{1,0:T(8,128)(2,1)S(1)} %collective-permute-done.3.refs_1_, ...), custom_call_target="tpu_custom_call" | custom-call | tf_op jit(solution)/shard_map/backward_own_and_far/pallas_call | solution.py:42
  47.0 5.0 %own_and_far_input_grads.1 = (bf16[192,2048]{1,0:T(8,128)(2,1)S(1)}, bf16[192,1024]{1,0:T(8,128)(2,1)S(1)}, f32[192,1024]{1,0:T(8,128)S(1)}) custom-call(s32[2]{0:T(128)S(1)} %pad_add_fusion.where, bf16[768,1024]{1,0:T(8,128)(2,1)S(1)} %get-tuple-element.85.refs_0_.refs_1_, bf16[768,1024]{1,0:T(8,128)(2,1)S(1)} %get-tuple-element.86.refs_1_.refs_2_, ...), custom_call_target="tpu_custom_call" | custom-call | flops 100000000 | tf_op jit(solution)/shard_map/own_and_far_input_grads/pallas_call | solution.py:42
  53.1 6.3 %forward_near.1 = (bf16[768,2048]{1,0:T(8,128)(2,1)S(1)}, bf16[768,1024]{1,0:T(8,128)(2,1)S(1)}, f32[384,1024]{1,0:T(8,128)S(1)}, f32[384,1024]{1,0:T(8,128)S(1)}) custom-call(s32[2]{0:T(128)S(1)} %pad_add_fusion.where, bf16[768,2048]{1,0:T(8,128)(2,1)S(1)} %get-tuple-element.77.refs_0_, ...), custom_call_target="tpu_custom_call", output_to_operand_aliasing={{0}: (1, {}), {1}: (2, {})} | custom-call | flops 60000002048 | tf_op jit(solution)/shard_map/forward_near/pallas_call | solution.py:42
  63.8 3.5 %backward_near.1 = (bf16[768,2048]{1,0:T(8,128)(2,1)S(1)}, bf16[768,1024]{1,0:T(8,128)(2,1)S(1)}, bf16[768,1024]{1,0:T(8,128)(2,1)S(1)}) custom-call(s32[2]{0:T(128)S(1)} %pad_add_fusion.where, bf16[768,2048]{1,0:T(8,128)(2,1)S(1)} %get-tuple-element.84.refs_0_, ...), custom_call_target="tpu_custom_call", output_to_operand_aliasing={{0}: (1, {}), {1}: (2, {}), {2}: (3, {})} | custom-call | flops 1000000000 | tf_op jit(solution)/shard_map/backward_near/pallas_call | solution.py:42
  67.3 2.7 %near_grads_away.1 = (bf16[192,1024]{1,0:T(8,128)(2,1)S(1)}, bf16[192,1024]{1,0:T(8,128)(2,1)S(1)}) custom-call(s32[2]{0:T(128)S(1)} %pad_add_fusion.where, bf16[768,1024]{1,0:T(8,128)(2,1)S(1)} %get-tuple-element.96.refs_0_.refs_1_.refs_3_, bf16[768,1024]{1,0:T(8,128)(2,1)S(1)} %get-tuple-element.94.refs_1_.refs_2_.refs_4_, ...), custom_call_target="tpu_custom_call" | custom-call | flops 20000000000 | tf_op jit(solution)/shard_map/near_grads_away/pallas_call | solution.py:42
  72.9 2.6 %near_grads_here.1 = (bf16[192,1024]{1,0:T(8,128)(2,1)S(1)}, bf16[192,1024]{1,0:T(8,128)(2,1)S(1)}) custom-call(s32[2]{0:T(128)S(1)} %pad_add_fusion.where, bf16[768,1024]{1,0:T(8,128)(2,1)S(1)} %get-tuple-element.96.refs_0_.refs_1_.refs_3_, bf16[768,1024]{1,0:T(8,128)(2,1)S(1)} %get-tuple-element.94.refs_1_.refs_2_.refs_4_, ...), custom_call_target="tpu_custom_call" | custom-call | flops 100000000 | tf_op jit(solution)/shard_map/near_grads_here/pallas_call | solution.py:42
  75.6 3.5 %gate_and_up_0.1 = (bf16[1,2048,1024]{2,1,0:T(8,128)(2,1)}, bf16[1,2048,1024]{2,1,0:T(8,128)(2,1)}) custom-call(s32[2]{0:T(128)S(1)} %pad_add_fusion.where, bf16[768,2048]{1,0:T(8,128)(2,1)S(1)} %get-tuple-element.114.refs_0_.refs_2_, bf16[768,1024]{1,0:T(8,128)(2,1)S(1)} %get-tuple-element.96.refs_0_.refs_1_.refs_3_, ...), custom_call_target="tpu_custom_call" | custom-call | flops 1000000000 | tf_op jit(solution)/shard_map/gate_and_up_0/pallas_call | solution.py:42
  85.7 3.7 %collective-permute-start.19 = (bf16[256,512]{1,0:T(8,128)(2,1)S(1)}, bf16[256,512]{1,0:T(8,128)(2,1)S(1)}, u32[]{:S(2)}, u32[]{:S(2)}) collective-permute-start(bf16[256,512]{1,0:T(8,128)(2,1)S(1)} %get-tuple-element.122), channel_id=1, source_target_pairs={{0,3},{1,2},{2,1},{3,0},{4,7},{5,6},{6,5},{7,4},{8,11},{9,10},{10,... | collective-permute-start | bytes 786440 | tf_op jit(solution)/shard_map/ppermute | solution.py:426
  89.4 5.9 %down_grad.1 = bf16[1,1024,2048]{2,1,0:T(8,128)(2,1)} custom-call(s32[2]{0:T(128)S(1)} %pad_add_fusion.where, bf16[768,1024]{1,0:T(8,128)(2,1)S(1)} %get-tuple-element.105.refs_0_, bf16[768,2048]{1,0:T(8,128)(2,1)S(1)} %get-tuple-element.106.refs_1_), custom_call_target="tpu_custom_call" | custom-call | tf_op jit(solution)/shard_map/down_grad/pallas_call | solution.py:42
  97.1 3.5 %gate_and_up_1.1 = (bf16[1,2048,1024]{2,1,0:T(8,128)(2,1)}, bf16[1,2048,1024]{2,1,0:T(8,128)(2,1)}) custom-call(s32[2]{0:T(128)S(1)} %pad_add_fusion.where, bf16[1,2048,1024]{2,1,0:T(8,128)(2,1)} %get-tuple-element.100.refs_0_, bf16[1,2048,1024]{2,1,0:T(8,128)(2,1)} %get-tuple-element.113.refs_1_, ...), custom_call_target="tpu_custom_call", output_to_operand_aliasing={{0}: (1, {}), {1}: (2, {})} | custom-call | flops 5000000000 | tf_op jit(solution)/shard_map/gate_and_up_1/pallas_call | solution.py:42
  102.3 3.5 %gate_and_up_2.1 = (bf16[1,2048,1024]{2,1,0:T(8,128)(2,1)}, bf16[1,2048,1024]{2,1,0:T(8,128)(2,1)}) custom-call(s32[2]{0:T(128)S(1)} %pad_add_fusion.where, bf16[1,2048,1024]{2,1,0:T(8,128)(2,1)} %get-tuple-element.115.refs_0_, bf16[1,2048,1024]{2,1,0:T(8,128)(2,1)} %get-tuple-element.117.refs_1_, ...), custom_call_target="tpu_custom_call", output_to_operand_aliasing={{0}: (1, {}), {1}: (2, {})} | custom-call | flops 20000000000 | tf_op jit(solution)/shard_map/gate_and_up_2/pallas_call | solution.py:42
  105.8 3.5 %gate_and_up_3.1 = (bf16[1,2048,1024]{2,1,0:T(8,128)(2,1)}, bf16[1,2048,1024]{2,1,0:T(8,128)(2,1)}) custom-call(s32[2]{0:T(128)S(1)} %pad_add_fusion.where, bf16[1,2048,1024]{2,1,0:T(8,128)(2,1)} %get-tuple-element.118.refs_0_, bf16[1,2048,1024]{2,1,0:T(8,128)(2,1)} %get-tuple-element.119.refs_1_, ...), custom_call_target="tpu_custom_call", output_to_operand_aliasing={{0}: (1, {}), {1}: (2, {})} | custom-call | flops 20000000000 | tf_op jit(solution)/shard_map/gate_and_up_3/pallas_call | solution.py:42
  109.4 2.5 %collective-permute-done.18.refs_0_ = bf16[256,512]{1,0:T(8,128)(2,1)S(1)} collective-permute-done((bf16[256,512]{1,0:T(8,128)(2,1)S(1)}, bf16[256,512]{1,0:T(8,128)(2,1)S(1)}, u32[]{:S(2)}, u32[]{:S(2)}) %collective-permute-start.18) | collective-permute-done | bytes 262176 | tf_op jit(solution)/shard_map/ppermute | solution.py:426
  112.0 2.7 %collective-permute-done.22 = bf16[256,512]{1,0:T(8,128)(2,1)S(1)} collective-permute-done((bf16[256,512]{1,0:T(8,128)(2,1)S(1)}, bf16[256,512]{1,0:T(8,128)(2,1)S(1)}, u32[]{:S(2)}, u32[]{:S(2)}) %collective-permute-start.22) | collective-permute-done | bytes 262176 | tf_op jit(solution)/shard_map/ppermute | solution.py:426
  (56 shorter events, 28.3 us)
Async XLA Ops:
  0.6 4.3 %collective-permute-start.1 = (bf16[256,2048]{1,0:T(8,128)(2,1)}, bf16[256,2048]{1,0:T(8,128)(2,1)S(1)}, u32[]{:S(2)}, u32[]{:S(2)}) collective-permute-start(bf16[256,2048]{1,0:T(8,128)(2,1)} %refs_2_.7), channel_id=1, source_target_pairs={{0,4},{4,0},{8,12},{12,8},{16,20},{20,16},{24,28},{28,24},{1,5},{5... | collective-permute-start | bytes 3145736 | tf_op jit(solution)/shard_map/ppermute | solution.py:426
  1.1 10.0 %collective-permute-start.2 = (bf16[256,2048]{1,0:T(8,128)(2,1)}, bf16[256,2048]{1,0:T(8,128)(2,1)S(1)}, u32[]{:S(2)}, u32[]{:S(2)}) collective-permute-start(bf16[256,2048]{1,0:T(8,128)(2,1)} %refs_2_.8), channel_id=1, source_target_pairs={{0,4},{4,0},{8,12},{12,8},{16,20},{20,16},{24,28},{28,24},{1,5},{5... | collective-permute-start | bytes 3145736 | tf_op jit(solution)/shard_map/ppermute | solution.py:426
  2.6 2.3 %collective-permute-start = (f32[4,256]{1,0:T(4,128)S(1)}, f32[4,256]{1,0:T(4,128)S(1)}, u32[]{:S(2)}, u32[]{:S(2)}) collective-permute-start(f32[4,256]{1,0:T(4,128)S(1)} %pad_maximum_fusion.refs_0_), channel_id=1, source_target_pairs={{0,4},{4,0},{8,12},{12,8},{16,20},{20,16},{24,28},{28,24},{1,5},{5... | collective-permute-start | bytes 12296 | tf_op jit(solution)/shard_map/ppermute | solution.py:426
  3.1 31.5 %copy-start = (bf16[1,2048,1024]{2,1,0:T(8,128)(2,1)S(1)}, bf16[1,2048,1024]{2,1,0:T(8,128)(2,1)}, u32[]{:S(2)}) copy-start(bf16[1,2048,1024]{2,1,0:T(8,128)(2,1)} %refs_2_.11) | copy-start | bytes 12582916
  7.3 14.1 %collective-permute-start.5 = (bf16[192,1024]{1,0:T(8,128)(2,1)S(1)}, bf16[192,1024]{1,0:T(8,128)(2,1)S(1)}, u32[]{:S(2)}, u32[]{:S(2)}) collective-permute-start(bf16[192,1024]{1,0:T(8,128)(2,1)S(1)} %place_far_tokens.1), channel_id=1, source_target_pairs={{0,24},{4,28},{8,16},{12,20},{16,8},{20,12},{24,0},{28,4},{1,25},{... | collective-permute-start | bytes 1179656 | tf_op jit(solution)/shard_map/ppermute | solution.py:426
  14.5 15.0 %collective-permute-start.3 = (bf16[192,1024]{1,0:T(8,128)(2,1)S(1)}, bf16[192,1024]{1,0:T(8,128)(2,1)S(1)}, u32[]{:S(2)}, u32[]{:S(2)}) collective-permute-start(bf16[192,1024]{1,0:T(8,128)(2,1)S(1)} %get-tuple-element.67), channel_id=1, source_target_pairs={{0,24},{4,28},{8,16},{12,20},{16,8},{20,12},{24,0},{28,4},{1,25},{... | collective-permute-start | bytes 1179656 | tf_op jit(solution)/shard_map/ppermute | solution.py:426
  17.8 35.3 %collective-permute-start.8 = (bf16[192,2048]{1,0:T(8,128)(2,1)S(1)}, bf16[192,2048]{1,0:T(8,128)(2,1)S(1)}, u32[]{:S(2)}, u32[]{:S(2)}) collective-permute-start(bf16[192,2048]{1,0:T(8,128)(2,1)S(1)} %get-tuple-element.79), channel_id=1, source_target_pairs={{0,8},{4,12},{8,0},{12,4},{16,24},{20,28},{24,16},{28,20},{1,9},{5... | collective-permute-start | bytes 2359304 | tf_op jit(solution)/shard_map/ppermute | solution.py:426
  19.8 33.3 %collective-permute-start.9 = (bf16[192,2048]{1,0:T(8,128)(2,1)S(1)}, bf16[192,2048]{1,0:T(8,128)(2,1)S(1)}, u32[]{:S(2)}, u32[]{:S(2)}) collective-permute-start(bf16[192,2048]{1,0:T(8,128)(2,1)S(1)} %get-tuple-element.80), channel_id=1, source_target_pairs={{0,16},{4,20},{8,24},{12,28},{16,0},{20,4},{24,8},{28,12},{1,17},{... | collective-permute-start | bytes 2359304 | tf_op jit(solution)/shard_map/ppermute | solution.py:426
  21.4 10.2 %collective-permute-start.6 = (bf16[192,1024]{1,0:T(8,128)(2,1)S(1)}, bf16[192,1024]{1,0:T(8,128)(2,1)S(1)}, u32[]{:S(2)}, u32[]{:S(2)}) collective-permute-start(bf16[192,1024]{1,0:T(8,128)(2,1)S(1)} %collective-permute-done.5.refs_1_), channel_id=1, source_target_pairs={{0,1},{1,0},{2,3},{3,2},{4,5},{5,4},{6,7},{7,6},{8,9},{9,8},{10,11... | collective-permute-start | bytes 1179656 | tf_op jit(solution)/shard_map/ppermute | solution.py:426
  29.5 13.8 %collective-permute-start.4 = (bf16[192,1024]{1,0:T(8,128)(2,1)S(1)}, bf16[192,1024]{1,0:T(8,128)(2,1)S(1)}, u32[]{:S(2)}, u32[]{:S(2)}) collective-permute-start(bf16[192,1024]{1,0:T(8,128)(2,1)S(1)} %collective-permute-done.3.refs_1_), channel_id=1, source_target_pairs={{0,1},{1,0},{2,3},{3,2},{4,5},{5,4},{6,7},{7,6},{8,9},{9,8},{10,11... | collective-permute-start | bytes 1179656 | tf_op jit(solution)/shard_map/ppermute | solution.py:426
  31.6 31.5 %collective-permute-start.12 = (bf16[192,2048]{1,0:T(8,128)(2,1)S(1)}, bf16[192,2048]{1,0:T(8,128)(2,1)S(1)}, u32[]{:S(2)}, u32[]{:S(2)}) collective-permute-start(bf16[192,2048]{1,0:T(8,128)(2,1)S(1)} %get-tuple-element.90), channel_id=1, source_target_pairs={{0,16},{4,20},{8,24},{12,28},{16,0},{20,4},{24,8},{28,12},{1,17},{... | collective-permute-start | bytes 2359304 | tf_op jit(solution)/shard_map/ppermute | solution.py:426
  33.1 30.7 %collective-permute-start.11 = (bf16[192,2048]{1,0:T(8,128)(2,1)S(1)}, bf16[192,2048]{1,0:T(8,128)(2,1)S(1)}, u32[]{:S(2)}, u32[]{:S(2)}) collective-permute-start(bf16[192,2048]{1,0:T(8,128)(2,1)S(1)} %get-tuple-element.88), channel_id=1, source_target_pairs={{0,8},{4,12},{8,0},{12,4},{16,24},{20,28},{24,16},{28,20},{1,9},{5... | collective-permute-start | bytes 2359304 | tf_op jit(solution)/shard_map/ppermute | solution.py:426
  52.0 8.8 %collective-permute-start.7 = (bf16[192,1024]{1,0:T(8,128)(2,1)S(1)}, bf16[192,1024]{1,0:T(8,128)(2,1)S(1)}, u32[]{:S(2)}, u32[]{:S(2)}) collective-permute-start(bf16[192,1024]{1,0:T(8,128)(2,1)S(1)} %get-tuple-element.75), channel_id=1, source_target_pairs={{0,1},{1,0},{2,3},{3,2},{4,5},{5,4},{6,7},{7,6},{8,9},{9,8},{10,11... | collective-permute-start | bytes 1179656 | tf_op jit(solution)/shard_map/ppermute | solution.py:426
  60.8 14.8 %collective-permute-start.10 = (bf16[192,1024]{1,0:T(8,128)(2,1)S(1)}, bf16[192,1024]{1,0:T(8,128)(2,1)S(1)}, u32[]{:S(2)}, u32[]{:S(2)}) collective-permute-start(bf16[192,1024]{1,0:T(8,128)(2,1)S(1)} %add_convert_fusion.1), channel_id=1, source_target_pairs={{0,24},{4,28},{8,16},{12,20},{16,8},{20,12},{24,0},{28,4},{1,25},{... | collective-permute-start | bytes 1179656 | tf_op jit(solution)/shard_map/ppermute | solution.py:426
  70.0 10.6 %collective-permute-start.14 = (bf16[192,1024]{1,0:T(8,128)(2,1)S(1)}, bf16[192,1024]{1,0:T(8,128)(2,1)S(1)}, u32[]{:S(2)}, u32[]{:S(2)}) collective-permute-start(bf16[192,1024]{1,0:T(8,128)(2,1)S(1)} %get-tuple-element.95), channel_id=1, source_target_pairs={{0,8},{4,12},{8,0},{12,4},{16,24},{20,28},{24,16},{28,20},{1,9},{5... | collective-permute-start | bytes 1179656 | tf_op jit(solution)/shard_map/ppermute | solution.py:426
  71.6 10.5 %collective-permute-start.15 = (bf16[192,1024]{1,0:T(8,128)(2,1)S(1)}, bf16[192,1024]{1,0:T(8,128)(2,1)S(1)}, u32[]{:S(2)}, u32[]{:S(2)}) collective-permute-start(bf16[192,1024]{1,0:T(8,128)(2,1)S(1)} %get-tuple-element.102), channel_id=1, source_target_pairs={{0,16},{4,20},{8,24},{12,28},{16,0},{20,4},{24,8},{28,12},{1,17},{... | collective-permute-start | bytes 1179656 | tf_op jit(solution)/shard_map/ppermute | solution.py:426
  83.3 2.2 %collective-permute-start.16 = (bf16[256,1024]{1,0:T(8,128)(2,1)S(1)}, bf16[256,1024]{1,0:T(8,128)(2,1)S(1)}, u32[]{:S(2)}, u32[]{:S(2)}) collective-permute-start(bf16[256,1024]{1,0:T(8,128)(2,1)S(1)} %get-tuple-element.104), channel_id=1, source_target_pairs={{0,4},{4,0},{8,12},{12,8},{16,20},{20,16},{24,28},{28,24},{1,5},{5... | collective-permute-start | bytes 1572872 | tf_op jit(solution)/shard_map/ppermute | solution.py:426
  83.4 11.9 %collective-permute-start.13 = (bf16[192,1024]{1,0:T(8,128)(2,1)S(1)}, bf16[192,1024]{1,0:T(8,128)(2,1)S(1)}, u32[]{:S(2)}, u32[]{:S(2)}) collective-permute-start(bf16[192,1024]{1,0:T(8,128)(2,1)S(1)} %get-tuple-element.97), channel_id=1, source_target_pairs={{0,8},{4,12},{8,0},{12,4},{16,24},{20,28},{24,16},{28,20},{1,9},{5... | collective-permute-start | bytes 1179656 | tf_op jit(solution)/shard_map/ppermute | solution.py:426
  83.8 11.4 %collective-permute-start.17 = (bf16[192,1024]{1,0:T(8,128)(2,1)S(1)}, bf16[192,1024]{1,0:T(8,128)(2,1)S(1)}, u32[]{:S(2)}, u32[]{:S(2)}) collective-permute-start(bf16[192,1024]{1,0:T(8,128)(2,1)S(1)} %get-tuple-element.108), channel_id=1, source_target_pairs={{0,16},{4,20},{8,24},{12,28},{16,0},{20,4},{24,8},{28,12},{1,17},{... | collective-permute-start | bytes 1179656 | tf_op jit(solution)/shard_map/ppermute | solution.py:426
  85.7 23.6 %collective-permute-start.19 = (bf16[256,512]{1,0:T(8,128)(2,1)S(1)}, bf16[256,512]{1,0:T(8,128)(2,1)S(1)}, u32[]{:S(2)}, u32[]{:S(2)}) collective-permute-start(bf16[256,512]{1,0:T(8,128)(2,1)S(1)} %get-tuple-element.122), channel_id=1, source_target_pairs={{0,3},{1,2},{2,1},{3,0},{4,7},{5,6},{6,5},{7,4},{8,11},{9,10},{10,... | collective-permute-start | bytes 786440 | tf_op jit(solution)/shard_map/ppermute | solution.py:426
  89.4 22.5 %collective-permute-start.18 = (bf16[256,512]{1,0:T(8,128)(2,1)S(1)}, bf16[256,512]{1,0:T(8,128)(2,1)S(1)}, u32[]{:S(2)}, u32[]{:S(2)}) collective-permute-start(bf16[256,512]{1,0:T(8,128)(2,1)S(1)} %get-tuple-element.123), channel_id=1, source_target_pairs={{0,2},{1,3},{2,0},{3,1},{4,6},{5,7},{6,4},{7,5},{8,10},{9,11},{10,... | collective-permute-start | bytes 786440 | tf_op jit(solution)/shard_map/ppermute | solution.py:426
  96.6 15.4 %collective-permute-start.20 = (bf16[256,512]{1,0:T(8,128)(2,1)S(1)}, bf16[256,512]{1,0:T(8,128)(2,1)S(1)}, u32[]{:S(2)}, u32[]{:S(2)}) collective-permute-start(bf16[256,512]{1,0:T(8,128)(2,1)S(1)} %get-tuple-element.110), channel_id=1, source_target_pairs={{0,4},{4,0},{8,12},{12,8},{16,20},{20,16},{24,28},{28,24},{1,5},{5... | collective-permute-start | bytes 786440 | tf_op jit(solution)/shard_map/ppermute | solution.py:426
  96.6 4.0 %collective-permute-start.21 = (bf16[256,512]{1,0:T(8,128)(2,1)S(1)}, bf16[256,512]{1,0:T(8,128)(2,1)S(1)}, u32[]{:S(2)}, u32[]{:S(2)}) collective-permute-start(bf16[256,512]{1,0:T(8,128)(2,1)S(1)} %get-tuple-element.112), channel_id=1, source_target_pairs={{0,4},{4,0},{8,12},{12,8},{16,20},{20,16},{24,28},{28,24},{1,5},{5... | collective-permute-start | bytes 786440 | tf_op jit(solution)/shard_map/ppermute | solution.py:426
  100.7 14.0 %collective-permute-start.22 = (bf16[256,512]{1,0:T(8,128)(2,1)S(1)}, bf16[256,512]{1,0:T(8,128)(2,1)S(1)}, u32[]{:S(2)}, u32[]{:S(2)}) collective-permute-start(bf16[256,512]{1,0:T(8,128)(2,1)S(1)} %add_convert_fusion.3), channel_id=1, source_target_pairs={{0,1},{1,0},{2,3},{3,2},{4,5},{5,4},{6,7},{7,6},{8,9},{9,8},{10,11... | collective-permute-start | bytes 786440 | tf_op jit(solution)/shard_map/ppermute | solution.py:426
  (3 other events, 12.3 us)

commit v5 on v4

--- a/solution.py
+++ b/solution.py
@@ -12,10 +12,6 @@
 VMEM_LIMIT = 20 * 1024 * 1024
 COST = {"forward_near": 60000, "backward_near": 1000, "own_and_far_input_grads": 100, "near_grads_away": 20000, "near_grads_here": 100, "gate_and_up_0": 1000, "gate_and_up_1": 5000, "gate_and_up_2": 20000, "gate_and_up_3": 20000, "combine_away": 20000, "combine_here": 20000, "place_tokens": 100}
 COST = {name: 10**6 * cost for name, cost in COST.items()}
-FAR_FIRST = 'down'
-SIDE_LAST = 'core'
-OPT_DOWN_LATE = True
-OPT_FAR_WAITS = False
 
 
 def contract(left, right, left_dim, right_dim):
@@ -94,7 +90,8 @@
                 outs[len(chips) + side][place * cap : (place + 1) * cap, :] = placing.astype(BF16)
             if chip not in chips:
                 continue
-            rows = tables[side][:, half] if chip in plan.far else tables[side][...]
+            narrow = chip in plan.far and width > outs[chips.index(chip)].shape[1]
+            rows = tables[side][:, half] if narrow else tables[side][...]
             block = jnp.dot(placing.astype(BF16), rows, preferred_element_type=F32)
             if with_gate:
                 gate = jnp.where(ids0 == d, metas[side][2:3, :], metas[side][3:4, :])
@@ -109,12 +106,16 @@
     if placings:
         outs = outs + [like(len(plan.chips) * cap, toks)] * 2
     args = (*metas, *tables)
+    specs = [whole(a) for a in args]
+    if chips == plan.far:
+        half = pl.BlockSpec((toks, width // 2), lambda i, where: (0, where[1] & 1))
+        specs = specs[:2] + [half, half]
     return call(
         functools.partial(place_kernel, plan, cap, with_gate, chips, placings),
         name,
         where,
         args,
-        [whole(a) for a in args],
+        specs,
         outs,
         [whole(o) for o in outs],
         (1,),
@@ -215,7 +216,7 @@
     count = (len(full) + len(halves)) * cap
     rows = 2 * count
     units = w_down.shape[1]
-    tile = 256
+    tile = 512
     blocks = [*full, *halves, *others]
     column = pl.BlockSpec((count, tile), lambda j, _: (0, j))
     out_column = pl.BlockSpec((count, tile), lambda j, _: (chunk, j))
@@ -327,7 +328,7 @@
 
 def outer(name, where, left, rights, part=0, parts=1, kept=()):
     rows, width = left.shape
-    tile = 256
+    tile = 512
     steps = width // tile // parts
     first = part * steps
     outs = [like(1, width, r.shape[1]) for r in rights]
@@ -426,12 +427,6 @@
     return lax.ppermute(rows, axis, [(i, i ^ mask) for i in range(count)])
 
 
-def cross(rows, shift):
-    dp = lax.axis_size("dp")
-    count = lax.axis_size("expert") * dp
-    return lax.ppermute(rows, ("expert", "dp"), [(i, i ^ (dp + shift)) for i in range(count)])
-
-
 def body(tokens, grad_out, expert_ids, gate_vals, w_gate, w_up, w_down):
     plan = Plan(lax.axis_size("expert"))
     dp = lax.axis_size("dp")
@@ -489,7 +484,7 @@
     x_all, hidden, to_a, to_b = forward(
         "forward_near", where, 1, pick(x, plan.near), [], [], w_gate, w_up, (after(x_all, give), hidden)
     )
-    far_sum = (keep + after(got, hidden, *(pick(r, plan.near) if OPT_FAR_WAITS else [])).astype(F32)).astype(BF16)
+    far_sum = (keep + after(got, hidden).astype(F32)).astype(BF16)
     rows = 2 * cap
     far = [swap(far_sum[i * rows : (i + 1) * rows], "expert", 2 * c) for i, c in enumerate(plan.far)]
     kept = (after(r_all, far_sum), after(grad_a, give), after(grad_b, give))
@@ -497,7 +492,7 @@
         "backward_near", where, 1, pick(r, plan.near), [], [], w_down, to_a, to_b, kept
     )
     away_part = near_grad(plan, where, grad_a, grad_b, w_gate, w_up, dp, cap, True)
-    grad_a = after(grad_a, away_part[0], *(far if FAR_FIRST == "here" else []))
+    grad_a = after(grad_a, away_part[0], *far)
     here_part = near_grad(plan, where, grad_a, grad_b, w_gate, w_up, dp, cap, False)
 
     def send_back(part):
@@ -508,13 +503,8 @@
     away, here = list(range(dp // 2, dp)), list(range(dp // 2))
 
     rights = [grad_a, grad_b]
-    first = [here_part[0], *(far if FAR_FIRST == "down" else [])]
-    if OPT_DOWN_LATE:
-        grads = outer("gate_and_up_0", where, after(x_all, *first), rights, 0, 4)
-        away_rows[0] = after(away_rows[0], grads[0])
-    else:
-        (grad_down,) = outer("down_grad", where, after(hidden, *first), [r_all])
-        away_rows[0] = after(away_rows[0], grad_down)
+    grads = outer("gate_and_up_0", where, after(x_all, here_part[0]), rights, 0, 4)
+    away_rows[0] = after(away_rows[0], grads[0])
     away_sum, other = combine(
         plan, where, placings, [own, *far, *away_rows], dp, cap, away, True
     )
@@ -522,12 +512,8 @@
     away_sum = (away_sum + other.astype(F32)).astype(BF16)
     parts = [away_sum[:, n * slab : (n + 1) * slab] for n in range(len(away))]
     away_sums = [swap(part, "dp", s) for part, s in zip(parts, away, strict=True)]
-    if OPT_DOWN_LATE:
-        (grad_down,) = outer("down_grad", where, after(hidden, *parts), [r_all])
-        here_rows[0] = after(here_rows[0], grad_down)
-    else:
-        grads = outer("gate_and_up_0", where, after(x_all, *parts), rights, 0, 4)
-        here_rows[0] = after(here_rows[0], grads[0])
+    (grad_down,) = outer("down_grad", where, after(hidden, *parts), [r_all])
+    here_rows[0] = after(here_rows[0], grad_down)
     total, other, *rest = combine(
         plan, where, placings, [own, *far, *here_rows], dp, cap, here, False
     )
@@ -536,12 +522,9 @@
     for part in range(1, 4):
         grads = outer(f"gate_and_up_{part}", where, x_all, rights, part, 4, grads)
         for n, s in enumerate(here[1:] if part == 1 else []):
-            if SIDE_LAST == "cross":
-                got += [swap(rest[2 * n], "dp", s), cross(rest[2 * n + 1], s)]
-            else:
-                other = after(swap(rest[2 * n + 1], "expert", 1), grads[0])
-                both = rest[2 * n].astype(F32) + other.astype(F32)
-                got += [swap(both.astype(BF16), "dp", s)]
+            other = after(swap(rest[2 * n + 1], "expert", 1), grads[0])
+            both = rest[2 * n].astype(F32) + other.astype(F32)
+            got += [swap(both.astype(BF16), "dp", s)]
     grad_gate, grad_up = grads
     total = total + add_up(away_sums)
     for part in got:

time: 116 us -> 115 us (level)
  Pallas kernels: 61.7 us -> 59.7 us
    pallas_call x15, Pallas kernels: 59.1 us -> 57.1 us  [call(): pl.pallas_call(inner, input_output_aliases={i + 1: i for i in range(len(k...]
  transfers between devices with their start and end apart: 23 -> 23, of which waited for: 9 -> 9; matrix products, arithmetic and copies ran while one was open for 2% -> 2% of each run, Pallas kernels for 52% -> 51%
where the time goes in v5:
time: 115 us
  Pallas kernels  59.7 us (52%)
  starting transfers between devices  28.1 us (24%)
  waiting for transfers between devices  21.1 us (18%)
  other arithmetic  2.62 us (2%)
  local copies, waits for them, and re-layouts  2.24 us (2%)
    pallas_call x15, Pallas kernels, call(): pl.pallas_call(inner, input_output_aliases={i + 1: i for i in range(len(k...  57.1 us
    ppermute x23, starting transfers between devices, swap(): return lax.ppermute(rows, axis, [(i, i ^ mask) for i in range(count)])  28.1 us
    ppermute x23, waiting for transfers between devices, swap(): return lax.ppermute(rows, axis, [(i, i ^ mask) for i in range(count)])  21.1 us
    pallas_call x2, Pallas kernels, combine(): pl.pallas_call(functools.partial(combine_kernel, plan, cap, dp, shifts, s...  2.53 us
  transfers between devices with their start and end apart: 23, of which 9 were waited for; matrix products, arithmetic and copies ran while one was open for 2% of the time, Pallas kernels for 51%

profile of v5, /device:TPU:0, one launch (start us, length us, event | category | flops | bytes accessed | tf_op | source)
XLA Modules:
  0.0 114.6 jit_solution(1825762408939519514)
XLA Ops:
  4.9 2.1 %place_far_tokens.1 = bf16[192,1024]{1,0:T(8,128)(2,1)S(1)} custom-call(s32[2]{0:T(128)S(1)} %pad_add_fusion.where, f32[4,256]{1,0:T(4,128)S(1)} %pad_maximum_fusion.refs_0_, f32[4,256]{1,0:T(4,128)S(1)} %collective-permute-done.refs_1_, bf16[256,2048]{1,0:T(8,128)(2,1)} %refs_2_.7, bf16[256,2048]{1,0:T(8,128)(2,1)S(1)} %collective-permute-done.1.refs_3_), custom_call_target="tpu_custom_call" | custom-call | tf_op jit(solution)/shard_map/place_far_tokens/pallas_call | solution.py:38
  7.1 3.9 %collective-permute-start.5 = (bf16[192,1024]{1,0:T(8,128)(2,1)S(1)}, bf16[192,1024]{1,0:T(8,128)(2,1)S(1)}, u32[]{:S(2)}, u32[]{:S(2)}) collective-permute-start(bf16[192,1024]{1,0:T(8,128)(2,1)S(1)} %place_far_tokens.1), channel_id=1, source_target_pairs={{0,24},{4,28},{8,16},{12,20},{16,8},{20,12},{24,0},{28,4},{1,25},{... | collective-permute-start | bytes 1179656 | tf_op jit(solution)/shard_map/ppermute | solution.py:427
  11.0 3.4 %place_scaled.1 = (bf16[192,2048]{1,0:T(8,128)(2,1)S(1)}, bf16[192,2048]{1,0:T(8,128)(2,1)S(1)}, bf16[192,2048]{1,0:T(8,128)(2,1)S(1)}, bf16[192,1024]{1,0:T(8,128)(2,1)S(1)}) custom-call(s32[2]{0:T(128)S(1)} %pad_add_fusion.where, f32[4,256]{1,0:T(4,128)S(1)} %pad_maximum_fusion.refs_0_, f32[4,256]{1,0:T(4,128)S(1)} %collective-permute-done.refs_1_, ...), custom_call_target="tpu_custom_call" | custom-call | tf_op jit(solution)/shard_map/place_scaled/pallas_call | solution.py:38
  14.5 3.2 %place_tokens.1 = (bf16[192,2048]{1,0:T(8,128)(2,1)S(1)}, bf16[192,2048]{1,0:T(8,128)(2,1)S(1)}, bf16[192,2048]{1,0:T(8,128)(2,1)S(1)}, bf16[384,256]{1,0:T(8,128)(2,1)S(1)}, bf16[384,256]{1,0:T(8,128)(2,1)S(1)}) custom-call(s32[2]{0:T(128)S(1)} %pad_add_fusion.where, f32[4,256]{1,0:T(4,128)S(1)} %pad_maximum_fusion.refs_0_, ...), custom_call_target="tpu_custom_call" | custom-call | flops 100000000 | tf_op jit(solution)/shard_map/place_tokens/pallas_call | solution.py:38
  17.6 2.0 %collective-permute-start.8 = (bf16[192,2048]{1,0:T(8,128)(2,1)S(1)}, bf16[192,2048]{1,0:T(8,128)(2,1)S(1)}, u32[]{:S(2)}, u32[]{:S(2)}) collective-permute-start(bf16[192,2048]{1,0:T(8,128)(2,1)S(1)} %get-tuple-element.79), channel_id=1, source_target_pairs={{0,8},{4,12},{8,0},{12,4},{16,24},{20,28},{24,16},{28,20},{1,9},{5... | collective-permute-start | bytes 2359304 | tf_op jit(solution)/shard_map/ppermute | solution.py:427
  22.9 6.4 %collective-permute-done.3.refs_1_ = bf16[192,1024]{1,0:T(8,128)(2,1)S(1)} collective-permute-done((bf16[192,1024]{1,0:T(8,128)(2,1)S(1)}, bf16[192,1024]{1,0:T(8,128)(2,1)S(1)}, u32[]{:S(2)}, u32[]{:S(2)}) %collective-permute-start.3) | collective-permute-done | bytes 393248 | tf_op jit(solution)/shard_map/ppermute | solution.py:427
  29.3 2.1 %collective-permute-start.4 = (bf16[192,1024]{1,0:T(8,128)(2,1)S(1)}, bf16[192,1024]{1,0:T(8,128)(2,1)S(1)}, u32[]{:S(2)}, u32[]{:S(2)}) collective-permute-start(bf16[192,1024]{1,0:T(8,128)(2,1)S(1)} %collective-permute-done.3.refs_1_), channel_id=1, source_target_pairs={{0,1},{1,0},{2,3},{3,2},{4,5},{5,4},{6,7},{7,6},{8,9},{9,8},{10,11... | collective-permute-start | bytes 1179656 | tf_op jit(solution)/shard_map/ppermute | solution.py:427
  34.4 2.2 %copy-done.1 = bf16[1,2048,1024]{2,1,0:T(8,128)(2,1)S(1)} copy-done((bf16[1,2048,1024]{2,1,0:T(8,128)(2,1)S(1)}, bf16[1,2048,1024]{2,1,0:T(8,128)(2,1)}, u32[]{:S(2)}) %copy-start.1) | copy-done | bytes 4194328
  36.6 6.5 %forward_own_and_far.1 = (bf16[768,2048]{1,0:T(8,128)(2,1)S(1)}, bf16[768,1024]{1,0:T(8,128)(2,1)S(1)}, f32[384,1024]{1,0:T(8,128)S(1)}, f32[384,1024]{1,0:T(8,128)S(1)}) custom-call(s32[2]{0:T(128)S(1)} %pad_add_fusion.where, bf16[192,2048]{1,0:T(8,128)(2,1)S(1)} %get-tuple-element.68.refs_0_, bf16[192,1024]{1,0:T(8,128)(2,1)S(1)} %collective-permute-done.5.refs_1_, ...), custom_call_target="tpu_custom_call" | custom-call | tf_op jit(solution)/shard_map/forward_own_and_far/pallas_call | solution.py:38
  43.2 3.1 %backward_own_and_far.1 = (bf16[768,2048]{1,0:T(8,128)(2,1)S(1)}, bf16[768,1024]{1,0:T(8,128)(2,1)S(1)}, bf16[768,1024]{1,0:T(8,128)(2,1)S(1)}) custom-call(s32[2]{0:T(128)S(1)} %pad_add_fusion.where, bf16[192,2048]{1,0:T(8,128)(2,1)S(1)} %get-tuple-element.66.refs_0_, bf16[192,1024]{1,0:T(8,128)(2,1)S(1)} %collective-permute-done.3.refs_1_, ...), custom_call_target="tpu_custom_call" | custom-call | tf_op jit(solution)/shard_map/backward_own_and_far/pallas_call | solution.py:38
  46.3 5.0 %own_and_far_input_grads.1 = (bf16[192,2048]{1,0:T(8,128)(2,1)S(1)}, bf16[192,1024]{1,0:T(8,128)(2,1)S(1)}, f32[192,1024]{1,0:T(8,128)S(1)}) custom-call(s32[2]{0:T(128)S(1)} %pad_add_fusion.where, bf16[768,1024]{1,0:T(8,128)(2,1)S(1)} %get-tuple-element.85.refs_0_.refs_1_, bf16[768,1024]{1,0:T(8,128)(2,1)S(1)} %get-tuple-element.86.refs_1_.refs_2_, ...), custom_call_target="tpu_custom_call" | custom-call | flops 100000000 | tf_op jit(solution)/shard_map/own_and_far_input_grads/pallas_call | solution.py:38
  52.4 6.3 %forward_near.1 = (bf16[768,2048]{1,0:T(8,128)(2,1)S(1)}, bf16[768,1024]{1,0:T(8,128)(2,1)S(1)}, f32[384,1024]{1,0:T(8,128)S(1)}, f32[384,1024]{1,0:T(8,128)S(1)}) custom-call(s32[2]{0:T(128)S(1)} %pad_add_fusion.where, bf16[768,2048]{1,0:T(8,128)(2,1)S(1)} %get-tuple-element.77.refs_0_, ...), custom_call_target="tpu_custom_call", output_to_operand_aliasing={{0}: (1, {}), {1}: (2, {})} | custom-call | flops 60000002048 | tf_op jit(solution)/shard_map/forward_near/pallas_call | solution.py:38
  60.7 2.3 %collective-permute-done.12.refs_4_ = bf16[192,2048]{1,0:T(8,128)(2,1)S(1)} collective-permute-done((bf16[192,2048]{1,0:T(8,128)(2,1)S(1)}, bf16[192,2048]{1,0:T(8,128)(2,1)S(1)}, u32[]{:S(2)}, u32[]{:S(2)}) %collective-permute-start.12) | collective-permute-done | bytes 786464 | tf_op jit(solution)/shard_map/ppermute | solution.py:427
  63.6 3.1 %backward_near.1 = (bf16[768,2048]{1,0:T(8,128)(2,1)S(1)}, bf16[768,1024]{1,0:T(8,128)(2,1)S(1)}, bf16[768,1024]{1,0:T(8,128)(2,1)S(1)}) custom-call(s32[2]{0:T(128)S(1)} %pad_add_fusion.where, bf16[768,2048]{1,0:T(8,128)(2,1)S(1)} %get-tuple-element.84.refs_0_, ...), custom_call_target="tpu_custom_call", output_to_operand_aliasing={{0}: (1, {}), {1}: (2, {}), {2}: (3, {})} | custom-call | flops 1000000000 | tf_op jit(solution)/shard_map/backward_near/pallas_call | solution.py:38
  66.7 2.6 %near_grads_away.1 = (bf16[192,1024]{1,0:T(8,128)(2,1)S(1)}, bf16[192,1024]{1,0:T(8,128)(2,1)S(1)}) custom-call(s32[2]{0:T(128)S(1)} %pad_add_fusion.where, bf16[768,1024]{1,0:T(8,128)(2,1)S(1)} %get-tuple-element.96.refs_0_.refs_1_.refs_3_, bf16[768,1024]{1,0:T(8,128)(2,1)S(1)} %get-tuple-element.94.refs_1_.refs_2_.refs_4_, ...), custom_call_target="tpu_custom_call" | custom-call | flops 20000000000 | tf_op jit(solution)/shard_map/near_grads_away/pallas_call | solution.py:38
  72.3 2.6 %near_grads_here.1 = (bf16[192,1024]{1,0:T(8,128)(2,1)S(1)}, bf16[192,1024]{1,0:T(8,128)(2,1)S(1)}) custom-call(s32[2]{0:T(128)S(1)} %pad_add_fusion.where, bf16[768,1024]{1,0:T(8,128)(2,1)S(1)} %get-tuple-element.96.refs_0_.refs_1_.refs_3_, bf16[768,1024]{1,0:T(8,128)(2,1)S(1)} %get-tuple-element.94.refs_1_.refs_2_.refs_4_, ...), custom_call_target="tpu_custom_call" | custom-call | flops 100000000 | tf_op jit(solution)/shard_map/near_grads_here/pallas_call | solution.py:38
  74.9 3.4 %gate_and_up_0.1 = (bf16[1,2048,1024]{2,1,0:T(8,128)(2,1)}, bf16[1,2048,1024]{2,1,0:T(8,128)(2,1)}) custom-call(s32[2]{0:T(128)S(1)} %pad_add_fusion.where, bf16[768,2048]{1,0:T(8,128)(2,1)S(1)} %get-tuple-element.114.refs_0_.refs_2_, bf16[768,1024]{1,0:T(8,128)(2,1)S(1)} %get-tuple-element.96.refs_0_.refs_1_.refs_3_, ...), custom_call_target="tpu_custom_call" | custom-call | flops 1000000000 | tf_op jit(solution)/shard_map/gate_and_up_0/pallas_call | solution.py:38
  85.1 3.7 %collective-permute-start.19 = (bf16[256,512]{1,0:T(8,128)(2,1)S(1)}, bf16[256,512]{1,0:T(8,128)(2,1)S(1)}, u32[]{:S(2)}, u32[]{:S(2)}) collective-permute-start(bf16[256,512]{1,0:T(8,128)(2,1)S(1)} %get-tuple-element.122), channel_id=1, source_target_pairs={{0,3},{1,2},{2,1},{3,0},{4,7},{5,6},{6,5},{7,4},{8,11},{9,10},{10,... | collective-permute-start | bytes 786440 | tf_op jit(solution)/shard_map/ppermute | solution.py:427
  88.7 5.7 %down_grad.1 = bf16[1,1024,2048]{2,1,0:T(8,128)(2,1)} custom-call(s32[2]{0:T(128)S(1)} %pad_add_fusion.where, bf16[768,1024]{1,0:T(8,128)(2,1)S(1)} %get-tuple-element.105.refs_0_, bf16[768,2048]{1,0:T(8,128)(2,1)S(1)} %get-tuple-element.106.refs_1_), custom_call_target="tpu_custom_call" | custom-call | tf_op jit(solution)/shard_map/down_grad/pallas_call | solution.py:38
  96.3 3.3 %gate_and_up_1.1 = (bf16[1,2048,1024]{2,1,0:T(8,128)(2,1)}, bf16[1,2048,1024]{2,1,0:T(8,128)(2,1)}) custom-call(s32[2]{0:T(128)S(1)} %pad_add_fusion.where, bf16[1,2048,1024]{2,1,0:T(8,128)(2,1)} %get-tuple-element.100.refs_0_, bf16[1,2048,1024]{2,1,0:T(8,128)(2,1)} %get-tuple-element.113.refs_1_, ...), custom_call_target="tpu_custom_call", output_to_operand_aliasing={{0}: (1, {}), {1}: (2, {})} | custom-call | flops 5000000000 | tf_op jit(solution)/shard_map/gate_and_up_1/pallas_call | solution.py:38
  101.5 3.3 %gate_and_up_2.1 = (bf16[1,2048,1024]{2,1,0:T(8,128)(2,1)}, bf16[1,2048,1024]{2,1,0:T(8,128)(2,1)}) custom-call(s32[2]{0:T(128)S(1)} %pad_add_fusion.where, bf16[1,2048,1024]{2,1,0:T(8,128)(2,1)} %get-tuple-element.115.refs_0_, bf16[1,2048,1024]{2,1,0:T(8,128)(2,1)} %get-tuple-element.117.refs_1_, ...), custom_call_target="tpu_custom_call", output_to_operand_aliasing={{0}: (1, {}), {1}: (2, {})} | custom-call | flops 20000000000 | tf_op jit(solution)/shard_map/gate_and_up_2/pallas_call | solution.py:38
  104.8 3.3 %gate_and_up_3.1 = (bf16[1,2048,1024]{2,1,0:T(8,128)(2,1)}, bf16[1,2048,1024]{2,1,0:T(8,128)(2,1)}) custom-call(s32[2]{0:T(128)S(1)} %pad_add_fusion.where, bf16[1,2048,1024]{2,1,0:T(8,128)(2,1)} %get-tuple-element.118.refs_0_, bf16[1,2048,1024]{2,1,0:T(8,128)(2,1)} %get-tuple-element.119.refs_1_, ...), custom_call_target="tpu_custom_call", output_to_operand_aliasing={{0}: (1, {}), {1}: (2, {})} | custom-call | flops 20000000000 | tf_op jit(solution)/shard_map/gate_and_up_3/pallas_call | solution.py:38
  108.1 3.1 %collective-permute-done.18.refs_0_ = bf16[256,512]{1,0:T(8,128)(2,1)S(1)} collective-permute-done((bf16[256,512]{1,0:T(8,128)(2,1)S(1)}, bf16[256,512]{1,0:T(8,128)(2,1)S(1)}, u32[]{:S(2)}, u32[]{:S(2)}) %collective-permute-start.18) | collective-permute-done | bytes 262176 | tf_op jit(solution)/shard_map/ppermute | solution.py:427
  111.3 2.4 %collective-permute-done.22 = bf16[256,512]{1,0:T(8,128)(2,1)S(1)} collective-permute-done((bf16[256,512]{1,0:T(8,128)(2,1)S(1)}, bf16[256,512]{1,0:T(8,128)(2,1)S(1)}, u32[]{:S(2)}, u32[]{:S(2)}) %collective-permute-start.22) | collective-permute-done | bytes 262176 | tf_op jit(solution)/shard_map/ppermute | solution.py:427
  (56 shorter events, 28.7 us)
Async XLA Ops:
  0.6 4.3 %collective-permute-start.1 = (bf16[256,2048]{1,0:T(8,128)(2,1)}, bf16[256,2048]{1,0:T(8,128)(2,1)S(1)}, u32[]{:S(2)}, u32[]{:S(2)}) collective-permute-start(bf16[256,2048]{1,0:T(8,128)(2,1)} %refs_2_.7), channel_id=1, source_target_pairs={{0,4},{4,0},{8,12},{12,8},{16,20},{20,16},{24,28},{28,24},{1,5},{5... | collective-permute-start | bytes 3145736 | tf_op jit(solution)/shard_map/ppermute | solution.py:427
  1.1 9.8 %collective-permute-start.2 = (bf16[256,2048]{1,0:T(8,128)(2,1)}, bf16[256,2048]{1,0:T(8,128)(2,1)S(1)}, u32[]{:S(2)}, u32[]{:S(2)}) collective-permute-start(bf16[256,2048]{1,0:T(8,128)(2,1)} %refs_2_.8), channel_id=1, source_target_pairs={{0,4},{4,0},{8,12},{12,8},{16,20},{20,16},{24,28},{28,24},{1,5},{5... | collective-permute-start | bytes 3145736 | tf_op jit(solution)/shard_map/ppermute | solution.py:427
  2.6 2.3 %collective-permute-start = (f32[4,256]{1,0:T(4,128)S(1)}, f32[4,256]{1,0:T(4,128)S(1)}, u32[]{:S(2)}, u32[]{:S(2)}) collective-permute-start(f32[4,256]{1,0:T(4,128)S(1)} %pad_maximum_fusion.refs_0_), channel_id=1, source_target_pairs={{0,4},{4,0},{8,12},{12,8},{16,20},{20,16},{24,28},{28,24},{1,5},{5... | collective-permute-start | bytes 12296 | tf_op jit(solution)/shard_map/ppermute | solution.py:427
  3.1 31.3 %copy-start = (bf16[1,2048,1024]{2,1,0:T(8,128)(2,1)S(1)}, bf16[1,2048,1024]{2,1,0:T(8,128)(2,1)}, u32[]{:S(2)}) copy-start(bf16[1,2048,1024]{2,1,0:T(8,128)(2,1)} %refs_2_.11) | copy-start | bytes 12582916
  7.1 14.1 %collective-permute-start.5 = (bf16[192,1024]{1,0:T(8,128)(2,1)S(1)}, bf16[192,1024]{1,0:T(8,128)(2,1)S(1)}, u32[]{:S(2)}, u32[]{:S(2)}) collective-permute-start(bf16[192,1024]{1,0:T(8,128)(2,1)S(1)} %place_far_tokens.1), channel_id=1, source_target_pairs={{0,24},{4,28},{8,16},{12,20},{16,8},{20,12},{24,0},{28,4},{1,25},{... | collective-permute-start | bytes 1179656 | tf_op jit(solution)/shard_map/ppermute | solution.py:427
  14.4 15.0 %collective-permute-start.3 = (bf16[192,1024]{1,0:T(8,128)(2,1)S(1)}, bf16[192,1024]{1,0:T(8,128)(2,1)S(1)}, u32[]{:S(2)}, u32[]{:S(2)}) collective-permute-start(bf16[192,1024]{1,0:T(8,128)(2,1)S(1)} %get-tuple-element.67), channel_id=1, source_target_pairs={{0,24},{4,28},{8,16},{12,20},{16,8},{20,12},{24,0},{28,4},{1,25},{... | collective-permute-start | bytes 1179656 | tf_op jit(solution)/shard_map/ppermute | solution.py:427
  17.6 34.8 %collective-permute-start.8 = (bf16[192,2048]{1,0:T(8,128)(2,1)S(1)}, bf16[192,2048]{1,0:T(8,128)(2,1)S(1)}, u32[]{:S(2)}, u32[]{:S(2)}) collective-permute-start(bf16[192,2048]{1,0:T(8,128)(2,1)S(1)} %get-tuple-element.79), channel_id=1, source_target_pairs={{0,8},{4,12},{8,0},{12,4},{16,24},{20,28},{24,16},{28,20},{1,9},{5... | collective-permute-start | bytes 2359304 | tf_op jit(solution)/shard_map/ppermute | solution.py:427
  19.7 32.8 %collective-permute-start.9 = (bf16[192,2048]{1,0:T(8,128)(2,1)S(1)}, bf16[192,2048]{1,0:T(8,128)(2,1)S(1)}, u32[]{:S(2)}, u32[]{:S(2)}) collective-permute-start(bf16[192,2048]{1,0:T(8,128)(2,1)S(1)} %get-tuple-element.80), channel_id=1, source_target_pairs={{0,16},{4,20},{8,24},{12,28},{16,0},{20,4},{24,8},{28,12},{1,17},{... | collective-permute-start | bytes 2359304 | tf_op jit(solution)/shard_map/ppermute | solution.py:427
  21.2 10.2 %collective-permute-start.6 = (bf16[192,1024]{1,0:T(8,128)(2,1)S(1)}, bf16[192,1024]{1,0:T(8,128)(2,1)S(1)}, u32[]{:S(2)}, u32[]{:S(2)}) collective-permute-start(bf16[192,1024]{1,0:T(8,128)(2,1)S(1)} %collective-permute-done.5.refs_1_), channel_id=1, source_target_pairs={{0,1},{1,0},{2,3},{3,2},{4,5},{5,4},{6,7},{7,6},{8,9},{9,8},{10,11... | collective-permute-start | bytes 1179656 | tf_op jit(solution)/shard_map/ppermute | solution.py:427
  29.3 13.8 %collective-permute-start.4 = (bf16[192,1024]{1,0:T(8,128)(2,1)S(1)}, bf16[192,1024]{1,0:T(8,128)(2,1)S(1)}, u32[]{:S(2)}, u32[]{:S(2)}) collective-permute-start(bf16[192,1024]{1,0:T(8,128)(2,1)S(1)} %collective-permute-done.3.refs_1_), channel_id=1, source_target_pairs={{0,1},{1,0},{2,3},{3,2},{4,5},{5,4},{6,7},{7,6},{8,9},{9,8},{10,11... | collective-permute-start | bytes 1179656 | tf_op jit(solution)/shard_map/ppermute | solution.py:427
  31.4 31.5 %collective-permute-start.12 = (bf16[192,2048]{1,0:T(8,128)(2,1)S(1)}, bf16[192,2048]{1,0:T(8,128)(2,1)S(1)}, u32[]{:S(2)}, u32[]{:S(2)}) collective-permute-start(bf16[192,2048]{1,0:T(8,128)(2,1)S(1)} %get-tuple-element.90), channel_id=1, source_target_pairs={{0,16},{4,20},{8,24},{12,28},{16,0},{20,4},{24,8},{28,12},{1,17},{... | collective-permute-start | bytes 2359304 | tf_op jit(solution)/shard_map/ppermute | solution.py:427
  32.9 30.7 %collective-permute-start.11 = (bf16[192,2048]{1,0:T(8,128)(2,1)S(1)}, bf16[192,2048]{1,0:T(8,128)(2,1)S(1)}, u32[]{:S(2)}, u32[]{:S(2)}) collective-permute-start(bf16[192,2048]{1,0:T(8,128)(2,1)S(1)} %get-tuple-element.88), channel_id=1, source_target_pairs={{0,8},{4,12},{8,0},{12,4},{16,24},{20,28},{24,16},{28,20},{1,9},{5... | collective-permute-start | bytes 2359304 | tf_op jit(solution)/shard_map/ppermute | solution.py:427
  51.3 8.7 %collective-permute-start.7 = (bf16[192,1024]{1,0:T(8,128)(2,1)S(1)}, bf16[192,1024]{1,0:T(8,128)(2,1)S(1)}, u32[]{:S(2)}, u32[]{:S(2)}) collective-permute-start(bf16[192,1024]{1,0:T(8,128)(2,1)S(1)} %get-tuple-element.75), channel_id=1, source_target_pairs={{0,1},{1,0},{2,3},{3,2},{4,5},{5,4},{6,7},{7,6},{8,9},{9,8},{10,11... | collective-permute-start | bytes 1179656 | tf_op jit(solution)/shard_map/ppermute | solution.py:427
  60.2 12.1 %collective-permute-start.10 = (bf16[192,1024]{1,0:T(8,128)(2,1)S(1)}, bf16[192,1024]{1,0:T(8,128)(2,1)S(1)}, u32[]{:S(2)}, u32[]{:S(2)}) collective-permute-start(bf16[192,1024]{1,0:T(8,128)(2,1)S(1)} %add_convert_fusion.1), channel_id=1, source_target_pairs={{0,24},{4,28},{8,16},{12,20},{16,8},{20,12},{24,0},{28,4},{1,25},{... | collective-permute-start | bytes 1179656 | tf_op jit(solution)/shard_map/ppermute | solution.py:427
  69.3 10.6 %collective-permute-start.14 = (bf16[192,1024]{1,0:T(8,128)(2,1)S(1)}, bf16[192,1024]{1,0:T(8,128)(2,1)S(1)}, u32[]{:S(2)}, u32[]{:S(2)}) collective-permute-start(bf16[192,1024]{1,0:T(8,128)(2,1)S(1)} %get-tuple-element.95), channel_id=1, source_target_pairs={{0,8},{4,12},{8,0},{12,4},{16,24},{20,28},{24,16},{28,20},{1,9},{5... | collective-permute-start | bytes 1179656 | tf_op jit(solution)/shard_map/ppermute | solution.py:427
  70.9 10.5 %collective-permute-start.15 = (bf16[192,1024]{1,0:T(8,128)(2,1)S(1)}, bf16[192,1024]{1,0:T(8,128)(2,1)S(1)}, u32[]{:S(2)}, u32[]{:S(2)}) collective-permute-start(bf16[192,1024]{1,0:T(8,128)(2,1)S(1)} %get-tuple-element.102), channel_id=1, source_target_pairs={{0,16},{4,20},{8,24},{12,28},{16,0},{20,4},{24,8},{28,12},{1,17},{... | collective-permute-start | bytes 1179656 | tf_op jit(solution)/shard_map/ppermute | solution.py:427
  82.7 2.2 %collective-permute-start.16 = (bf16[256,1024]{1,0:T(8,128)(2,1)S(1)}, bf16[256,1024]{1,0:T(8,128)(2,1)S(1)}, u32[]{:S(2)}, u32[]{:S(2)}) collective-permute-start(bf16[256,1024]{1,0:T(8,128)(2,1)S(1)} %get-tuple-element.104), channel_id=1, source_target_pairs={{0,4},{4,0},{8,12},{12,8},{16,20},{20,16},{24,28},{28,24},{1,5},{5... | collective-permute-start | bytes 1572872 | tf_op jit(solution)/shard_map/ppermute | solution.py:427
  82.7 11.7 %collective-permute-start.13 = (bf16[192,1024]{1,0:T(8,128)(2,1)S(1)}, bf16[192,1024]{1,0:T(8,128)(2,1)S(1)}, u32[]{:S(2)}, u32[]{:S(2)}) collective-permute-start(bf16[192,1024]{1,0:T(8,128)(2,1)S(1)} %get-tuple-element.97), channel_id=1, source_target_pairs={{0,8},{4,12},{8,0},{12,4},{16,24},{20,28},{24,16},{28,20},{1,9},{5... | collective-permute-start | bytes 1179656 | tf_op jit(solution)/shard_map/ppermute | solution.py:427
  83.2 11.3 %collective-permute-start.17 = (bf16[192,1024]{1,0:T(8,128)(2,1)S(1)}, bf16[192,1024]{1,0:T(8,128)(2,1)S(1)}, u32[]{:S(2)}, u32[]{:S(2)}) collective-permute-start(bf16[192,1024]{1,0:T(8,128)(2,1)S(1)} %get-tuple-element.108), channel_id=1, source_target_pairs={{0,16},{4,20},{8,24},{12,28},{16,0},{20,4},{24,8},{28,12},{1,17},{... | collective-permute-start | bytes 1179656 | tf_op jit(solution)/shard_map/ppermute | solution.py:427
  85.1 23.1 %collective-permute-start.19 = (bf16[256,512]{1,0:T(8,128)(2,1)S(1)}, bf16[256,512]{1,0:T(8,128)(2,1)S(1)}, u32[]{:S(2)}, u32[]{:S(2)}) collective-permute-start(bf16[256,512]{1,0:T(8,128)(2,1)S(1)} %get-tuple-element.122), channel_id=1, source_target_pairs={{0,3},{1,2},{2,1},{3,0},{4,7},{5,6},{6,5},{7,4},{8,11},{9,10},{10,... | collective-permute-start | bytes 786440 | tf_op jit(solution)/shard_map/ppermute | solution.py:427
  88.7 22.5 %collective-permute-start.18 = (bf16[256,512]{1,0:T(8,128)(2,1)S(1)}, bf16[256,512]{1,0:T(8,128)(2,1)S(1)}, u32[]{:S(2)}, u32[]{:S(2)}) collective-permute-start(bf16[256,512]{1,0:T(8,128)(2,1)S(1)} %get-tuple-element.123), channel_id=1, source_target_pairs={{0,2},{1,3},{2,0},{3,1},{4,6},{5,7},{6,4},{7,5},{8,10},{9,11},{10,... | collective-permute-start | bytes 786440 | tf_op jit(solution)/shard_map/ppermute | solution.py:427
  95.7 15.6 %collective-permute-start.20 = (bf16[256,512]{1,0:T(8,128)(2,1)S(1)}, bf16[256,512]{1,0:T(8,128)(2,1)S(1)}, u32[]{:S(2)}, u32[]{:S(2)}) collective-permute-start(bf16[256,512]{1,0:T(8,128)(2,1)S(1)} %get-tuple-element.110), channel_id=1, source_target_pairs={{0,4},{4,0},{8,12},{12,8},{16,20},{20,16},{24,28},{28,24},{1,5},{5... | collective-permute-start | bytes 786440 | tf_op jit(solution)/shard_map/ppermute | solution.py:427
  95.8 3.8 %collective-permute-start.21 = (bf16[256,512]{1,0:T(8,128)(2,1)S(1)}, bf16[256,512]{1,0:T(8,128)(2,1)S(1)}, u32[]{:S(2)}, u32[]{:S(2)}) collective-permute-start(bf16[256,512]{1,0:T(8,128)(2,1)S(1)} %get-tuple-element.112), channel_id=1, source_target_pairs={{0,4},{4,0},{8,12},{12,8},{16,20},{20,16},{24,28},{28,24},{1,5},{5... | collective-permute-start | bytes 786440 | tf_op jit(solution)/shard_map/ppermute | solution.py:427
  99.7 14.0 %collective-permute-start.22 = (bf16[256,512]{1,0:T(8,128)(2,1)S(1)}, bf16[256,512]{1,0:T(8,128)(2,1)S(1)}, u32[]{:S(2)}, u32[]{:S(2)}) collective-permute-start(bf16[256,512]{1,0:T(8,128)(2,1)S(1)} %add_convert_fusion.3), channel_id=1, source_target_pairs={{0,1},{1,0},{2,3},{3,2},{4,5},{5,4},{6,7},{7,6},{8,9},{9,8},{10,11... | collective-permute-start | bytes 786440 | tf_op jit(solution)/shard_map/ppermute | solution.py:427
  (3 other events, 11.8 us)
